TPU v7x, 256 devices: a whole 4x4x8 slice. The times are simulated.
256 devices in a mesh: front: 64 (over z, y, core), blk: 4 (over x).
Axes of the slice: x: 4, y: 4, z: 8, core: 2. Of those that a mesh axis runs over, the one named last changes fastest.
Arguments:
- pivot_inverse_0: float32 [1024, 1024], P('front', 'blk'), may hold values from -1 to 2, as said below
- pivot_inverse_1: float32 [2048, 1024], P('front', 'blk'), may hold values from -1 to 2, as said below
- below_factor_1: float32 [1024, 1024], P('front', 'blk'), may hold values from -0.1875 to 0.1875
- selector_1: int32 [2, 4], replicated, may hold values from 0 to 7, as said below
- pivot_inverse_2: float32 [4096, 1024], P('front', 'blk'), may hold values from -1 to 2, as said below
- below_factor_2: float32 [4096, 1024], P('front', 'blk'), may hold values from -0.125 to 0.125
- selector_2: int32 [4, 8], replicated, may hold values from 0 to 11, as said below
- pivot_inverse_3: float32 [8192, 1024], P('front', 'blk'), may hold values from -1 to 2, as said below
- below_factor_3: float32 [12288, 1024], P('front', 'blk'), may hold values from -0.109375 to 0.109375
- selector_3: int32 [8, 12], replicated, may hold values from 0 to 15, as said below
Outputs:
- sigma_diag_0: float32 [1024, 1024], P('front', 'blk')
- sigma_diag_1: float32 [2048, 1024], P('front', 'blk')
- sigma_below_1: float32 [1024, 1024], P('front', 'blk')
- sigma_diag_2: float32 [4096, 1024], P('front', 'blk')
- sigma_below_2: float32 [4096, 1024], P('front', 'blk')
- sigma_diag_3: float32 [8192, 1024], P('front', 'blk')
- sigma_below_3: float32 [12288, 1024], P('front', 'blk')
Inputs may be any that keep to these rules, and one draw needn't show every extreme that they name: `selector_1`: each row holds 4 distinct increasing block numbers of the root front's 8 blocks, always the first and the last. `selector_2`: each row holds 8 distinct increasing block numbers of its parent front's 12 blocks, always the first and the last. `selector_3`: each row holds 12 distinct increasing block numbers of its parent front's 16 blocks, always the first and the last. `pivot_inverse_0`: lower triangular in each front's 1024 x 1024 block; diagonal entries between 0.4 and 2.0, entries below the diagonal under 0.9 / sqrt(1024) in magnitude. `pivot_inverse_1`: lower triangular in each front's 1024 x 1024 block; diagonal entries between 0.4 and 2.0, entries below the diagonal under 0.9 / sqrt(1024) in magnitude. `pivot_inverse_2`: lower triangular in each front's 1024 x 1024 block; diagonal entries between 0.4 and 2.0, entries below the diagonal under 0.9 / sqrt(1024) in magnitude. `pivot_inverse_3`: lower triangular in each front's 1024 x 1024 block; diagonal entries between 0.4 and 2.0, entries below the diagonal under 0.9 / sqrt(1024) in magnitude.
All inputs are finite; a program needn't handle non-finite values.
Results may differ from a plain program's by a relative error of at most 0.00015.
Values sent between devices are 32-bit elements; how exact they have to be, the bound alone decides.
No kernel may reach another device: no remote copies, remote signals or barrier semaphores. Data moves between devices by JAX's collectives and lax.ppermute only.
A program may use at most 64 MiB of HBM per device.

v0:
```python
import jax
import jax.numpy as jnp
from jax import lax
from jax.sharding import PartitionSpec as P

S = 1024
BLOCK = 128
U1 = 512
U2 = 1024
U3 = 1536


def swapped(array, axis, distance):
    return lax.ppermute(array, axis, [(i, i ^ 1 << distance) for i in range(lax.axis_size(axis))])


def product(left, right):
    return jnp.dot(left, right, precision=lax.Precision.HIGHEST, preferred_element_type=jnp.float32)


def inner_product(left, right):
    return lax.dot_general(
        left,
        right,
        (((0,), (0,)), ((), ())),
        precision=lax.Precision.HIGHEST,
        preferred_element_type=jnp.float32,
    )


def index_range(start, length):
    return start + jnp.arange(length, dtype=jnp.int32)


def block_rows(selector):
    offsets = jnp.arange(BLOCK, dtype=jnp.int32)
    return (selector[..., :, None] * BLOCK + offsets).reshape(selector.shape[:-1] + (-1,))


def whole_rows(values):
    return lax.all_gather(values, "blk", axis=1, tiled=True)


def group_pieces(values, levels):
    device = lax.axis_index("front")
    for level_bit in range(levels):
        other = swapped(values, "front", level_bit)
        second = device >> level_bit & 1 == 1
        values = jnp.where(
            second, jnp.concatenate([other, values], 0), jnp.concatenate([values, other], 0)
        )
    return values


def group_sums(values, levels):
    device = lax.axis_index("front")
    for level_bit in reversed(range(levels)):
        half_rows = values.shape[0] // 2
        lower_half = values[:half_rows]
        upper_half = values[half_rows:]
        second = device >> level_bit & 1 == 1
        keeping = jnp.where(second, upper_half, lower_half)
        sending = jnp.where(second, lower_half, upper_half)
        values = keeping + swapped(sending, "front", level_bit)
    return values


def sweep_level(parent, selector, inverse, factor, count, width):
    fronts_total = lax.axis_size("front")
    quarters = lax.axis_size("blk")
    device = lax.axis_index("front")
    column_part = lax.axis_index("blk")
    group = fronts_total // count
    levels = group.bit_length() - 1
    front_id = device // group
    slot = device % group
    parent_front = front_id // 2
    parent_rows, row_ids, column_ids, pivot_local = parent
    pair = lax.dynamic_slice_in_dim(selector, parent_front * 2, 2, 0)
    mine = lax.dynamic_index_in_dim(selector, front_id, 0, keepdims=False)
    mine_rows = block_rows(mine)
    own = width // group
    pair_rows = block_rows(pair).reshape(-1)
    onehot = (row_ids[:, None] == pair_rows[None, :]).astype(jnp.float32)
    selected = group_sums(inner_product(onehot, parent_rows), levels + 1)
    picker = (column_ids[:, None] == mine_rows[None, :]).astype(jnp.float32)
    ancestor = lax.psum_scatter(product(selected, picker), "blk", scatter_dimension=1, tiled=True)
    inverse_columns = group_pieces(inverse, levels)
    factor_rows, inverse_rows = whole_rows((factor, inverse))
    coupling = product(factor_rows, inverse_columns)
    gram_part = inner_product(inverse_rows, inverse)
    coupling_rows, ancestor_rows = whole_rows((coupling, ancestor))
    coupling_columns = group_pieces(coupling, levels)
    below = -product(ancestor_rows, coupling_columns)
    top_part = -jnp.concatenate(
        [inner_product(coupling_rows, below), inner_product(coupling_rows, ancestor)], 1
    )
    quarter = S // quarters
    gram = group_sums(gram_part, levels)
    summed = group_sums(top_part, levels)
    diagonal = gram + summed[:, :quarter]
    upper = summed[:, quarter:]
    next_rows = jnp.concatenate(
        [jnp.concatenate([diagonal, upper], 1), jnp.concatenate([below, ancestor], 1)], 0
    )
    pivot_count = S // group
    next_row_ids = jnp.concatenate(
        [index_range(slot * pivot_count, pivot_count), S + index_range(slot * own, own)]
    )
    update_quarter = width // quarters
    next_column_ids = jnp.concatenate(
        [
            index_range(column_part * quarter, quarter),
            S + index_range(column_part * update_quarter, update_quarter),
        ]
    )
    return (diagonal, below, (next_rows, next_row_ids, next_column_ids, pivot_count))


def shards(
    pivot_inverse_0,
    pivot_inverse_1,
    below_factor_1,
    selector_1,
    pivot_inverse_2,
    below_factor_2,
    selector_2,
    pivot_inverse_3,
    below_factor_3,
    selector_3,
):
    fronts_total = lax.axis_size("front")
    quarters = lax.axis_size("blk")
    device = lax.axis_index("front")
    column_part = lax.axis_index("blk")
    root_rows = whole_rows(pivot_inverse_0)
    sigma_diag_0 = group_sums(
        inner_product(root_rows, pivot_inverse_0), fronts_total.bit_length() - 1
    )
    pivot_count = S // fronts_total
    quarter = S // quarters
    parent = (
        sigma_diag_0,
        index_range(device * pivot_count, pivot_count),
        index_range(column_part * quarter, quarter),
        pivot_count,
    )
    sigma_diag_1, sigma_below_1, parent = sweep_level(
        parent, selector_1, pivot_inverse_1, below_factor_1, 2, U1
    )
    sigma_diag_2, sigma_below_2, parent = sweep_level(
        parent, selector_2, pivot_inverse_2, below_factor_2, 4, U2
    )
    sigma_diag_3, sigma_below_3, parent = sweep_level(
        parent, selector_3, pivot_inverse_3, below_factor_3, 8, U3
    )
    return (
        sigma_diag_0,
        sigma_diag_1,
        sigma_below_1,
        sigma_diag_2,
        sigma_below_2,
        sigma_diag_3,
        sigma_below_3,
    )


def solution(mesh):
    return jax.shard_map(
        shards,
        mesh=mesh,
        in_specs=(
            P("front", "blk"),
            P("front", "blk"),
            P("front", "blk"),
            P(),
            P("front", "blk"),
            P("front", "blk"),
            P(),
            P("front", "blk"),
            P("front", "blk"),
            P(),
        ),
        out_specs=(
            P("front", "blk"),
            P("front", "blk"),
            P("front", "blk"),
            P("front", "blk"),
            P("front", "blk"),
            P("front", "blk"),
            P("front", "blk"),
        ),
        check_vma=False,
    )
```

profile of v0, /device:TPU:1, one launch (start us, length us, event | category | flops | bytes accessed | tf_op | source)
XLA Modules:
  0.0 790.6 jit_solution(5668126056154373688)
XLA Ops:
  7.2 10.4 %all_gather.39 = f32[16,1024]{1,0:T(8,128)S(1)} all-gather(f32[16,256]{1,0:T(8,128)} %param.10), channel_id=1, replica_groups=mesh['front'=64,'blk'=4] {'blk'}, dimensions={1}, use_global_device_ids=true | all-gather | bytes 81920 | tf_op jit(solution)/shard_map/all_gather | solution.py:41
  20.2 6.9 collective-permute-start
  31.0 10.0 %all_gather.40 = f32[32,1024]{1,0:T(8,128)S(1)} all-gather(f32[32,256]{1,0:T(8,128)S(1)} %copy-done.4), channel_id=1, replica_groups=mesh['front'=64,'blk'=4] {'blk'}, dimensions={1}, use_global_device_ids=true | all-gather | bytes 163840 | tf_op jit(solution)/shard_map/all_gather | solution.py:41
  42.1 9.8 %collective-permute-start.1 = (f32[256,256]{1,0:T(8,128)S(1)}, f32[256,256]{1,0:T(8,128)S(1)}, u32[]{:S(2)}, u32[]{:S(2)}) collective-permute-start(f32[256,256]{1,0:T(8,128)S(1)} %slice_select_fusion.23), channel_id=1, source_target_pairs={{0,64},{4,68},{8,72},{12,76},{16,80},{20,84},{24,88},{28,92},{32,9... | collective-permute-start | bytes 786440 | tf_op jit(solution)/shard_map/ppermute | solution.py:14
  52.8 22.7 %collective-permute-done.1 = f32[256,256]{1,0:T(8,128)S(1)} collective-permute-done((f32[256,256]{1,0:T(8,128)S(1)}, f32[256,256]{1,0:T(8,128)S(1)}, u32[]{:S(2)}, u32[]{:S(2)}) %collective-permute-start.1) | collective-permute-done | bytes 262176 | tf_op jit(solution)/shard_map/ppermute | solution.py:14
  75.7 13.8 %collective-permute-done.2 = f32[128,256]{1,0:T(8,128)S(1)} collective-permute-done((f32[128,256]{1,0:T(8,128)S(1)}, f32[128,256]{1,0:T(8,128)S(1)}, u32[]{:S(2)}, u32[]{:S(2)}) %collective-permute-start.2) | collective-permute-done | bytes 131104 | tf_op jit(solution)/shard_map/ppermute | solution.py:14
  109.7 26.6 %collective-permute-done.14 = f32[256,256]{1,0:T(8,128)S(1)} collective-permute-done((f32[256,256]{1,0:T(8,128)S(1)}, f32[256,256]{1,0:T(8,128)S(1)}, u32[]{:S(2)}, u32[]{:S(2)}) %collective-permute-start.14) | collective-permute-done | bytes 262176 | tf_op jit(solution)/shard_map/ppermute | solution.py:14
  140.9 9.2 %all_gather.41 = f32[16,1024]{1,0:T(8,128)S(1)} all-gather(f32[16,256]{1,0:T(8,128)S(1)} %copy-done.14), channel_id=1, replica_groups=mesh['front'=64,'blk'=4] {'blk'}, dimensions={1}, use_global_device_ids=true | all-gather | bytes 81920 | tf_op jit(solution)/shard_map/all_gather | solution.py:41
  150.1 18.3 %collective-permute-done.15 = f32[512,256]{1,0:T(8,128)} collective-permute-done((f32[512,256]{1,0:T(8,128)}, f32[512,256]{1,0:T(8,128)}, u32[]{:S(2)}, u32[]{:S(2)}) %collective-permute-start.15) | collective-permute-done | bytes 524320 | tf_op jit(solution)/shard_map/ppermute | solution.py:14
  192.2 9.4 %all_gather.42 = f32[16,1024]{1,0:T(8,128)S(1)} all-gather(f32[16,256]{1,0:T(8,128)S(1)} %convolution_bitcast_fusion.2), channel_id=1, replica_groups=mesh['front'=64,'blk'=4] {'blk'}, dimensions={1}, use_global_device_ids=true | all-gather | bytes 81920 | tf_op jit(solution)/shard_map/all_gather | solution.py:41
  201.5 9.5 %reduce-scatter.4.cloned.1.call-done = f32[16,128]{1,0:T(8,128)} async-done(((f32[16,512]{1,0:T(8,128)}), f32[16,128]{1,0:T(8,128)}) %reduce-scatter.4.cloned.1.call-update) | async-done | bytes 8208 | tf_op jit(solution)/shard_map/reduce_scatter | solution.py:87
  211.1 9.4 %all_gather.43 = f32[16,512]{1,0:T(8,128)S(1)} all-gather(f32[16,128]{1,0:T(8,128)} %reduce-scatter.4.cloned.1.call-done), channel_id=1, replica_groups=mesh['front'=64,'blk'=4] {'blk'}, dimensions={1}, use_global_device_ids=true | all-gather | bytes 40960 | tf_op jit(solution)/shard_map/all_gather | solution.py:41
  228.2 31.2 %collective-permute-done.27 = f32[512,384]{1,0:T(8,128)} collective-permute-done((f32[512,384]{1,0:T(8,128)S(1)}, f32[512,384]{1,0:T(8,128)}, u32[]{:S(2)}, u32[]{:S(2)}) %collective-permute-start.27) | collective-permute-done | bytes 786464 | tf_op jit(solution)/shard_map/ppermute | solution.py:14
  262.1 7.9 %collective-permute-done.28 = f32[256,384]{1,0:T(8,128)S(1)} collective-permute-done((f32[256,384]{1,0:T(8,128)S(1)}, f32[256,384]{1,0:T(8,128)S(1)}, u32[]{:S(2)}, u32[]{:S(2)}) %collective-permute-start.28) | collective-permute-done | bytes 393248 | tf_op jit(solution)/shard_map/ppermute | solution.py:14
  292.3 67.9 %collective-permute-done.40 = f32[1024,384]{1,0:T(8,128)S(1)} collective-permute-done((f32[1024,384]{1,0:T(8,128)S(1)}, f32[1024,384]{1,0:T(8,128)S(1)}, u32[]{:S(2)}, u32[]{:S(2)}) %collective-permute-start.40) | collective-permute-done | bytes 1572896 | tf_op jit(solution)/shard_map/ppermute | solution.py:14
  368.4 10.1 %all_gather.45 = f32[64,1024]{1,0:T(8,128)S(1)} all-gather(f32[64,256]{1,0:T(8,128)S(1)} %copy-done.13), channel_id=1, replica_groups=mesh['front'=64,'blk'=4] {'blk'}, dimensions={1}, use_global_device_ids=true | all-gather | bytes 327680 | tf_op jit(solution)/shard_map/all_gather | solution.py:41
  412.2 9.5 %all_gather.44 = f32[64,1024]{1,0:T(8,128)S(1)} all-gather(f32[64,256]{1,0:T(8,128)S(1)} %copy-done.3), channel_id=1, replica_groups=mesh['front'=64,'blk'=4] {'blk'}, dimensions={1}, use_global_device_ids=true | all-gather | bytes 327680 | tf_op jit(solution)/shard_map/all_gather | solution.py:41
  422.7 10.0 %all_gather.46 = f32[64,1024]{1,0:T(8,128)S(1)} all-gather(f32[64,256]{1,0:T(8,128)S(1)} %convolution_bitcast_fusion.1), channel_id=1, replica_groups=mesh['front'=64,'blk'=4] {'blk'}, dimensions={1}, use_global_device_ids=true | all-gather | bytes 327680 | tf_op jit(solution)/shard_map/all_gather | solution.py:41
  432.7 9.6 %all_gather.47 = f32[64,1024]{1,0:T(8,128)S(1)} all-gather(f32[64,256]{1,0:T(8,128)} %reduce-scatter.6.cloned.1.call-done), channel_id=1, replica_groups=mesh['front'=64,'blk'=4] {'blk'}, dimensions={1}, use_global_device_ids=true | all-gather | bytes 327680 | tf_op jit(solution)/shard_map/all_gather | solution.py:41
  449.7 23.0 %collective-permute-done.32 = f32[512,256]{1,0:T(8,128)} collective-permute-done((f32[512,256]{1,0:T(8,128)}, f32[512,256]{1,0:T(8,128)}, u32[]{:S(2)}, u32[]{:S(2)}) %collective-permute-start.32) | collective-permute-done | bytes 524320 | tf_op jit(solution)/shard_map/ppermute | solution.py:14
  488.6 7.2 collective-permute-done.51
  496.0 12.1 %collective-permute-start.52 = (f32[64,512]{1,0:T(8,128)S(1)}, f32[64,512]{1,0:T(8,128)S(1)}, u32[]{:S(2)}, u32[]{:S(2)}) collective-permute-start(f32[64,512]{1,0:T(8,128)S(1)} %slice_select_fusion.28), channel_id=1, source_target_pairs={{0,4},{4,0},{8,12},{12,8},{16,20},{20,16},{24,28},{28,24},{32,36},... | collective-permute-start | bytes 393224 | tf_op jit(solution)/shard_map/ppermute | solution.py:14
  514.3 68.5 %collective-permute-done.59 = f32[1536,512]{1,0:T(8,128)S(1)} collective-permute-done((f32[1536,512]{1,0:T(8,128)S(1)}, f32[1536,512]{1,0:T(8,128)S(1)}, u32[]{:S(2)}, u32[]{:S(2)}) %collective-permute-start.59) | collective-permute-done | bytes 3145760 | tf_op jit(solution)/shard_map/ppermute | solution.py:14
  586.0 34.9 %collective-permute-done.60 = f32[768,512]{1,0:T(8,128)S(1)} collective-permute-done((f32[768,512]{1,0:T(8,128)S(1)}, f32[768,512]{1,0:T(8,128)S(1)}, u32[]{:S(2)}, u32[]{:S(2)}) %collective-permute-start.60) | collective-permute-done | bytes 1572896 | tf_op jit(solution)/shard_map/ppermute | solution.py:14
  622.0 16.8 %collective-permute-done.61 = f32[384,512]{1,0:T(8,128)S(1)} collective-permute-done((f32[384,512]{1,0:T(8,128)S(1)}, f32[384,512]{1,0:T(8,128)S(1)}, u32[]{:S(2)}, u32[]{:S(2)}) %collective-permute-start.61) | collective-permute-done | bytes 786464 | tf_op jit(solution)/shard_map/ppermute | solution.py:14
  647.8 7.2 collective-permute-done.57
  657.0 17.0 %all_gather.49 = f32[192,1024]{1,0:T(8,128)S(1)} all-gather(f32[192,256]{1,0:T(8,128)S(1)} %copy-done.7), channel_id=1, replica_groups=mesh['front'=64,'blk'=4] {'blk'}, dimensions={1}, use_global_device_ids=true | all-gather | bytes 983040 | tf_op jit(solution)/shard_map/all_gather | solution.py:41
  681.2 8.9 %collective-permute-done.64 = f32[384,256]{1,0:T(8,128)S(1)} collective-permute-done((f32[384,256]{1,0:T(8,128)S(1)}, f32[384,256]{1,0:T(8,128)S(1)}, u32[]{:S(2)}, u32[]{:S(2)}) %collective-permute-start.64) | collective-permute-done | bytes 393248 | tf_op jit(solution)/shard_map/ppermute | solution.py:14
  693.3 16.6 %all_gather.50 = f32[192,1024]{1,0:T(8,128)S(1)} all-gather(f32[192,256]{1,0:T(8,128)S(1)} %convolution_bitcast_fusion), channel_id=1, replica_groups=mesh['front'=64,'blk'=4] {'blk'}, dimensions={1}, use_global_device_ids=true | all-gather | bytes 983040 | tf_op jit(solution)/shard_map/all_gather | solution.py:41
  718.8 10.8 %all_gather.48 = f32[128,1024]{1,0:T(8,128)S(1)} all-gather(f32[128,256]{1,0:T(8,128)S(1)} %copy-done.1), channel_id=1, replica_groups=mesh['front'=64,'blk'=4] {'blk'}, dimensions={1}, use_global_device_ids=true | all-gather | bytes 655360 | tf_op jit(solution)/shard_map/all_gather | solution.py:41
  732.3 25.9 %collective-permute-done.53 = f32[512,256]{1,0:T(8,128)S(1)} collective-permute-done((f32[512,256]{1,0:T(8,128)S(1)}, f32[512,256]{1,0:T(8,128)S(1)}, u32[]{:S(2)}, u32[]{:S(2)}) %collective-permute-start.53) | collective-permute-done | bytes 524320 | tf_op jit(solution)/shard_map/ppermute | solution.py:14
  760.2 17.4 %collective-permute-done.54 = f32[256,256]{1,0:T(8,128)S(1)} collective-permute-done((f32[256,256]{1,0:T(8,128)S(1)}, f32[256,256]{1,0:T(8,128)S(1)}, u32[]{:S(2)}, u32[]{:S(2)}) %collective-permute-start.54) | collective-permute-done | bytes 262176 | tf_op jit(solution)/shard_map/ppermute | solution.py:14
  (318 shorter events, 207.0 us)
Async XLA Ops:
  7.2 203.9 %reduce-scatter.4.cloned.1.call-start = ((), (), s32[]{:S(2)}) async-start(), calls=%async_computation.3 | async-start | bytes 40960 | tf_op jit(solution)/shard_map/reduce_scatter | solution.py:87
  20.2 21.8 %collective-permute-start = (f32[512,256]{1,0:T(8,128)}, f32[512,256]{1,0:T(8,128)S(1)}, u32[]{:S(2)}, u32[]{:S(2)}) collective-permute-start(f32[512,256]{1,0:T(8,128)} %slice_select_fusion.14), channel_id=1, source_target_pairs={{0,128},{4,132},{8,136},{12,140},{16,144},{20,148},{24,152},{28,15... | collective-permute-start | bytes 1572872 | tf_op jit(solution)/shard_map/ppermute | solution.py:14
  27.1 68.6 %collective-permute-start.11 = (f32[32,256]{1,0:T(8,128)S(1)}, f32[32,256]{1,0:T(8,128)S(1)}, u32[]{:S(2)}, u32[]{:S(2)}) collective-permute-start(f32[32,256]{1,0:T(8,128)S(1)} %copy-done.4), channel_id=1, source_target_pairs={{0,4},{4,0},{8,12},{12,8},{16,20},{20,16},{24,28},{28,24},{32,36},... | collective-permute-start | bytes 98312 | tf_op jit(solution)/shard_map/ppermute | solution.py:14
  42.1 33.3 %collective-permute-start.1 = (f32[256,256]{1,0:T(8,128)S(1)}, f32[256,256]{1,0:T(8,128)S(1)}, u32[]{:S(2)}, u32[]{:S(2)}) collective-permute-start(f32[256,256]{1,0:T(8,128)S(1)} %slice_select_fusion.23), channel_id=1, source_target_pairs={{0,64},{4,68},{8,72},{12,76},{16,80},{20,84},{24,88},{28,92},{32,9... | collective-permute-start | bytes 786440 | tf_op jit(solution)/shard_map/ppermute | solution.py:14
  52.8 121.3 %collective-permute-start.6 = (f32[512,256]{1,0:T(8,128)}, f32[512,256]{1,0:T(8,128)S(1)}, u32[]{:S(2)}, u32[]{:S(2)}) collective-permute-start(f32[512,256]{1,0:T(8,128)} %slice_select_fusion.13), channel_id=1, source_target_pairs={{0,64},{4,68},{8,72},{12,76},{16,80},{20,84},{24,88},{28,92},{32,9... | collective-permute-start | bytes 1572872 | tf_op jit(solution)/shard_map/ppermute | solution.py:14
  104.7 32.9 %collective-permute-start.16 = (f32[512,256]{1,0:T(8,128)}, f32[512,256]{1,0:T(8,128)}, u32[]{:S(2)}, u32[]{:S(2)}) collective-permute-start(f32[512,256]{1,0:T(8,128)} %slice_select_fusion.12), channel_id=1, source_target_pairs={{0,128},{4,132},{8,136},{12,140},{16,144},{20,148},{24,152},{28,15... | collective-permute-start | bytes 1572872 | tf_op jit(solution)/shard_map/ppermute | solution.py:14
  109.5 26.9 %collective-permute-start.14 = (f32[256,256]{1,0:T(8,128)S(1)}, f32[256,256]{1,0:T(8,128)S(1)}, u32[]{:S(2)}, u32[]{:S(2)}) collective-permute-start(f32[256,256]{1,0:T(8,128)S(1)} %maximum_select_fusion.20), channel_id=1, source_target_pairs={{0,32},{4,36},{8,40},{12,44},{16,48},{20,52},{24,56},{28,60},{32,0... | collective-permute-start | bytes 786440 | tf_op jit(solution)/shard_map/ppermute | solution.py:14
  137.2 31.2 %collective-permute-start.15 = (f32[512,256]{1,0:T(8,128)}, f32[512,256]{1,0:T(8,128)}, u32[]{:S(2)}, u32[]{:S(2)}) collective-permute-start(f32[512,256]{1,0:T(8,128)} %maximum_select_fusion.13), channel_id=1, source_target_pairs={{0,64},{4,68},{8,72},{12,76},{16,80},{20,84},{24,88},{28,92},{32,9... | collective-permute-start | bytes 1572872 | tf_op jit(solution)/shard_map/ppermute | solution.py:14
  138.8 35.1 %collective-permute-start.17 = (f32[256,256]{1,0:T(8,128)S(1)}, f32[256,256]{1,0:T(8,128)S(1)}, u32[]{:S(2)}, u32[]{:S(2)}) collective-permute-start(f32[256,256]{1,0:T(8,128)S(1)} %slice_select_fusion.21), channel_id=1, source_target_pairs={{0,64},{4,68},{8,72},{12,76},{16,80},{20,84},{24,88},{28,92},{32,9... | collective-permute-start | bytes 786440 | tf_op jit(solution)/shard_map/ppermute | solution.py:14
  190.0 30.4 %collective-permute-start.26 = (f32[256,256]{1,0:T(8,128)S(1)}, f32[256,256]{1,0:T(8,128)S(1)}, u32[]{:S(2)}, u32[]{:S(2)}) collective-permute-start(f32[256,256]{1,0:T(8,128)S(1)} %maximum_select_fusion.21), channel_id=1, source_target_pairs={{0,64},{4,68},{8,72},{12,76},{16,80},{20,84},{24,88},{28,92},{32,9... | collective-permute-start | bytes 786440 | tf_op jit(solution)/shard_map/ppermute | solution.py:14
  191.8 240.9 %reduce-scatter.6.cloned.1.call-start = ((), (), s32[]{:S(2)}) async-start(), calls=%async_computation.4 | async-start | bytes 327680 | tf_op jit(solution)/shard_map/reduce_scatter | solution.py:87
  191.9 33.4 %collective-permute-start.7 = (f32[256,256]{1,0:T(8,128)S(1)}, f32[256,256]{1,0:T(8,128)S(1)}, u32[]{:S(2)}, u32[]{:S(2)}) collective-permute-start(f32[256,256]{1,0:T(8,128)S(1)} %slice_select_fusion.22), channel_id=1, source_target_pairs={{0,32},{4,36},{8,40},{12,44},{16,48},{20,52},{24,56},{28,60},{32,0... | collective-permute-start | bytes 786440 | tf_op jit(solution)/shard_map/ppermute | solution.py:14
  223.0 36.4 %collective-permute-start.27 = (f32[512,384]{1,0:T(8,128)S(1)}, f32[512,384]{1,0:T(8,128)}, u32[]{:S(2)}, u32[]{:S(2)}) collective-permute-start(f32[512,384]{1,0:T(8,128)S(1)} %slice_select_fusion.7), channel_id=1, source_target_pairs={{0,64},{4,68},{8,72},{12,76},{16,80},{20,84},{24,88},{28,92},{32,9... | collective-permute-start | bytes 2359304 | tf_op jit(solution)/shard_map/ppermute | solution.py:14
  225.4 36.6 %collective-permute-start.8 = (f32[128,256]{1,0:T(8,128)S(1)}, f32[128,256]{1,0:T(8,128)S(1)}, u32[]{:S(2)}, u32[]{:S(2)}) collective-permute-start(f32[128,256]{1,0:T(8,128)S(1)} %slice_select_fusion.31), channel_id=1, source_target_pairs={{0,16},{4,20},{8,24},{12,28},{16,0},{20,4},{24,8},{28,12},{32,48},... | collective-permute-start | bytes 393224 | tf_op jit(solution)/shard_map/ppermute | solution.py:14
  288.7 71.5 %collective-permute-start.40 = (f32[1024,384]{1,0:T(8,128)S(1)}, f32[1024,384]{1,0:T(8,128)S(1)}, u32[]{:S(2)}, u32[]{:S(2)}) collective-permute-start(f32[1024,384]{1,0:T(8,128)S(1)} %slice_select_fusion.2), channel_id=1, source_target_pairs={{0,64},{4,68},{8,72},{12,76},{16,80},{20,84},{24,88},{28,92},{32,9... | collective-permute-start | bytes 4718600 | tf_op jit(solution)/shard_map/ppermute | solution.py:14
  291.9 69.3 %collective-permute-start.36 = (f32[64,256]{1,0:T(8,128)S(1)}, f32[64,256]{1,0:T(8,128)S(1)}, u32[]{:S(2)}, u32[]{:S(2)}) collective-permute-start(f32[64,256]{1,0:T(8,128)S(1)} %copy-done.3), channel_id=1, source_target_pairs={{0,4},{4,0},{8,12},{12,8},{16,20},{20,16},{24,28},{28,24},{32,36},... | collective-permute-start | bytes 196616 | tf_op jit(solution)/shard_map/ppermute | solution.py:14
  360.5 20.0 %collective-permute-start.41 = (f32[512,384]{1,0:T(8,128)S(1)}, f32[512,384]{1,0:T(8,128)S(1)}, u32[]{:S(2)}, u32[]{:S(2)}) collective-permute-start(f32[512,384]{1,0:T(8,128)S(1)} %slice_select_fusion.6), channel_id=1, source_target_pairs={{0,32},{4,36},{8,40},{12,44},{16,48},{20,52},{24,56},{28,60},{32,0... | collective-permute-start | bytes 2359304 | tf_op jit(solution)/shard_map/ppermute | solution.py:14
  380.7 15.6 %collective-permute-start.42 = (f32[256,384]{1,0:T(8,128)S(1)}, f32[256,384]{1,0:T(8,128)S(1)}, u32[]{:S(2)}, u32[]{:S(2)}) collective-permute-start(f32[256,384]{1,0:T(8,128)S(1)} %slice_select_fusion.16), channel_id=1, source_target_pairs={{0,16},{4,20},{8,24},{12,28},{16,0},{20,4},{24,8},{28,12},{32,48},... | collective-permute-start | bytes 1179656 | tf_op jit(solution)/shard_map/ppermute | solution.py:14
  409.5 267.4 %reduce-scatter.8.cloned.1.call-start = ((), (), s32[]{:S(2)}) async-start(), calls=%async_computation.5 | async-start | bytes 1474560 | tf_op jit(solution)/shard_map/reduce_scatter | solution.py:87
  411.3 31.0 %collective-permute-start.48 = (f32[512,256]{1,0:T(8,128)S(1)}, f32[512,256]{1,0:T(8,128)S(1)}, u32[]{:S(2)}, u32[]{:S(2)}) collective-permute-start(f32[512,256]{1,0:T(8,128)S(1)} %maximum_select_fusion.17), channel_id=1, source_target_pairs={{0,32},{4,36},{8,40},{12,44},{16,48},{20,52},{24,56},{28,60},{32,0... | collective-permute-start | bytes 1572872 | tf_op jit(solution)/shard_map/ppermute | solution.py:14
  446.5 29.4 %collective-permute-start.49 = (f32[512,512]{1,0:T(8,128)}, f32[512,512]{1,0:T(8,128)}, u32[]{:S(2)}, u32[]{:S(2)}) collective-permute-start(f32[512,512]{1,0:T(8,128)} %slice_select_fusion.4), channel_id=1, source_target_pairs={{0,32},{4,36},{8,40},{12,44},{16,48},{20,52},{24,56},{28,60},{32,0... | collective-permute-start | bytes 3145736 | tf_op jit(solution)/shard_map/ppermute | solution.py:14
  448.2 24.4 %collective-permute-start.32 = (f32[512,256]{1,0:T(8,128)}, f32[512,256]{1,0:T(8,128)}, u32[]{:S(2)}, u32[]{:S(2)}) collective-permute-start(f32[512,256]{1,0:T(8,128)} %slice_select_fusion.11), channel_id=1, source_target_pairs={{0,32},{4,36},{8,40},{12,44},{16,48},{20,52},{24,56},{28,60},{32,0... | collective-permute-start | bytes 1572872 | tf_op jit(solution)/shard_map/ppermute | solution.py:14
  513.2 69.6 %collective-permute-start.59 = (f32[1536,512]{1,0:T(8,128)S(1)}, f32[1536,512]{1,0:T(8,128)S(1)}, u32[]{:S(2)}, u32[]{:S(2)}) collective-permute-start(f32[1536,512]{1,0:T(8,128)S(1)} %slice_select_fusion), channel_id=1, source_target_pairs={{0,32},{4,36},{8,40},{12,44},{16,48},{20,52},{24,56},{28,60},{32,0... | collective-permute-start | bytes 9437192 | tf_op jit(solution)/shard_map/ppermute | solution.py:14
  584.4 36.5 %collective-permute-start.60 = (f32[768,512]{1,0:T(8,128)S(1)}, f32[768,512]{1,0:T(8,128)S(1)}, u32[]{:S(2)}, u32[]{:S(2)}) collective-permute-start(f32[768,512]{1,0:T(8,128)S(1)} %slice_select_fusion.1), channel_id=1, source_target_pairs={{0,16},{4,20},{8,24},{12,28},{16,0},{20,4},{24,8},{28,12},{32,48},... | collective-permute-start | bytes 4718600 | tf_op jit(solution)/shard_map/ppermute | solution.py:14
  621.6 17.3 %collective-permute-start.61 = (f32[384,512]{1,0:T(8,128)S(1)}, f32[384,512]{1,0:T(8,128)S(1)}, u32[]{:S(2)}, u32[]{:S(2)}) collective-permute-start(f32[384,512]{1,0:T(8,128)S(1)} %slice_select_fusion.5), channel_id=1, source_target_pairs={{0,8},{4,12},{8,0},{12,4},{16,24},{20,28},{24,16},{28,20},{32,40},... | collective-permute-start | bytes 2359304 | tf_op jit(solution)/shard_map/ppermute | solution.py:14
  645.9 65.9 %all-gather.2.cloned.1.call-start = ((), (), s32[]{:S(2)}) async-start(), calls=%async_computation.6 | async-start | bytes 1474560 | tf_op jit(solution)/shard_map/all_gather | solution.py:41
  655.1 21.8 %collective-permute-start.58 = (f32[512,256]{1,0:T(8,128)S(1)}, f32[512,256]{1,0:T(8,128)S(1)}, u32[]{:S(2)}, u32[]{:S(2)}) collective-permute-start(f32[512,256]{1,0:T(8,128)S(1)} %maximum_select_fusion.18), channel_id=1, source_target_pairs={{0,16},{4,20},{8,24},{12,28},{16,0},{20,4},{24,8},{28,12},{32,48},... | collective-permute-start | bytes 1572872 | tf_op jit(solution)/shard_map/ppermute | solution.py:14
  690.2 21.6 %collective-permute-start.65 = (f32[768,256]{1,0:T(8,128)S(1)}, f32[768,256]{1,0:T(8,128)}, u32[]{:S(2)}, u32[]{:S(2)}) collective-permute-start(f32[768,256]{1,0:T(8,128)S(1)} %maximum_select_fusion.12), channel_id=1, source_target_pairs={{0,16},{4,20},{8,24},{12,28},{16,0},{20,4},{24,8},{28,12},{32,48},... | collective-permute-start | bytes 2359304 | tf_op jit(solution)/shard_map/ppermute | solution.py:14
  717.0 41.3 %collective-permute-start.66 = (f32[512,640]{1,0:T(8,128)S(1)}, f32[512,640]{1,0:T(8,128)S(1)}, u32[]{:S(2)}, u32[]{:S(2)}) collective-permute-start(f32[512,640]{1,0:T(8,128)S(1)} %slice_select_fusion.3), channel_id=1, source_target_pairs={{0,16},{4,20},{8,24},{12,28},{16,0},{20,4},{24,8},{28,12},{32,48},... | collective-permute-start | bytes 3932168 | tf_op jit(solution)/shard_map/ppermute | solution.py:14
  730.7 27.5 %collective-permute-start.53 = (f32[512,256]{1,0:T(8,128)S(1)}, f32[512,256]{1,0:T(8,128)S(1)}, u32[]{:S(2)}, u32[]{:S(2)}) collective-permute-start(f32[512,256]{1,0:T(8,128)S(1)} %slice_select_fusion.9), channel_id=1, source_target_pairs={{0,16},{4,20},{8,24},{12,28},{16,0},{20,4},{24,8},{28,12},{32,48},... | collective-permute-start | bytes 1572872 | tf_op jit(solution)/shard_map/ppermute | solution.py:14
  758.6 19.2 %collective-permute-start.67 = (f32[256,640]{1,0:T(8,128)S(1)}, f32[256,640]{1,0:T(8,128)S(1)}, u32[]{:S(2)}, u32[]{:S(2)}) collective-permute-start(f32[256,640]{1,0:T(8,128)S(1)} %slice_select_fusion.8), channel_id=1, source_target_pairs={{0,8},{4,12},{8,0},{12,4},{16,24},{20,28},{24,16},{28,20},{32,40},... | collective-permute-start | bytes 1966088 | tf_op jit(solution)/shard_map/ppermute | solution.py:14
  758.9 18.8 %collective-permute-start.54 = (f32[256,256]{1,0:T(8,128)S(1)}, f32[256,256]{1,0:T(8,128)S(1)}, u32[]{:S(2)}, u32[]{:S(2)}) collective-permute-start(f32[256,256]{1,0:T(8,128)S(1)} %slice_select_fusion.18), channel_id=1, source_target_pairs={{0,8},{4,12},{8,0},{12,4},{16,24},{20,28},{24,16},{28,20},{32,40},... | collective-permute-start | bytes 786440 | tf_op jit(solution)/shard_map/ppermute | solution.py:14
  (58 other events, 503.0 us)
Sparse Core Ops, SparseCore 0:
  191.9 19.0 reduce-scatter.3
  409.6 18.9 reduce-scatter.5
  646.0 30.8 reduce-scatter.7
  678.6 31.3 all-gather.1
where the time goes:
time: 799 us; the launch traced here: 791 us
  waiting for transfers between devices  463 us (58%)
  blocking collectives  132 us (17%)
  starting transfers between devices  129 us (16%)
  matrix products  30.3 us (4%)
  other arithmetic  21.7 us (3%)
  between operations  15 us (2%)
    ppermute x69, waiting for transfers between devices, swapped(): lax.ppermute(array, axis, [(i, i ^ 1 << distance) for i in range(lax.axis...  450 us
    all_gather x12, blocking collectives, whole_rows(): return lax.all_gather(values, 'blk', axis=1, tiled=True)  132 us
    ppermute x69, starting transfers between devices, swapped(): lax.ppermute(array, axis, [(i, i ^ 1 << distance) for i in range(lax.axis...  129 us
    dot_general x13, matrix products, inner_product(): lax.dot_general(left, right, (((0,), (0,)), ((), ())), precision=lax.Prec...  17.6 us
  transfers between devices with their start and end apart: 73, of which 45 were waited for; matrix products, arithmetic and copies ran while one was open for 4% of the time, Pallas kernels for 0%

commit v1 on v0

v1 whole, which is shorter than its diff:
```python
import jax
import jax.numpy as jnp
from jax import lax
from jax.sharding import Mesh, PartitionSpec as P

S = 1024
BLOCK = 128
U1 = 512
U2 = 1024
U3 = 1536
COLS = 256
PRECISION = lax.Precision.HIGH


def product(left, right):
    return jnp.dot(left, right, precision=PRECISION, preferred_element_type=jnp.float32)


def inner_product(left, right):
    return lax.dot_general(
        left,
        right,
        (((0,), (0,)), ((), ())),
        precision=PRECISION,
        preferred_element_type=jnp.float32,
    )


def swapped(array, axis, distance):
    return lax.ppermute(array, axis, [(i, i ^ distance) for i in range(lax.axis_size(axis))])


def gathered(values, axes, parts):
    spread = jnp.broadcast_to(values[None], (parts,) + values.shape)
    return lax.all_to_all(spread, axes, 0, 0)


def paired(values, axis, stack_axis):
    other = swapped(values, axis, 1)
    second = lax.axis_index(axis) == 1
    return jnp.where(
        second, jnp.stack([other, values], stack_axis), jnp.stack([values, other], stack_axis)
    )


def wide(pieces):
    return jnp.concatenate([pieces[part] for part in range(pieces.shape[0])], 1)


def gathered_x(values):
    me = lax.axis_index("x")
    rows = values.shape[0]
    out = jnp.zeros((rows, 4 * COLS), values.dtype)
    for distance in (0, 1, 3, 2):
        piece = swapped(values, "x", distance) if distance else values
        out = lax.dynamic_update_slice(out, piece, (0, (me ^ distance) * COLS))
    return out


def group_rows(values):
    return paired(gathered(values, "y", 4), "c", 1)


def group_sums(partial):
    core = lax.axis_index("c")
    keeping = lax.dynamic_index_in_dim(partial, core, 1, keepdims=False)
    sending = lax.dynamic_index_in_dim(partial, 1 - core, 1, keepdims=False)
    half = keeping + swapped(sending, "c", 1)
    return jnp.sum(lax.all_to_all(half, "y", 0, 0), 0)


def chosen(rows, selector, count):
    return jnp.concatenate(
        [
            lax.dynamic_slice_in_dim(rows, selector[block] * BLOCK, BLOCK, 1)
            for block in range(count)
        ],
        1,
    )


def columns(rows, start, length):
    return lax.dynamic_slice_in_dim(rows, start, length, 1)


def split(rows):
    return rows.reshape(4, 2, rows.shape[0] // 8, COLS)


def shards(v0, v1, b1, selector_1, v2, b2, selector_2, v3, b3, selector_3):
    half = lax.axis_index("h")
    quarter = lax.axis_index("q")
    pair = lax.axis_index("p")
    front_1 = half
    front_2 = half * 2 + quarter
    front_3 = front_2 * 2 + pair
    slot_1 = quarter * 2 + pair
    mine_1 = lax.dynamic_index_in_dim(selector_1, front_1, 0, keepdims=False)
    mine_2 = lax.dynamic_index_in_dim(selector_2, front_2, 0, keepdims=False)
    mine_3 = lax.dynamic_index_in_dim(selector_3, front_3, 0, keepdims=False)

    level_2 = paired(jnp.concatenate([v2, b2], 0), "p", 0)
    level_1 = gathered(jnp.concatenate([v1, b1], 0), ("q", "p"), 4)
    level_0 = gathered(v0, ("h", "q", "p"), 8)
    v0 = level_0.reshape(128, COLS)
    v1 = level_1[:, :32].reshape(128, COLS)
    b1 = level_1[:, 32:].reshape(64, COLS)
    v2 = level_2[:, :64].reshape(128, COLS)
    b2 = level_2[:, 64:].reshape(128, COLS)

    factor_rows = gathered_x(jnp.concatenate([b1, b2, b3], 0))
    inverse_columns = group_rows(jnp.concatenate([v1, v2, v3], 0))
    v1_columns = (
        inverse_columns[:, :, :128].reshape(8, 4, 32, COLS).swapaxes(0, 1).reshape(S, COLS)
    )
    v2_columns = (
        inverse_columns[:, :, 128:256].reshape(8, 2, 64, COLS).swapaxes(0, 1).reshape(S, COLS)
    )
    v3_columns = inverse_columns[:, :, 256:].reshape(S, COLS)
    w1 = product(factor_rows[:64], v1_columns)
    w2 = product(factor_rows[64:192], v2_columns)
    w3 = product(factor_rows[192:], v3_columns)
    inverse_rows = gathered_x(jnp.concatenate([v0, v1, v2, v3], 0))
    coupling_columns = group_rows(jnp.concatenate([w1, w2, w3], 0))
    w1_columns = (
        coupling_columns[:, :, :64].reshape(8, 4, 16, COLS).swapaxes(0, 1).reshape(U1, COLS)
    )
    w2_columns = (
        coupling_columns[:, :, 64:192].reshape(8, 2, 64, COLS).swapaxes(0, 1).reshape(U2, COLS)
    )
    w3_columns = coupling_columns[:, :, 192:].reshape(U3, COLS)
    w3_rows = gathered_x(w3)

    v0_rows = inverse_rows[:128]
    v1_rows = inverse_rows[128:256]
    v2_rows = inverse_rows[256:384]
    v3_rows = inverse_rows[384:]
    f0 = chosen(v0_rows, mine_1, 4)
    m1 = product(f0, w1_columns)
    m1_rows = gathered_x(m1)
    x1 = jnp.concatenate(
        [
            jnp.concatenate([v1_rows, jnp.zeros((128, U1), jnp.float32)], 1),
            jnp.concatenate([-m1_rows, f0], 1),
        ],
        0,
    )
    f1 = chosen(x1, mine_2, 8)
    m2 = product(f1, w2_columns)
    m2_rows = gathered_x(m2)
    x2 = jnp.concatenate(
        [
            jnp.concatenate([v2_rows, jnp.zeros((128, U2), jnp.float32)], 1),
            jnp.concatenate([-m2_rows, f1], 1),
        ],
        0,
    )
    f2 = chosen(x2, mine_3, 12)
    m3 = product(f2, w3_columns)

    d0 = inner_product(columns(v0_rows, front_3 * 128, 128), v0)
    d1 = inner_product(
        columns(x1, slot_1 * 256, 256), jnp.concatenate([v1, -m1], 0)
    )
    e1 = -inner_product(columns(f0, slot_1 * 128, 128), m1)
    d2 = inner_product(columns(x2, pair * 512, 512), jnp.concatenate([v2, -m2], 0))
    e2 = -inner_product(columns(f1, pair * 512, 512), m2)
    e3 = -inner_product(f2, m3)
    summed = group_sums(
        jnp.concatenate([split(d0), split(d1), split(e1), split(d2), split(e2), split(e3)], 2)
    )
    d0 = summed[:16]
    d1 = summed[16:48]
    e1 = summed[48:64]
    d2 = summed[64:128]
    e2 = summed[128:192]
    e3 = summed[192:]
    d3 = group_sums(split(inner_product(v3_rows, v3) - inner_product(w3_rows, e3)))
    return d0, d1, e1, d2, e2, d3, e3


def solution(mesh):
    devices = mesh.devices.reshape(2, 2, 2, 4, 2, 4)
    fine = Mesh(devices, ("h", "q", "p", "y", "c", "x"))
    tiled = P(("h", "q", "p", "y", "c"), "x")
    return jax.shard_map(
        shards,
        mesh=fine,
        in_specs=(tiled, tiled, tiled, P(), tiled, tiled, P(), tiled, tiled, P()),
        out_specs=(tiled,) * 7,
        check_vma=False,
    )
```

time: 799 us -> 221 us (0.28)
  waiting for transfers between devices: 463 us -> 72.8 us
  blocking collectives: 132 us -> 21.1 us
  starting transfers between devices: 129 us -> 54 us
  local copies, waits for them, and re-layouts: 0.14 us -> 28.1 us
  matrix products: 30.3 us -> 10.4 us
    ppermute x69 -> x20, waiting for transfers between devices: 450 us -> 38.2 us  [swapped(): lax.ppermute(array, axis, [(i, i ^ distance) for i in range(lax.axis_size...]
    all_gather x12 -> x0, blocking collectives: 132 us -> none  [whole_rows(): return lax.all_gather(values, 'blk', axis=1, tiled=True)]
    ppermute x69 -> x20, starting transfers between devices: 129 us -> 30.8 us  [swapped(): lax.ppermute(array, axis, [(i, i ^ distance) for i in range(lax.axis_size...]
    all_to_all x0 -> x5, waiting for transfers between devices: none -> 34.6 us  [the longest x3 18 us: gathered(): return lax.all_to_all(spread, axes, 0, 0)]
    all_to_all x0 -> x5, starting transfers between devices: none -> 23.2 us  [the longest x3 15.3 us: gathered(): return lax.all_to_all(spread, axes, 0, 0)]
    all_to_all x0 -> x1, blocking collectives: none -> 21.1 us  [gathered(): return lax.all_to_all(spread, axes, 0, 0)]
    dot_general x22 -> x14, matrix products: 30.3 us -> 10.4 us  [the longest x8 6.88 us: inner_product(): lax.dot_general(left, right, (((0,), (0,)), ((), ())), precision=PRECISIO...]
    reduce_scatter x3 -> x0, waiting for transfers between devices: 12.4 us -> none  [sweep_level(): lax.psum_scatter(product(selected, picker), 'blk', scatter_dimension=1, t...]
  transfers between devices with their start and end apart: 73 -> 25, of which waited for: 45 -> 16; matrix products, arithmetic and copies ran while one was open for 4% -> 12% of each run, Pallas kernels for 0% -> 0%
where the time goes in v1:
time: 221 us; the launch traced here: 220 us
  waiting for transfers between devices  72.8 us (33%)
  starting transfers between devices  54 us (24%)
  local copies, waits for them, and re-layouts  28.1 us (13%)
  blocking collectives  21.1 us (10%)
  between operations  16.9 us (8%)
  other arithmetic  16.3 us (7%)
  matrix products  10.4 us (5%)
    ppermute x20, waiting for transfers between devices, swapped(): lax.ppermute(array, axis, [(i, i ^ distance) for i in range(lax.axis_size...  38.2 us
    ppermute x20, starting transfers between devices, swapped(): lax.ppermute(array, axis, [(i, i ^ distance) for i in range(lax.axis_size...  30.8 us
    all_to_all x1, blocking collectives, gathered(): return lax.all_to_all(spread, axes, 0, 0)  21.1 us
    all_to_all x3, waiting for transfers between devices, gathered(): return lax.all_to_all(spread, axes, 0, 0)  18 us
    all_to_all x2, waiting for transfers between devices, group_sums(): return jnp.sum(lax.all_to_all(half, 'y', 0, 0), 0)  16.5 us
    all_to_all x3, starting transfers between devices, gathered(): return lax.all_to_all(spread, axes, 0, 0)  15.3 us
    all_to_all x2, starting transfers between devices, group_sums(): return jnp.sum(lax.all_to_all(half, 'y', 0, 0), 0)  7.96 us
    dot_general x8, matrix products, inner_product(): lax.dot_general(left, right, (((0,), (0,)), ((), ())), precision=PRECISIO...  6.88 us
  transfers between devices with their start and end apart: 25, of which 16 were waited for; matrix products, arithmetic and copies ran while one was open for 12% of the time, Pallas kernels for 0%

profile of v1, /device:TPU:1, one launch (start us, length us, event | category | flops | bytes accessed | tf_op | source)
XLA Modules:
  0.0 219.6 jit_solution(17074981525978478851)
XLA Ops:
  2.4 2.5 %collective-permute-start = (f32[128,256]{1,0:T(8,128)S(1)}, f32[128,256]{1,0:T(8,128)S(1)}, u32[]{:S(2)}, u32[]{:S(2)}) collective-permute-start(f32[128,256]{1,0:T(8,128)S(1)} %constant_dynamic-update-slice_fusion), channel_id=1, source_target_pairs={{0,32},{32,0},{1,33},{33,1},{2,34},{34,2},{3,35},{35,3},{4,36},{36... | collective-permute-start | bytes 393224 | tf_op jit(solution)/shard_map/ppermute | solution.py:30
  6.3 4.3 %all-to-all-start.1 = ((f32[4,48,256]{2,1,0:T(8,128)}), f32[4,48,256]{2,1,0:T(8,128)S(1)}, u32[]{:S(2)}, u32[]{:S(2)}) async-start(f32[4,48,256]{2,1,0:T(8,128)} %broadcast_in_dim.18), calls=%async_computation.1 | async-start | bytes 393216 | tf_op jit(solution)/shard_map/all_to_all | solution.py:35
  11.3 4.5 %all-to-all-done.1 = f32[4,48,256]{2,1,0:T(8,128)S(1)} async-done(((f32[4,48,256]{2,1,0:T(8,128)}), f32[4,48,256]{2,1,0:T(8,128)S(1)}, u32[]{:S(2)}, u32[]{:S(2)}) %all-to-all-start.1) | async-done | bytes 196640 | tf_op jit(solution)/shard_map/all_to_all | solution.py:35
  16.6 21.1 %all_to_all.30 = f32[4,384,256]{2,1,0:T(8,128)S(1)} all-to-all(f32[4,384,256]{2,1,0:T(8,128)S(1)} %broadcast_in_dim.20), channel_id=1, replica_groups=mesh['h'=2,'q'=2,'p'=2,'y'=4,'c'=2,'x'=4] {'y'}, dimensions={0} | all-to-all | bytes 3145728 | tf_op jit(solution)/shard_map/all_to_all | solution.py:35
  37.7 4.7 %collective-permute-start.7 = (f32[4,384,256]{2,1,0:T(8,128)S(1)}, f32[4,384,256]{2,1,0:T(8,128)}, u32[]{:S(2)}, u32[]{:S(2)}) collective-permute-start(f32[4,384,256]{2,1,0:T(8,128)S(1)} %all_to_all.30), channel_id=1, source_target_pairs={{0,4},{4,0},{1,5},{5,1},{2,6},{6,2},{3,7},{7,3},{8,12},{12,8},{9,1... | collective-permute-start | bytes 4718600 | tf_op jit(solution)/shard_map/ppermute | solution.py:30
  42.6 1.8 pad_maximum_fusion.1
  45.6 1.8 collective-permute-start.5
  48.7 6.5 %all-to-all-start = ((f32[8,16,256]{2,1,0:T(8,128)}), f32[8,16,256]{2,1,0:T(8,128)S(1)}, u32[]{:S(2)}, u32[]{:S(2)}) async-start(f32[8,16,256]{2,1,0:T(8,128)} %broadcast_in_dim.17), calls=%async_computation | async-start | bytes 262144 | tf_op jit(solution)/shard_map/all_to_all | solution.py:35
  56.5 7.8 %collective-permute-done.5 = f32[384,256]{1,0:T(8,128)} collective-permute-done((f32[384,256]{1,0:T(8,128)}, f32[384,256]{1,0:T(8,128)}, u32[]{:S(2)}, u32[]{:S(2)}) %collective-permute-start.5) | collective-permute-done | bytes 393248 | tf_op jit(solution)/shard_map/ppermute | solution.py:30
  67.2 2.3 %maximum_select_fusion = f32[4,2,384,256]{3,2,1,0:T(8,128)S(1)} fusion(f32[4,1,384,256]{3,2,1,0:T(8,128)S(1)} %bitcast.93, f32[4,1,384,256]{3,2,1,0:T(8,128)} %bitcast.15, pred[]{:T(512)S(6)} %eq.8), kind=kLoop, calls=%fused_computation.2 | loop fusion | flops 2359296 | bytes 6291457 | tf_op jit(solution)/shard_map/jit(_where)/select_n | solution.py:41
  73.0 4.5 %all-to-all-start.3 = ((f32[4,384,256]{2,1,0:T(8,128)}), f32[4,384,256]{2,1,0:T(8,128)}, u32[]{:S(2)}, u32[]{:S(2)}) async-start(f32[4,384,256]{2,1,0:T(8,128)} %broadcast_in_dim.42), calls=%async_computation.3 | async-start | bytes 3145728 | tf_op jit(solution)/shard_map/all_to_all | solution.py:35
  80.0 2.7 %collective-permute-start.2 = (f32[512,256]{1,0:T(8,128)}, f32[512,256]{1,0:T(8,128)}, u32[]{:S(2)}, u32[]{:S(2)}) collective-permute-start(f32[512,256]{1,0:T(8,128)} %get-tuple-element.18), channel_id=1, source_target_pairs={{0,3},{1,2},{2,1},{3,0},{4,7},{5,6},{6,5},{7,4},{8,11},{9,10},{10,... | collective-permute-start | bytes 1572872 | tf_op jit(solution)/shard_map/ppermute | solution.py:30
  82.7 13.5 %all-to-all-done.3 = f32[4,384,256]{2,1,0:T(8,128)} async-done(((f32[4,384,256]{2,1,0:T(8,128)}), f32[4,384,256]{2,1,0:T(8,128)}, u32[]{:S(2)}, u32[]{:S(2)}) %all-to-all-start.3) | async-done | bytes 1572896 | tf_op jit(solution)/shard_map/all_to_all | solution.py:35
  96.3 2.9 %collective-permute-start.8 = (f32[4,384,256]{2,1,0:T(8,128)}, f32[4,384,256]{2,1,0:T(8,128)}, u32[]{:S(2)}, u32[]{:S(2)}) collective-permute-start(f32[4,384,256]{2,1,0:T(8,128)} %all-to-all-done.3), channel_id=1, source_target_pairs={{0,4},{4,0},{1,5},{5,1},{2,6},{6,2},{3,7},{7,3},{8,12},{12,8},{9,1... | collective-permute-start | bytes 4718600 | tf_op jit(solution)/shard_map/ppermute | solution.py:30
  99.2 2.2 %collective-permute-start.3 = (f32[512,256]{1,0:T(8,128)}, f32[512,256]{1,0:T(8,128)}, u32[]{:S(2)}, u32[]{:S(2)}) collective-permute-start(f32[512,256]{1,0:T(8,128)} %get-tuple-element.18), channel_id=1, source_target_pairs={{0,2},{1,3},{2,0},{3,1},{4,6},{5,7},{6,4},{7,5},{8,10},{9,11},{10,... | collective-permute-start | bytes 1572872 | tf_op jit(solution)/shard_map/ppermute | solution.py:30
  125.9 3.3 %maximum_select_fusion.1 = f32[4,2,384,256]{3,2,1,0:T(8,128)S(1)} fusion(f32[4,1,384,256]{3,2,1,0:T(8,128)} %bitcast.25, f32[4,1,384,256]{3,2,1,0:T(8,128)} %bitcast.24, pred[]{:T(512)S(6)} %eq.8), kind=kLoop, calls=%fused_computation.3 | loop fusion | flops 2359296 | bytes 6291457 | tf_op jit(solution)/shard_map/jit(_where)/select_n | solution.py:41
  131.4 2.9 %collective-permute-start.11 = (f32[128,256]{1,0:T(8,128)S(1)}, f32[128,256]{1,0:T(8,128)S(1)}, u32[]{:S(2)}, u32[]{:S(2)}) collective-permute-start(f32[128,256]{1,0:T(8,128)S(1)} %get-tuple-element.56), channel_id=1, source_target_pairs={{0,2},{1,3},{2,0},{3,1},{4,6},{5,7},{6,4},{7,5},{8,10},{9,11},{10,... | collective-permute-start | bytes 393224 | tf_op jit(solution)/shard_map/ppermute | solution.py:30
  135.8 3.7 %collective-permute-done.11 = f32[128,256]{1,0:T(8,128)S(1)} collective-permute-done((f32[128,256]{1,0:T(8,128)S(1)}, f32[128,256]{1,0:T(8,128)S(1)}, u32[]{:S(2)}, u32[]{:S(2)}) %collective-permute-start.11) | collective-permute-done | bytes 131104 | tf_op jit(solution)/shard_map/ppermute | solution.py:30
  141.4 1.9 collective-permute-start.13
  144.6 8.2 %collective-permute-done.12 = f32[256,256]{1,0:T(8,128)S(1)} collective-permute-done((f32[256,256]{1,0:T(8,128)S(1)}, f32[256,256]{1,0:T(8,128)S(1)}, u32[]{:S(2)}, u32[]{:S(2)}) %collective-permute-start.12) | collective-permute-done | bytes 262176 | tf_op jit(solution)/shard_map/ppermute | solution.py:30
  152.8 3.4 %collective-permute-done.13 = f32[256,256]{1,0:T(8,128)S(1)} collective-permute-done((f32[256,256]{1,0:T(8,128)S(1)}, f32[256,256]{1,0:T(8,128)S(1)}, u32[]{:S(2)}, u32[]{:S(2)}) %collective-permute-start.13) | collective-permute-done | bytes 262176 | tf_op jit(solution)/shard_map/ppermute | solution.py:30
  160.4 2.1 convolution_negate_fusion
  163.5 1.6 copy-done.3
  166.9 3.4 %collective-permute-done.15 = f32[4,384,256]{2,1,0:T(8,128)} collective-permute-done((f32[4,384,256]{2,1,0:T(8,128)}, f32[4,384,256]{2,1,0:T(8,128)}, u32[]{:S(2)}, u32[]{:S(2)}) %collective-permute-start.15) | collective-permute-done | bytes 1572896 | tf_op jit(solution)/shard_map/ppermute | solution.py:30
  170.3 3.3 %bitcast_add_fusion = f32[4,384,256]{2,1,0:T(8,128)} fusion(f32[4,384,256]{2,1,0:T(8,128)} %collective-permute-done.15, f32[4,2,384,256]{3,2,1,0:T(8,128)} %copy-done.3, s32[]{:T(128)S(6)} %select_n.198), kind=kLoop, calls=%fused_computation.7 | loop fusion | flops 393216 | bytes 4718596 | tf_op jit(solution)/shard_map/add | solution.py:68
  173.5 4.5 %all-to-all-start.4 = ((f32[4,384,256]{2,1,0:T(8,128)}), f32[4,384,256]{2,1,0:T(8,128)}, u32[]{:S(2)}, u32[]{:S(2)}) async-start(f32[4,384,256]{2,1,0:T(8,128)} %bitcast_add_fusion), calls=%async_computation.4 | async-start | bytes 3145728 | tf_op jit(solution)/shard_map/all_to_all | solution.py:69
  179.1 2.2 %collective-permute-start.18 = (f32[192,256]{1,0:T(8,128)S(1)}, f32[192,256]{1,0:T(8,128)S(1)}, u32[]{:S(2)}, u32[]{:S(2)}) collective-permute-start(f32[192,256]{1,0:T(8,128)S(1)} %copy-done.10), channel_id=1, source_target_pairs={{0,2},{1,3},{2,0},{3,1},{4,6},{5,7},{6,4},{7,5},{8,10},{9,11},{10,... | collective-permute-start | bytes 589832 | tf_op jit(solution)/shard_map/ppermute | solution.py:30
  181.4 3.0 %collective-permute-done.16 = f32[192,256]{1,0:T(8,128)S(1)} collective-permute-done((f32[192,256]{1,0:T(8,128)S(1)}, f32[192,256]{1,0:T(8,128)S(1)}, u32[]{:S(2)}, u32[]{:S(2)}) %collective-permute-start.16) | collective-permute-done | bytes 196640 | tf_op jit(solution)/shard_map/ppermute | solution.py:30
  184.4 5.5 %collective-permute-done.17 = f32[192,256]{1,0:T(8,128)S(1)} collective-permute-done((f32[192,256]{1,0:T(8,128)S(1)}, f32[192,256]{1,0:T(8,128)S(1)}, u32[]{:S(2)}, u32[]{:S(2)}) %collective-permute-start.17) | collective-permute-done | bytes 196640 | tf_op jit(solution)/shard_map/ppermute | solution.py:30
  189.9 8.6 %all-to-all-done.4 = f32[4,384,256]{2,1,0:T(8,128)} async-done(((f32[4,384,256]{2,1,0:T(8,128)}), f32[4,384,256]{2,1,0:T(8,128)}, u32[]{:S(2)}, u32[]{:S(2)}) %all-to-all-start.4) | async-done | bytes 1572896 | tf_op jit(solution)/shard_map/all_to_all | solution.py:69
  206.3 3.5 %all-to-all-start.5 = ((f32[4,128,256]{2,1,0:T(8,128)}), f32[4,128,256]{2,1,0:T(8,128)S(1)}, u32[]{:S(2)}, u32[]{:S(2)}) async-start(f32[4,128,256]{2,1,0:T(8,128)} %bitcast_add_fusion.1), calls=%async_computation.5 | async-start | bytes 1048576 | tf_op jit(solution)/shard_map/all_to_all | solution.py:69
  211.0 7.9 %all-to-all-done.5 = f32[4,128,256]{2,1,0:T(8,128)S(1)} async-done(((f32[4,128,256]{2,1,0:T(8,128)}), f32[4,128,256]{2,1,0:T(8,128)S(1)}, u32[]{:S(2)}, u32[]{:S(2)}) %all-to-all-start.5) | async-done | bytes 524320 | tf_op jit(solution)/shard_map/all_to_all | solution.py:69
  (171 shorter events, 50.7 us)
Async XLA Ops:
  0.6 109.1 %copy-start = (s32[8,12]{1,0:T(8,128)S(1)}, s32[8,12]{1,0:T(8,128)}, u32[]{:S(2)}) copy-start(s32[8,12]{1,0:T(8,128)} %param.19) | copy-start | bytes 1156
  0.6 15.1 %copy-start.6 = (f32[128,256]{1,0:T(8,128)S(1)}, f32[128,256]{1,0:T(8,128)}, u32[]{:S(2)}) copy-start(f32[128,256]{1,0:T(8,128)} %param.17) | copy-start | bytes 393220
  2.4 8.2 %collective-permute-start = (f32[128,256]{1,0:T(8,128)S(1)}, f32[128,256]{1,0:T(8,128)S(1)}, u32[]{:S(2)}, u32[]{:S(2)}) collective-permute-start(f32[128,256]{1,0:T(8,128)S(1)} %constant_dynamic-update-slice_fusion), channel_id=1, source_target_pairs={{0,32},{32,0},{1,33},{33,1},{2,34},{34,2},{3,35},{35,3},{4,36},{36... | collective-permute-start | bytes 393224 | tf_op jit(solution)/shard_map/ppermute | solution.py:30
  6.3 9.4 %all-to-all-start.1 = ((f32[4,48,256]{2,1,0:T(8,128)}), f32[4,48,256]{2,1,0:T(8,128)S(1)}, u32[]{:S(2)}, u32[]{:S(2)}) async-start(f32[4,48,256]{2,1,0:T(8,128)} %broadcast_in_dim.18), calls=%async_computation.1 | async-start | bytes 393216 | tf_op jit(solution)/shard_map/all_to_all | solution.py:35
  16.6 26.0 %slice-start.1 = ((f32[4,48,256]{2,1,0:T(8,128)}), f32[4,16,256]{2,1,0:T(8,128)S(1)}, s32[]{:S(2)}) async-start(f32[4,48,256]{2,1,0:T(8,128)} %copy-done.11), calls=%async_computation.7 | async-start | bytes 131072 | tf_op jit(solution)/shard_map/slice | solution.py:107
  37.7 10.3 %copy-start.13 = (f32[16,256]{1,0:T(8,128)S(1)}, f32[16,256]{1,0:T(8,128)}, u32[]{:S(2)}) copy-start(f32[16,256]{1,0:T(8,128)} %param.10) | copy-start | bytes 49156
  37.7 29.4 %collective-permute-start.7 = (f32[4,384,256]{2,1,0:T(8,128)S(1)}, f32[4,384,256]{2,1,0:T(8,128)}, u32[]{:S(2)}, u32[]{:S(2)}) collective-permute-start(f32[4,384,256]{2,1,0:T(8,128)S(1)} %all_to_all.30), channel_id=1, source_target_pairs={{0,4},{4,0},{1,5},{5,1},{2,6},{6,2},{3,7},{7,3},{8,12},{12,8},{9,1... | collective-permute-start | bytes 4718600 | tf_op jit(solution)/shard_map/ppermute | solution.py:30
  44.4 11.1 %collective-permute-start.4 = (f32[384,256]{1,0:T(8,128)}, f32[384,256]{1,0:T(8,128)}, u32[]{:S(2)}, u32[]{:S(2)}) collective-permute-start(f32[384,256]{1,0:T(8,128)} %get-tuple-element.24), channel_id=1, source_target_pairs={{0,1},{1,0},{2,3},{3,2},{4,5},{5,4},{6,7},{7,6},{8,9},{9,8},{10,11... | collective-permute-start | bytes 1179656 | tf_op jit(solution)/shard_map/ppermute | solution.py:30
  45.6 18.6 %collective-permute-start.5 = (f32[384,256]{1,0:T(8,128)}, f32[384,256]{1,0:T(8,128)}, u32[]{:S(2)}, u32[]{:S(2)}) collective-permute-start(f32[384,256]{1,0:T(8,128)} %get-tuple-element.24), channel_id=1, source_target_pairs={{0,3},{1,2},{2,1},{3,0},{4,7},{5,6},{6,5},{7,4},{8,11},{9,10},{10,... | collective-permute-start | bytes 1179656 | tf_op jit(solution)/shard_map/ppermute | solution.py:30
  47.4 18.7 %collective-permute-start.6 = (f32[384,256]{1,0:T(8,128)}, f32[384,256]{1,0:T(8,128)}, u32[]{:S(2)}, u32[]{:S(2)}) collective-permute-start(f32[384,256]{1,0:T(8,128)} %get-tuple-element.24), channel_id=1, source_target_pairs={{0,2},{1,3},{2,0},{3,1},{4,6},{5,7},{6,4},{7,5},{8,10},{9,11},{10,... | collective-permute-start | bytes 1179656 | tf_op jit(solution)/shard_map/ppermute | solution.py:30
  48.7 22.8 %all-to-all-start = ((f32[8,16,256]{2,1,0:T(8,128)}), f32[8,16,256]{2,1,0:T(8,128)S(1)}, u32[]{:S(2)}, u32[]{:S(2)}) async-start(f32[8,16,256]{2,1,0:T(8,128)} %broadcast_in_dim.17), calls=%async_computation | async-start | bytes 262144 | tf_op jit(solution)/shard_map/all_to_all | solution.py:35
  73.0 23.3 %all-to-all-start.3 = ((f32[4,384,256]{2,1,0:T(8,128)}), f32[4,384,256]{2,1,0:T(8,128)}, u32[]{:S(2)}, u32[]{:S(2)}) async-start(f32[4,384,256]{2,1,0:T(8,128)} %broadcast_in_dim.42), calls=%async_computation.3 | async-start | bytes 3145728 | tf_op jit(solution)/shard_map/all_to_all | solution.py:35
  77.5 21.7 %copy-start.14 = (s32[2,4]{1,0:T(2,128)S(1)}, s32[2,4]{1,0:T(2,128)}, u32[]{:S(2)}) copy-start(s32[2,4]{1,0:T(2,128)} %param.13) | copy-start | bytes 100
  79.3 38.7 %collective-permute-start.1 = (f32[512,256]{1,0:T(8,128)}, f32[512,256]{1,0:T(8,128)}, u32[]{:S(2)}, u32[]{:S(2)}) collective-permute-start(f32[512,256]{1,0:T(8,128)} %get-tuple-element.18), channel_id=1, source_target_pairs={{0,1},{1,0},{2,3},{3,2},{4,5},{5,4},{6,7},{7,6},{8,9},{9,8},{10,11... | collective-permute-start | bytes 1572872 | tf_op jit(solution)/shard_map/ppermute | solution.py:30
  80.0 39.2 %collective-permute-start.2 = (f32[512,256]{1,0:T(8,128)}, f32[512,256]{1,0:T(8,128)}, u32[]{:S(2)}, u32[]{:S(2)}) collective-permute-start(f32[512,256]{1,0:T(8,128)} %get-tuple-element.18), channel_id=1, source_target_pairs={{0,3},{1,2},{2,1},{3,0},{4,7},{5,6},{6,5},{7,4},{8,11},{9,10},{10,... | collective-permute-start | bytes 1572872 | tf_op jit(solution)/shard_map/ppermute | solution.py:30
  96.3 29.6 %collective-permute-start.8 = (f32[4,384,256]{2,1,0:T(8,128)}, f32[4,384,256]{2,1,0:T(8,128)}, u32[]{:S(2)}, u32[]{:S(2)}) collective-permute-start(f32[4,384,256]{2,1,0:T(8,128)} %all-to-all-done.3), channel_id=1, source_target_pairs={{0,4},{4,0},{1,5},{5,1},{2,6},{6,2},{3,7},{7,3},{8,12},{12,8},{9,1... | collective-permute-start | bytes 4718600 | tf_op jit(solution)/shard_map/ppermute | solution.py:30
  99.2 21.1 %collective-permute-start.3 = (f32[512,256]{1,0:T(8,128)}, f32[512,256]{1,0:T(8,128)}, u32[]{:S(2)}, u32[]{:S(2)}) collective-permute-start(f32[512,256]{1,0:T(8,128)} %get-tuple-element.18), channel_id=1, source_target_pairs={{0,2},{1,3},{2,0},{3,1},{4,6},{5,7},{6,4},{7,5},{8,10},{9,11},{10,... | collective-permute-start | bytes 1572872 | tf_op jit(solution)/shard_map/ppermute | solution.py:30
  129.7 6.1 %collective-permute-start.10 = (f32[128,256]{1,0:T(8,128)S(1)}, f32[128,256]{1,0:T(8,128)S(1)}, u32[]{:S(2)}, u32[]{:S(2)}) collective-permute-start(f32[128,256]{1,0:T(8,128)S(1)} %get-tuple-element.56), channel_id=1, source_target_pairs={{0,3},{1,2},{2,1},{3,0},{4,7},{5,6},{6,5},{7,4},{8,11},{9,10},{10,... | collective-permute-start | bytes 393224 | tf_op jit(solution)/shard_map/ppermute | solution.py:30
  130.3 4.8 %collective-permute-start.9 = (f32[128,256]{1,0:T(8,128)S(1)}, f32[128,256]{1,0:T(8,128)S(1)}, u32[]{:S(2)}, u32[]{:S(2)}) collective-permute-start(f32[128,256]{1,0:T(8,128)S(1)} %get-tuple-element.56), channel_id=1, source_target_pairs={{0,1},{1,0},{2,3},{3,2},{4,5},{5,4},{6,7},{7,6},{8,9},{9,8},{10,11... | collective-permute-start | bytes 393224 | tf_op jit(solution)/shard_map/ppermute | solution.py:30
  131.4 8.0 %collective-permute-start.11 = (f32[128,256]{1,0:T(8,128)S(1)}, f32[128,256]{1,0:T(8,128)S(1)}, u32[]{:S(2)}, u32[]{:S(2)}) collective-permute-start(f32[128,256]{1,0:T(8,128)S(1)} %get-tuple-element.56), channel_id=1, source_target_pairs={{0,2},{1,3},{2,0},{3,1},{4,6},{5,7},{6,4},{7,5},{8,10},{9,11},{10,... | collective-permute-start | bytes 393224 | tf_op jit(solution)/shard_map/ppermute | solution.py:30
  140.8 15.5 %collective-permute-start.14 = (f32[256,256]{1,0:T(8,128)S(1)}, f32[256,256]{1,0:T(8,128)S(1)}, u32[]{:S(2)}, u32[]{:S(2)}) collective-permute-start(f32[256,256]{1,0:T(8,128)S(1)} %get-tuple-element.57), channel_id=1, source_target_pairs={{0,2},{1,3},{2,0},{3,1},{4,6},{5,7},{6,4},{7,5},{8,10},{9,11},{10,... | collective-permute-start | bytes 786440 | tf_op jit(solution)/shard_map/ppermute | solution.py:30
  141.4 14.8 %collective-permute-start.13 = (f32[256,256]{1,0:T(8,128)S(1)}, f32[256,256]{1,0:T(8,128)S(1)}, u32[]{:S(2)}, u32[]{:S(2)}) collective-permute-start(f32[256,256]{1,0:T(8,128)S(1)} %get-tuple-element.57), channel_id=1, source_target_pairs={{0,3},{1,2},{2,1},{3,0},{4,7},{5,6},{6,5},{7,4},{8,11},{9,10},{10,... | collective-permute-start | bytes 786440 | tf_op jit(solution)/shard_map/ppermute | solution.py:30
  143.3 9.5 %collective-permute-start.12 = (f32[256,256]{1,0:T(8,128)S(1)}, f32[256,256]{1,0:T(8,128)S(1)}, u32[]{:S(2)}, u32[]{:S(2)}) collective-permute-start(f32[256,256]{1,0:T(8,128)S(1)} %get-tuple-element.57), channel_id=1, source_target_pairs={{0,1},{1,0},{2,3},{3,2},{4,5},{5,4},{6,7},{7,6},{8,9},{9,8},{10,11... | collective-permute-start | bytes 786440 | tf_op jit(solution)/shard_map/ppermute | solution.py:30
  166.4 3.9 %collective-permute-start.15 = (f32[4,384,256]{2,1,0:T(8,128)}, f32[4,384,256]{2,1,0:T(8,128)}, u32[]{:S(2)}, u32[]{:S(2)}) collective-permute-start(f32[4,384,256]{2,1,0:T(8,128)} %dynamic-slice_bitcast_fusion), channel_id=1, source_target_pairs={{0,4},{4,0},{1,5},{5,1},{2,6},{6,2},{3,7},{7,3},{8,12},{12,8},{9,1... | collective-permute-start | bytes 4718600 | tf_op jit(solution)/shard_map/ppermute | solution.py:30
  173.5 25.0 %all-to-all-start.4 = ((f32[4,384,256]{2,1,0:T(8,128)}), f32[4,384,256]{2,1,0:T(8,128)}, u32[]{:S(2)}, u32[]{:S(2)}) async-start(f32[4,384,256]{2,1,0:T(8,128)} %bitcast_add_fusion), calls=%async_computation.4 | async-start | bytes 3145728 | tf_op jit(solution)/shard_map/all_to_all | solution.py:69
  178.0 6.3 %collective-permute-start.16 = (f32[192,256]{1,0:T(8,128)S(1)}, f32[192,256]{1,0:T(8,128)S(1)}, u32[]{:S(2)}, u32[]{:S(2)}) collective-permute-start(f32[192,256]{1,0:T(8,128)S(1)} %copy-done.10), channel_id=1, source_target_pairs={{0,1},{1,0},{2,3},{3,2},{4,5},{5,4},{6,7},{7,6},{8,9},{9,8},{10,11... | collective-permute-start | bytes 589832 | tf_op jit(solution)/shard_map/ppermute | solution.py:30
  178.1 11.7 %collective-permute-start.17 = (f32[192,256]{1,0:T(8,128)S(1)}, f32[192,256]{1,0:T(8,128)S(1)}, u32[]{:S(2)}, u32[]{:S(2)}) collective-permute-start(f32[192,256]{1,0:T(8,128)S(1)} %copy-done.10), channel_id=1, source_target_pairs={{0,3},{1,2},{2,1},{3,0},{4,7},{5,6},{6,5},{7,4},{8,11},{9,10},{10,... | collective-permute-start | bytes 589832 | tf_op jit(solution)/shard_map/ppermute | solution.py:30
  179.1 10.8 %collective-permute-start.18 = (f32[192,256]{1,0:T(8,128)S(1)}, f32[192,256]{1,0:T(8,128)S(1)}, u32[]{:S(2)}, u32[]{:S(2)}) collective-permute-start(f32[192,256]{1,0:T(8,128)S(1)} %copy-done.10), channel_id=1, source_target_pairs={{0,2},{1,3},{2,0},{3,1},{4,6},{5,7},{6,4},{7,5},{8,10},{9,11},{10,... | collective-permute-start | bytes 589832 | tf_op jit(solution)/shard_map/ppermute | solution.py:30
  189.9 11.9 %copy-start.8 = (f32[128,256]{1,0:T(8,128)S(1)}, f32[128,256]{1,0:T(8,128)}, u32[]{:S(2)}) copy-start(f32[128,256]{1,0:T(8,128)} %param.17) | copy-start | bytes 393220
  202.5 17.1 %copy-start.1 = (s32[8,12]{1,0:T(8,128)S(1)}, s32[8,12]{1,0:T(8,128)}, u32[]{:S(2)}) copy-start(s32[8,12]{1,0:T(8,128)} %param.19) | copy-start | bytes 1156
  202.6 2.8 %collective-permute-start.19 = (f32[4,128,256]{2,1,0:T(8,128)S(1)}, f32[4,128,256]{2,1,0:T(8,128)S(1)}, u32[]{:S(2)}, u32[]{:S(2)}) collective-permute-start(f32[4,128,256]{2,1,0:T(8,128)S(1)} %dynamic-slice_bitcast_fusion.1), channel_id=1, source_target_pairs={{0,4},{4,0},{1,5},{5,1},{2,6},{6,2},{3,7},{7,3},{8,12},{12,8},{9,1... | collective-permute-start | bytes 1572872 | tf_op jit(solution)/shard_map/ppermute | solution.py:30
  206.3 12.7 %all-to-all-start.5 = ((f32[4,128,256]{2,1,0:T(8,128)}), f32[4,128,256]{2,1,0:T(8,128)S(1)}, u32[]{:S(2)}, u32[]{:S(2)}) async-start(f32[4,128,256]{2,1,0:T(8,128)} %bitcast_add_fusion.1), calls=%async_computation.5 | async-start | bytes 1048576 | tf_op jit(solution)/shard_map/all_to_all | solution.py:69
  (10 other events, 23.6 us)

commit v2 on v1

--- a/solution.py
+++ b/solution.py
@@ -100,44 +100,43 @@
     mine_3 = lax.dynamic_index_in_dim(selector_3, front_3, 0, keepdims=False)
 
     level_2 = paired(jnp.concatenate([v2, b2], 0), "p", 0)
-    level_1 = gathered(jnp.concatenate([v1, b1], 0), ("q", "p"), 4)
-    level_0 = gathered(v0, ("h", "q", "p"), 8)
-    v0 = level_0.reshape(128, COLS)
+    level_1 = paired(jnp.concatenate([v1, b1, v0], 0), "p", 0)
+    level_1 = paired(level_1, "q", 0).reshape(4, 64, COLS)
+    v0 = level_1[:, 48:].reshape(64, COLS)
+    v0 = jnp.concatenate([v0, swapped(v0, "h", 1)], 0)
     v1 = level_1[:, :32].reshape(128, COLS)
-    b1 = level_1[:, 32:].reshape(64, COLS)
+    b1 = level_1[:, 32:48].reshape(64, COLS)
     v2 = level_2[:, :64].reshape(128, COLS)
     b2 = level_2[:, 64:].reshape(128, COLS)
 
-    factor_rows = gathered_x(jnp.concatenate([b1, b2, b3], 0))
-    inverse_columns = group_rows(jnp.concatenate([v1, v2, v3], 0))
-    v1_columns = (
-        inverse_columns[:, :, :128].reshape(8, 4, 32, COLS).swapaxes(0, 1).reshape(S, COLS)
+    b3_rows = gathered_x(b3)
+    v3_columns = group_rows(v3).reshape(S, COLS)
+
+    b2_rows = gathered_x(b2)
+    early, v3_columns = lax.optimization_barrier(
+        (jnp.concatenate([v1, v2, b1], 0), v3_columns)
     )
-    v2_columns = (
-        inverse_columns[:, :, 128:256].reshape(8, 2, 64, COLS).swapaxes(0, 1).reshape(S, COLS)
-    )
-    v3_columns = inverse_columns[:, :, 256:].reshape(S, COLS)
-    w1 = product(factor_rows[:64], v1_columns)
-    w2 = product(factor_rows[64:192], v2_columns)
-    w3 = product(factor_rows[192:], v3_columns)
-    inverse_rows = gathered_x(jnp.concatenate([v0, v1, v2, v3], 0))
-    coupling_columns = group_rows(jnp.concatenate([w1, w2, w3], 0))
-    w1_columns = (
-        coupling_columns[:, :, :64].reshape(8, 4, 16, COLS).swapaxes(0, 1).reshape(U1, COLS)
+    w3 = product(b3_rows, v3_columns)
+    early = group_rows(early)
+    v1_columns = early[:, :, :128].reshape(8, 4, 32, COLS).swapaxes(0, 1).reshape(S, COLS)
+    v2_columns = early[:, :, 128:256].reshape(8, 2, 64, COLS).swapaxes(0, 1).reshape(S, COLS)
+    b1_columns = early[:, :, 256:].reshape(8, 4, 16, COLS).swapaxes(0, 1).reshape(U1, COLS)
+    w2 = product(b2_rows, v2_columns)
+    w2_part = gathered(w2, "y", 4)
+
+    v0_rows = gathered_x(v0)
+    f0 = chosen(v0_rows, mine_1, 4)
+    y1_rows, w2_part, w3 = lax.optimization_barrier(
+        (gathered_x(product(f0, b1_columns)), w2_part, w3)
     )
     w2_columns = (
-        coupling_columns[:, :, 64:192].reshape(8, 2, 64, COLS).swapaxes(0, 1).reshape(U2, COLS)
+        paired(w2_part, "c", 1).reshape(8, 2, 64, COLS).swapaxes(0, 1).reshape(U2, COLS)
     )
-    w3_columns = coupling_columns[:, :, 192:].reshape(U3, COLS)
-    w3_rows = gathered_x(w3)
-
-    v0_rows = inverse_rows[:128]
-    v1_rows = inverse_rows[128:256]
-    v2_rows = inverse_rows[256:384]
-    v3_rows = inverse_rows[384:]
-    f0 = chosen(v0_rows, mine_1, 4)
-    m1 = product(f0, w1_columns)
+    m1 = product(y1_rows, v1_columns)
     m1_rows = gathered_x(m1)
+    ancestor_rows = gathered_x(jnp.concatenate([v1, v2], 0))
+    v1_rows = ancestor_rows[:128]
+    v2_rows = ancestor_rows[128:]
     x1 = jnp.concatenate(
         [
             jnp.concatenate([v1_rows, jnp.zeros((128, U1), jnp.float32)], 1),
@@ -148,6 +147,19 @@
     f1 = chosen(x1, mine_2, 8)
     m2 = product(f1, w2_columns)
     m2_rows = gathered_x(m2)
+    w3_columns = group_rows(w3).reshape(U3, COLS)
+
+    d0 = inner_product(columns(v0_rows, front_3 * 128, 128), v0)
+    d1 = inner_product(columns(x1, slot_1 * 256, 256), jnp.concatenate([v1, -m1], 0))
+    e1 = -inner_product(columns(f0, slot_1 * 128, 128), m1)
+    e2 = -inner_product(columns(f1, pair * 512, 512), m2)
+    summed = group_sums(jnp.concatenate([split(d0), split(d1), split(e1), split(e2)], 2))
+
+    m2_rows, w3_columns, summed = lax.optimization_barrier((m2_rows, w3_columns, summed))
+    d0 = summed[:16]
+    d1 = summed[16:48]
+    e1 = summed[48:64]
+    e2 = summed[64:]
     x2 = jnp.concatenate(
         [
             jnp.concatenate([v2_rows, jnp.zeros((128, U2), jnp.float32)], 1),
@@ -157,24 +169,15 @@
     )
     f2 = chosen(x2, mine_3, 12)
     m3 = product(f2, w3_columns)
-
-    d0 = inner_product(columns(v0_rows, front_3 * 128, 128), v0)
-    d1 = inner_product(
-        columns(x1, slot_1 * 256, 256), jnp.concatenate([v1, -m1], 0)
-    )
-    e1 = -inner_product(columns(f0, slot_1 * 128, 128), m1)
+    own_rows, m3 = lax.optimization_barrier((jnp.concatenate([v3, w3], 0), m3))
+    own_rows = gathered_x(own_rows)
+    v3_rows = own_rows[:128]
+    w3_rows = own_rows[128:]
     d2 = inner_product(columns(x2, pair * 512, 512), jnp.concatenate([v2, -m2], 0))
-    e2 = -inner_product(columns(f1, pair * 512, 512), m2)
     e3 = -inner_product(f2, m3)
-    summed = group_sums(
-        jnp.concatenate([split(d0), split(d1), split(e1), split(d2), split(e2), split(e3)], 2)
-    )
-    d0 = summed[:16]
-    d1 = summed[16:48]
-    e1 = summed[48:64]
-    d2 = summed[64:128]
-    e2 = summed[128:192]
-    e3 = summed[192:]
+    summed = group_sums(jnp.concatenate([split(d2), split(e3)], 2))
+    d2 = summed[:64]
+    e3 = summed[64:]
     d3 = group_sums(split(inner_product(v3_rows, v3) - inner_product(w3_rows, e3)))
     return d0, d1, e1, d2, e2, d3, e3
 

time: 221 us -> 221 us (level)
  waiting for transfers between devices: 72.8 us -> 43.4 us
  starting transfers between devices: 54 us -> 83.3 us
  blocking collectives: 21.1 us -> 0 us
  local copies, waits for them, and re-layouts: 28.1 us -> 42.4 us
  matrix products: 10.4 us -> 15.7 us
    ppermute x20 -> x35, starting transfers between devices: 30.8 us -> 55.5 us  [swapped(): lax.ppermute(array, axis, [(i, i ^ distance) for i in range(lax.axis_size...]
    all_to_all x1 -> x0, blocking collectives: 21.1 us -> none  [gathered(): return lax.all_to_all(spread, axes, 0, 0)]
    dynamic_update_slice x15 -> x26, local copies, waits for them, and re-layouts: 6.56 us -> 20 us  [gathered_x(): out = lax.dynamic_update_slice(out, piece, (0, (me ^ distance) * COLS))]
    all_to_all x3 -> x4, waiting for transfers between devices: 18 us -> 5.8 us  [gathered(): return lax.all_to_all(spread, axes, 0, 0)]
    all_to_all x2 -> x3, waiting for transfers between devices: 16.5 us -> 6.41 us  [group_sums(): return jnp.sum(lax.all_to_all(half, 'y', 0, 0), 0)]
    ppermute x20 -> x35, waiting for transfers between devices: 38.2 us -> 31.2 us  [swapped(): lax.ppermute(array, axis, [(i, i ^ distance) for i in range(lax.axis_size...]
    all_to_all x2 -> x3, starting transfers between devices: 7.96 us -> 11.8 us  [group_sums(): return jnp.sum(lax.all_to_all(half, 'y', 0, 0), 0)]
    dot_general x6, matrix products: 3.52 us -> 7.18 us  [product(): jnp.dot(left, right, precision=PRECISION, preferred_element_type=jnp.floa...]
  transfers between devices with their start and end apart: 25 -> 42, of which waited for: 16 -> 13; matrix products, arithmetic and copies ran while one was open for 12% -> 28% of each run, Pallas kernels for 0% -> 0%
where the time goes in v2:
time: 221 us; the launch traced here: 219 us
  starting transfers between devices  83.3 us (38%)
  waiting for transfers between devices  43.4 us (20%)
  local copies, waits for them, and re-layouts  42.4 us (19%)
  between operations  17.2 us (8%)
  other arithmetic  17 us (8%)
  matrix products  15.7 us (7%)
    ppermute x35, starting transfers between devices, swapped(): lax.ppermute(array, axis, [(i, i ^ distance) for i in range(lax.axis_size...  55.5 us
    ppermute x35, waiting for transfers between devices, swapped(): lax.ppermute(array, axis, [(i, i ^ distance) for i in range(lax.axis_size...  31.2 us
    dynamic_update_slice x26, local copies, waits for them, and re-layouts, gathered_x(): out = lax.dynamic_update_slice(out, piece, (0, (me ^ distance) * COLS))  20 us
    all_to_all x4, starting transfers between devices, gathered(): return lax.all_to_all(spread, axes, 0, 0)  16 us
    all_to_all x3, starting transfers between devices, group_sums(): return jnp.sum(lax.all_to_all(half, 'y', 0, 0), 0)  11.8 us
    dot_general x8, matrix products, inner_product(): lax.dot_general(left, right, (((0,), (0,)), ((), ())), precision=PRECISIO...  8.48 us
    dot_general x6, matrix products, product(): jnp.dot(left, right, precision=PRECISION, preferred_element_type=jnp.floa...  7.18 us
    all_to_all x3, waiting for transfers between devices, group_sums(): return jnp.sum(lax.all_to_all(half, 'y', 0, 0), 0)  6.41 us
  transfers between devices with their start and end apart: 42, of which 13 were waited for; matrix products, arithmetic and copies ran while one was open for 28% of the time, Pallas kernels for 0%

profile of v2, /device:TPU:1, one launch (start us, length us, event | category | flops | bytes accessed | tf_op | source)
XLA Modules:
  0.0 219.0 jit_solution(4606568442113891622)
XLA Ops:
  0.7 2.1 collective-permute-start.18
  2.8 1.8 collective-permute-start.19
  12.5 4.2 %all-to-all-start = ((f32[4,128,256]{2,1,0:T(8,128)}), f32[4,128,256]{2,1,0:T(8,128)S(1)}, u32[]{:S(2)}, u32[]{:S(2)}) async-start(f32[4,128,256]{2,1,0:T(8,128)} %broadcast_in_dim.12), calls=%async_computation | async-start | bytes 1048576 | tf_op jit(solution)/shard_map/all_to_all | solution.py:35
  19.8 3.1 %collective-permute-start.1 = (f32[2,64,256]{2,1,0:T(8,128)S(1)}, f32[2,64,256]{2,1,0:T(8,128)S(1)}, u32[]{:S(2)}, u32[]{:S(2)}) collective-permute-start(f32[2,64,256]{2,1,0:T(8,128)S(1)} %maximum_select_fusion.6), channel_id=1, source_target_pairs={{0,64},{64,0},{1,65},{65,1},{2,66},{66,2},{3,67},{67,3},{4,68},{68... | collective-permute-start | bytes 393224 | tf_op jit(solution)/shard_map/ppermute | solution.py:30
  23.7 3.6 %collective-permute-start.10 = (f32[4,128,256]{2,1,0:T(8,128)S(1)}, f32[4,128,256]{2,1,0:T(8,128)S(1)}, u32[]{:S(2)}, u32[]{:S(2)}) collective-permute-start(f32[4,128,256]{2,1,0:T(8,128)S(1)} %all-to-all-done), channel_id=1, source_target_pairs={{0,4},{4,0},{1,5},{5,1},{2,6},{6,2},{3,7},{7,3},{8,12},{12,8},{9,1... | collective-permute-start | bytes 1572872 | tf_op jit(solution)/shard_map/ppermute | solution.py:30
  30.1 3.5 %all-to-all-start.1 = ((f32[4,320,256]{2,1,0:T(8,128)}), f32[4,320,256]{2,1,0:T(8,128)S(1)}, u32[]{:S(2)}, u32[]{:S(2)}) async-start(f32[4,320,256]{2,1,0:T(8,128)} %broadcast_in_dim.13), calls=%async_computation.1 | async-start | bytes 2621440 | tf_op jit(solution)/shard_map/all_to_all | solution.py:35
  42.8 1.8 collective-permute-start.16
  51.3 6.6 %collective-permute-start.6 = (f32[64,256]{1,0:T(8,128)}, f32[64,256]{1,0:T(8,128)S(1)}, u32[]{:S(2)}, u32[]{:S(2)}) collective-permute-start(f32[64,256]{1,0:T(8,128)} %bitcast.131), channel_id=1, source_target_pairs={{0,128},{128,0},{1,129},{129,1},{2,130},{130,2},{3,131},{131,3},{4... | collective-permute-start | bytes 196616 | tf_op jit(solution)/shard_map/ppermute | solution.py:30
  63.4 2.0 collective-permute-start.8
  67.5 5.7 %collective-permute-start.11 = (f32[4,320,256]{2,1,0:T(8,128)S(1)}, f32[4,320,256]{2,1,0:T(8,128)S(1)}, u32[]{:S(2)}, u32[]{:S(2)}) collective-permute-start(f32[4,320,256]{2,1,0:T(8,128)S(1)} %all-to-all-done.1), channel_id=1, source_target_pairs={{0,4},{4,0},{1,5},{5,1},{2,6},{6,2},{3,7},{7,3},{8,12},{12,8},{9,1... | collective-permute-start | bytes 3932168 | tf_op jit(solution)/shard_map/ppermute | solution.py:30
  74.8 1.9 collective-permute-start.4
  78.9 1.8 constant_dynamic-update-slice_fusion.25
  85.2 4.6 %collective-permute-done.4 = f32[256,256]{1,0:T(8,128)S(1)} collective-permute-done((f32[256,256]{1,0:T(8,128)}, f32[256,256]{1,0:T(8,128)S(1)}, u32[]{:S(2)}, u32[]{:S(2)}) %collective-permute-start.4) | collective-permute-done | bytes 262176 | tf_op jit(solution)/shard_map/ppermute | solution.py:30
  91.9 2.0 collective-permute-start.13
  96.3 4.5 %all-to-all-start.2 = ((f32[4,128,256]{2,1,0:T(8,128)}), f32[4,128,256]{2,1,0:T(8,128)}, u32[]{:S(2)}, u32[]{:S(2)}) async-start(f32[4,128,256]{2,1,0:T(8,128)} %broadcast_in_dim.14), calls=%async_computation.2 | async-start | bytes 1048576 | tf_op jit(solution)/shard_map/all_to_all | solution.py:35
  103.8 4.1 %collective-permute-done.14 = f32[128,256]{1,0:T(8,128)S(1)} collective-permute-done((f32[128,256]{1,0:T(8,128)S(1)}, f32[128,256]{1,0:T(8,128)S(1)}, u32[]{:S(2)}, u32[]{:S(2)}) %collective-permute-start.14) | collective-permute-done | bytes 131104 | tf_op jit(solution)/shard_map/ppermute | solution.py:30
  111.2 2.2 %collective-permute-start.23 = (f32[128,256]{1,0:T(8,128)}, f32[128,256]{1,0:T(8,128)S(1)}, u32[]{:S(2)}, u32[]{:S(2)}) collective-permute-start(f32[128,256]{1,0:T(8,128)} %get-tuple-element.75), channel_id=1, source_target_pairs={{0,2},{1,3},{2,0},{3,1},{4,6},{5,7},{6,4},{7,5},{8,10},{9,11},{10,... | collective-permute-start | bytes 393224 | tf_op jit(solution)/shard_map/ppermute | solution.py:30
  113.4 3.2 %collective-permute-start.24 = (f32[4,128,256]{2,1,0:T(8,128)}, f32[4,128,256]{2,1,0:T(8,128)}, u32[]{:S(2)}, u32[]{:S(2)}) collective-permute-start(f32[4,128,256]{2,1,0:T(8,128)} %all-to-all-done.2), channel_id=1, source_target_pairs={{0,4},{4,0},{1,5},{5,1},{2,6},{6,2},{3,7},{7,3},{8,12},{12,8},{9,1... | collective-permute-start | bytes 1572872 | tf_op jit(solution)/shard_map/ppermute | solution.py:30
  117.6 3.8 %all-to-all-start.3 = ((f32[4,192,256]{2,1,0:T(8,128)}), f32[4,192,256]{2,1,0:T(8,128)S(1)}, u32[]{:S(2)}, u32[]{:S(2)}) async-start(f32[4,192,256]{2,1,0:T(8,128)} %broadcast_in_dim.16), calls=%async_computation.3 | async-start | bytes 1572864 | tf_op jit(solution)/shard_map/all_to_all | solution.py:35
  129.5 4.0 %all-to-all-done.3 = f32[4,192,256]{2,1,0:T(8,128)S(1)} async-done(((f32[4,192,256]{2,1,0:T(8,128)}), f32[4,192,256]{2,1,0:T(8,128)S(1)}, u32[]{:S(2)}, u32[]{:S(2)}) %all-to-all-start.3) | async-done | bytes 786464 | tf_op jit(solution)/shard_map/all_to_all | solution.py:35
  148.1 1.9 bitcast_add_fusion.1
  150.0 4.1 %all-to-all-start.4 = ((f32[4,128,256]{2,1,0:T(8,128)}), f32[4,128,256]{2,1,0:T(8,128)}, u32[]{:S(2)}, u32[]{:S(2)}) async-start(f32[4,128,256]{2,1,0:T(8,128)} %bitcast_add_fusion.1), calls=%async_computation.4 | async-start | bytes 1048576 | tf_op jit(solution)/shard_map/all_to_all | solution.py:69
  155.9 4.6 %collective-permute-done.26 = f32[256,256]{1,0:T(8,128)} collective-permute-done((f32[256,256]{1,0:T(8,128)}, f32[256,256]{1,0:T(8,128)}, u32[]{:S(2)}, u32[]{:S(2)}) %collective-permute-start.26) | collective-permute-done | bytes 262176 | tf_op jit(solution)/shard_map/ppermute | solution.py:30
  163.9 2.1 maximum_select_fusion.1
  170.9 2.0 convolution_negate_fusion
  175.3 2.3 %collective-permute-done.30 = f32[4,256,256]{2,1,0:T(8,128)S(1)} collective-permute-done((f32[4,256,256]{2,1,0:T(8,128)S(1)}, f32[4,256,256]{2,1,0:T(8,128)S(1)}, u32[]{:S(2)}, u32[]{:S(2)}) %collective-permute-start.30) | collective-permute-done | bytes 1048608 | tf_op jit(solution)/shard_map/ppermute | solution.py:30
  178.7 3.6 %all-to-all-start.5 = ((f32[4,256,256]{2,1,0:T(8,128)}), f32[4,256,256]{2,1,0:T(8,128)S(1)}, u32[]{:S(2)}, u32[]{:S(2)}) async-start(f32[4,256,256]{2,1,0:T(8,128)} %fusion.4), calls=%async_computation.5 | async-start | bytes 2097152 | tf_op jit(solution)/shard_map/all_to_all | solution.py:69
  183.0 2.7 %collective-permute-start.33 = (f32[320,256]{1,0:T(8,128)S(1)}, f32[320,256]{1,0:T(8,128)S(1)}, u32[]{:S(2)}, u32[]{:S(2)}) collective-permute-start(f32[320,256]{1,0:T(8,128)S(1)} %copy-done.9), channel_id=1, source_target_pairs={{0,2},{1,3},{2,0},{3,1},{4,6},{5,7},{6,4},{7,5},{8,10},{9,11},{10,... | collective-permute-start | bytes 983048 | tf_op jit(solution)/shard_map/ppermute | solution.py:30
  185.9 5.5 %collective-permute-done.31 = f32[320,256]{1,0:T(8,128)S(1)} collective-permute-done((f32[320,256]{1,0:T(8,128)S(1)}, f32[320,256]{1,0:T(8,128)S(1)}, u32[]{:S(2)}, u32[]{:S(2)}) %collective-permute-start.31) | collective-permute-done | bytes 327712 | tf_op jit(solution)/shard_map/ppermute | solution.py:30
  191.4 8.3 %collective-permute-done.32 = f32[320,256]{1,0:T(8,128)S(1)} collective-permute-done((f32[320,256]{1,0:T(8,128)S(1)}, f32[320,256]{1,0:T(8,128)S(1)}, u32[]{:S(2)}, u32[]{:S(2)}) %collective-permute-start.32) | collective-permute-done | bytes 327712 | tf_op jit(solution)/shard_map/ppermute | solution.py:30
  205.4 4.0 %all-to-all-start.6 = ((f32[4,128,256]{2,1,0:T(8,128)}), f32[4,128,256]{2,1,0:T(8,128)S(1)}, u32[]{:S(2)}, u32[]{:S(2)}) async-start(f32[4,128,256]{2,1,0:T(8,128)} %bitcast_add_fusion), calls=%async_computation.6 | async-start | bytes 1048576 | tf_op jit(solution)/shard_map/all_to_all | solution.py:69
  211.9 6.4 %all-to-all-done.6 = f32[4,128,256]{2,1,0:T(8,128)S(1)} async-done(((f32[4,128,256]{2,1,0:T(8,128)}), f32[4,128,256]{2,1,0:T(8,128)S(1)}, u32[]{:S(2)}, u32[]{:S(2)}) %all-to-all-start.6) | async-done | bytes 524320 | tf_op jit(solution)/shard_map/all_to_all | solution.py:69
  (250 shorter events, 87.7 us)
Async XLA Ops:
  0.7 48.1 %collective-permute-start.18 = (f32[192,256]{1,0:T(8,128)}, f32[192,256]{1,0:T(8,128)}, u32[]{:S(2)}, u32[]{:S(2)}) collective-permute-start(f32[192,256]{1,0:T(8,128)} %param.18), channel_id=1, source_target_pairs={{0,1},{1,0},{2,3},{3,2},{4,5},{5,4},{6,7},{7,6},{8,9},{9,8},{10,11... | collective-permute-start | bytes 589832 | tf_op jit(solution)/shard_map/ppermute | solution.py:30
  2.8 48.5 %collective-permute-start.19 = (f32[192,256]{1,0:T(8,128)}, f32[192,256]{1,0:T(8,128)}, u32[]{:S(2)}, u32[]{:S(2)}) collective-permute-start(f32[192,256]{1,0:T(8,128)} %param.18), channel_id=1, source_target_pairs={{0,3},{1,2},{2,1},{3,0},{4,7},{5,6},{6,5},{7,4},{8,11},{9,10},{10,... | collective-permute-start | bytes 589832 | tf_op jit(solution)/shard_map/ppermute | solution.py:30
  4.6 54.9 %collective-permute-start.20 = (f32[192,256]{1,0:T(8,128)}, f32[192,256]{1,0:T(8,128)}, u32[]{:S(2)}, u32[]{:S(2)}) collective-permute-start(f32[192,256]{1,0:T(8,128)} %param.18), channel_id=1, source_target_pairs={{0,2},{1,3},{2,0},{3,1},{4,6},{5,7},{6,4},{7,5},{8,10},{9,11},{10,... | collective-permute-start | bytes 589832 | tf_op jit(solution)/shard_map/ppermute | solution.py:30
  7.4 12.3 %collective-permute-start = (f32[64,256]{1,0:T(8,128)S(1)}, f32[64,256]{1,0:T(8,128)S(1)}, u32[]{:S(2)}, u32[]{:S(2)}) collective-permute-start(f32[64,256]{1,0:T(8,128)S(1)} %constant_dynamic-update-slice_fusion), channel_id=1, source_target_pairs={{0,32},{32,0},{1,33},{33,1},{2,34},{34,2},{3,35},{35,3},{4,36},{36... | collective-permute-start | bytes 196616 | tf_op jit(solution)/shard_map/ppermute | solution.py:30
  10.8 12.1 %collective-permute-start.2 = (f32[128,256]{1,0:T(8,128)S(1)}, f32[128,256]{1,0:T(8,128)S(1)}, u32[]{:S(2)}, u32[]{:S(2)}) collective-permute-start(f32[128,256]{1,0:T(8,128)S(1)} %constant_dynamic-update-slice_fusion.3), channel_id=1, source_target_pairs={{0,32},{32,0},{1,33},{33,1},{2,34},{34,2},{3,35},{35,3},{4,36},{36... | collective-permute-start | bytes 393224 | tf_op jit(solution)/shard_map/ppermute | solution.py:30
  30.1 37.4 %all-to-all-start.1 = ((f32[4,320,256]{2,1,0:T(8,128)}), f32[4,320,256]{2,1,0:T(8,128)S(1)}, u32[]{:S(2)}, u32[]{:S(2)}) async-start(f32[4,320,256]{2,1,0:T(8,128)} %broadcast_in_dim.13), calls=%async_computation.1 | async-start | bytes 2621440 | tf_op jit(solution)/shard_map/all_to_all | solution.py:35
  42.0 21.4 %collective-permute-start.15 = (f32[128,256]{1,0:T(8,128)}, f32[128,256]{1,0:T(8,128)S(1)}, u32[]{:S(2)}, u32[]{:S(2)}) collective-permute-start(f32[128,256]{1,0:T(8,128)} %bitcast.24), channel_id=1, source_target_pairs={{0,1},{1,0},{2,3},{3,2},{4,5},{5,4},{6,7},{7,6},{8,9},{9,8},{10,11... | collective-permute-start | bytes 393224 | tf_op jit(solution)/shard_map/ppermute | solution.py:30
  42.8 23.4 %collective-permute-start.16 = (f32[128,256]{1,0:T(8,128)}, f32[128,256]{1,0:T(8,128)S(1)}, u32[]{:S(2)}, u32[]{:S(2)}) collective-permute-start(f32[128,256]{1,0:T(8,128)} %bitcast.24), channel_id=1, source_target_pairs={{0,3},{1,2},{2,1},{3,0},{4,7},{5,6},{6,5},{7,4},{8,11},{9,10},{10,... | collective-permute-start | bytes 393224 | tf_op jit(solution)/shard_map/ppermute | solution.py:30
  48.8 29.5 %collective-permute-start.17 = (f32[128,256]{1,0:T(8,128)}, f32[128,256]{1,0:T(8,128)}, u32[]{:S(2)}, u32[]{:S(2)}) collective-permute-start(f32[128,256]{1,0:T(8,128)} %bitcast.24), channel_id=1, source_target_pairs={{0,2},{1,3},{2,0},{3,1},{4,6},{5,7},{6,4},{7,5},{8,10},{9,11},{10,... | collective-permute-start | bytes 393224 | tf_op jit(solution)/shard_map/ppermute | solution.py:30
  59.5 24.7 %collective-permute-start.3 = (f32[256,256]{1,0:T(8,128)}, f32[256,256]{1,0:T(8,128)}, u32[]{:S(2)}, u32[]{:S(2)}) collective-permute-start(f32[256,256]{1,0:T(8,128)} %get-tuple-element.41), channel_id=1, source_target_pairs={{0,1},{1,0},{2,3},{3,2},{4,5},{5,4},{6,7},{7,6},{8,9},{9,8},{10,11... | collective-permute-start | bytes 786440 | tf_op jit(solution)/shard_map/ppermute | solution.py:30
  63.4 11.4 %collective-permute-start.8 = (f32[128,256]{1,0:T(8,128)}, f32[128,256]{1,0:T(8,128)}, u32[]{:S(2)}, u32[]{:S(2)}) collective-permute-start(f32[128,256]{1,0:T(8,128)} %get-tuple-element.47), channel_id=1, source_target_pairs={{0,3},{1,2},{2,1},{3,0},{4,7},{5,6},{6,5},{7,4},{8,11},{9,10},{10,... | collective-permute-start | bytes 393224 | tf_op jit(solution)/shard_map/ppermute | solution.py:30
  66.1 12.8 %collective-permute-start.9 = (f32[128,256]{1,0:T(8,128)}, f32[128,256]{1,0:T(8,128)}, u32[]{:S(2)}, u32[]{:S(2)}) collective-permute-start(f32[128,256]{1,0:T(8,128)} %get-tuple-element.47), channel_id=1, source_target_pairs={{0,2},{1,3},{2,0},{3,1},{4,6},{5,7},{6,4},{7,5},{8,10},{9,11},{10,... | collective-permute-start | bytes 393224 | tf_op jit(solution)/shard_map/ppermute | solution.py:30
  67.5 23.4 %collective-permute-start.11 = (f32[4,320,256]{2,1,0:T(8,128)S(1)}, f32[4,320,256]{2,1,0:T(8,128)S(1)}, u32[]{:S(2)}, u32[]{:S(2)}) collective-permute-start(f32[4,320,256]{2,1,0:T(8,128)S(1)} %all-to-all-done.1), channel_id=1, source_target_pairs={{0,4},{4,0},{1,5},{5,1},{2,6},{6,2},{3,7},{7,3},{8,12},{12,8},{9,1... | collective-permute-start | bytes 3932168 | tf_op jit(solution)/shard_map/ppermute | solution.py:30
  74.8 15.0 %collective-permute-start.4 = (f32[256,256]{1,0:T(8,128)}, f32[256,256]{1,0:T(8,128)S(1)}, u32[]{:S(2)}, u32[]{:S(2)}) collective-permute-start(f32[256,256]{1,0:T(8,128)} %get-tuple-element.41), channel_id=1, source_target_pairs={{0,3},{1,2},{2,1},{3,0},{4,7},{5,6},{6,5},{7,4},{8,11},{9,10},{10,... | collective-permute-start | bytes 786440 | tf_op jit(solution)/shard_map/ppermute | solution.py:30
  78.3 11.5 %collective-permute-start.5 = (f32[256,256]{1,0:T(8,128)}, f32[256,256]{1,0:T(8,128)S(1)}, u32[]{:S(2)}, u32[]{:S(2)}) collective-permute-start(f32[256,256]{1,0:T(8,128)} %get-tuple-element.41), channel_id=1, source_target_pairs={{0,2},{1,3},{2,0},{3,1},{4,6},{5,7},{6,4},{7,5},{8,10},{9,11},{10,... | collective-permute-start | bytes 786440 | tf_op jit(solution)/shard_map/ppermute | solution.py:30
  91.8 12.0 %collective-permute-start.12 = (f32[128,256]{1,0:T(8,128)S(1)}, f32[128,256]{1,0:T(8,128)S(1)}, u32[]{:S(2)}, u32[]{:S(2)}) collective-permute-start(f32[128,256]{1,0:T(8,128)S(1)} %get-tuple-element.74), channel_id=1, source_target_pairs={{0,1},{1,0},{2,3},{3,2},{4,5},{5,4},{6,7},{7,6},{8,9},{9,8},{10,11... | collective-permute-start | bytes 393224 | tf_op jit(solution)/shard_map/ppermute | solution.py:30
  91.9 11.9 %collective-permute-start.13 = (f32[128,256]{1,0:T(8,128)S(1)}, f32[128,256]{1,0:T(8,128)S(1)}, u32[]{:S(2)}, u32[]{:S(2)}) collective-permute-start(f32[128,256]{1,0:T(8,128)S(1)} %get-tuple-element.74), channel_id=1, source_target_pairs={{0,3},{1,2},{2,1},{3,0},{4,7},{5,6},{6,5},{7,4},{8,11},{9,10},{10,... | collective-permute-start | bytes 393224 | tf_op jit(solution)/shard_map/ppermute | solution.py:30
  96.3 12.7 %all-to-all-start.2 = ((f32[4,128,256]{2,1,0:T(8,128)}), f32[4,128,256]{2,1,0:T(8,128)}, u32[]{:S(2)}, u32[]{:S(2)}) async-start(f32[4,128,256]{2,1,0:T(8,128)} %broadcast_in_dim.14), calls=%async_computation.2 | async-start | bytes 1048576 | tf_op jit(solution)/shard_map/all_to_all | solution.py:35
  110.2 12.4 %collective-permute-start.21 = (f32[128,256]{1,0:T(8,128)}, f32[128,256]{1,0:T(8,128)S(1)}, u32[]{:S(2)}, u32[]{:S(2)}) collective-permute-start(f32[128,256]{1,0:T(8,128)} %get-tuple-element.75), channel_id=1, source_target_pairs={{0,1},{1,0},{2,3},{3,2},{4,5},{5,4},{6,7},{7,6},{8,9},{9,8},{10,11... | collective-permute-start | bytes 393224 | tf_op jit(solution)/shard_map/ppermute | solution.py:30
  110.5 12.2 %collective-permute-start.22 = (f32[128,256]{1,0:T(8,128)}, f32[128,256]{1,0:T(8,128)S(1)}, u32[]{:S(2)}, u32[]{:S(2)}) collective-permute-start(f32[128,256]{1,0:T(8,128)} %get-tuple-element.75), channel_id=1, source_target_pairs={{0,3},{1,2},{2,1},{3,0},{4,7},{5,6},{6,5},{7,4},{8,11},{9,10},{10,... | collective-permute-start | bytes 393224 | tf_op jit(solution)/shard_map/ppermute | solution.py:30
  111.2 11.5 %collective-permute-start.23 = (f32[128,256]{1,0:T(8,128)}, f32[128,256]{1,0:T(8,128)S(1)}, u32[]{:S(2)}, u32[]{:S(2)}) collective-permute-start(f32[128,256]{1,0:T(8,128)} %get-tuple-element.75), channel_id=1, source_target_pairs={{0,2},{1,3},{2,0},{3,1},{4,6},{5,7},{6,4},{7,5},{8,10},{9,11},{10,... | collective-permute-start | bytes 393224 | tf_op jit(solution)/shard_map/ppermute | solution.py:30
  117.6 15.9 %all-to-all-start.3 = ((f32[4,192,256]{2,1,0:T(8,128)}), f32[4,192,256]{2,1,0:T(8,128)S(1)}, u32[]{:S(2)}, u32[]{:S(2)}) async-start(f32[4,192,256]{2,1,0:T(8,128)} %broadcast_in_dim.16), calls=%async_computation.3 | async-start | bytes 1572864 | tf_op jit(solution)/shard_map/all_to_all | solution.py:35
  129.2 18.9 %collective-permute-start.29 = (f32[4,128,256]{2,1,0:T(8,128)}, f32[4,128,256]{2,1,0:T(8,128)}, u32[]{:S(2)}, u32[]{:S(2)}) collective-permute-start(f32[4,128,256]{2,1,0:T(8,128)} %dynamic-slice_bitcast_fusion.1), channel_id=1, source_target_pairs={{0,4},{4,0},{1,5},{5,1},{2,6},{6,2},{3,7},{7,3},{8,12},{12,8},{9,1... | collective-permute-start | bytes 1572872 | tf_op jit(solution)/shard_map/ppermute | solution.py:30
  133.5 30.4 %collective-permute-start.28 = (f32[4,192,256]{2,1,0:T(8,128)S(1)}, f32[4,192,256]{2,1,0:T(8,128)}, u32[]{:S(2)}, u32[]{:S(2)}) collective-permute-start(f32[4,192,256]{2,1,0:T(8,128)S(1)} %all-to-all-done.3), channel_id=1, source_target_pairs={{0,4},{4,0},{1,5},{5,1},{2,6},{6,2},{3,7},{7,3},{8,12},{12,8},{9,1... | collective-permute-start | bytes 2359304 | tf_op jit(solution)/shard_map/ppermute | solution.py:30
  143.0 11.2 %collective-permute-start.25 = (f32[256,256]{1,0:T(8,128)}, f32[256,256]{1,0:T(8,128)}, u32[]{:S(2)}, u32[]{:S(2)}) collective-permute-start(f32[256,256]{1,0:T(8,128)} %copy-done.12), channel_id=1, source_target_pairs={{0,1},{1,0},{2,3},{3,2},{4,5},{5,4},{6,7},{7,6},{8,9},{9,8},{10,11... | collective-permute-start | bytes 786440 | tf_op jit(solution)/shard_map/ppermute | solution.py:30
  145.9 14.6 %collective-permute-start.26 = (f32[256,256]{1,0:T(8,128)}, f32[256,256]{1,0:T(8,128)}, u32[]{:S(2)}, u32[]{:S(2)}) collective-permute-start(f32[256,256]{1,0:T(8,128)} %copy-done.12), channel_id=1, source_target_pairs={{0,3},{1,2},{2,1},{3,0},{4,7},{5,6},{6,5},{7,4},{8,11},{9,10},{10,... | collective-permute-start | bytes 786440 | tf_op jit(solution)/shard_map/ppermute | solution.py:30
  146.4 15.8 %collective-permute-start.27 = (f32[256,256]{1,0:T(8,128)}, f32[256,256]{1,0:T(8,128)}, u32[]{:S(2)}, u32[]{:S(2)}) collective-permute-start(f32[256,256]{1,0:T(8,128)} %copy-done.12), channel_id=1, source_target_pairs={{0,2},{1,3},{2,0},{3,1},{4,6},{5,7},{6,4},{7,5},{8,10},{9,11},{10,... | collective-permute-start | bytes 786440 | tf_op jit(solution)/shard_map/ppermute | solution.py:30
  150.0 16.0 %all-to-all-start.4 = ((f32[4,128,256]{2,1,0:T(8,128)}), f32[4,128,256]{2,1,0:T(8,128)}, u32[]{:S(2)}, u32[]{:S(2)}) async-start(f32[4,128,256]{2,1,0:T(8,128)} %bitcast_add_fusion.1), calls=%async_computation.4 | async-start | bytes 1048576 | tf_op jit(solution)/shard_map/all_to_all | solution.py:69
  178.7 21.1 %all-to-all-start.5 = ((f32[4,256,256]{2,1,0:T(8,128)}), f32[4,256,256]{2,1,0:T(8,128)S(1)}, u32[]{:S(2)}, u32[]{:S(2)}) async-start(f32[4,256,256]{2,1,0:T(8,128)} %fusion.4), calls=%async_computation.5 | async-start | bytes 2097152 | tf_op jit(solution)/shard_map/all_to_all | solution.py:69
  182.4 17.2 %collective-permute-start.32 = (f32[320,256]{1,0:T(8,128)S(1)}, f32[320,256]{1,0:T(8,128)S(1)}, u32[]{:S(2)}, u32[]{:S(2)}) collective-permute-start(f32[320,256]{1,0:T(8,128)S(1)} %copy-done.9), channel_id=1, source_target_pairs={{0,3},{1,2},{2,1},{3,0},{4,7},{5,6},{6,5},{7,4},{8,11},{9,10},{10,... | collective-permute-start | bytes 983048 | tf_op jit(solution)/shard_map/ppermute | solution.py:30
  183.0 16.7 %collective-permute-start.33 = (f32[320,256]{1,0:T(8,128)S(1)}, f32[320,256]{1,0:T(8,128)S(1)}, u32[]{:S(2)}, u32[]{:S(2)}) collective-permute-start(f32[320,256]{1,0:T(8,128)S(1)} %copy-done.9), channel_id=1, source_target_pairs={{0,2},{1,3},{2,0},{3,1},{4,6},{5,7},{6,4},{7,5},{8,10},{9,11},{10,... | collective-permute-start | bytes 983048 | tf_op jit(solution)/shard_map/ppermute | solution.py:30
  205.4 12.9 %all-to-all-start.6 = ((f32[4,128,256]{2,1,0:T(8,128)}), f32[4,128,256]{2,1,0:T(8,128)S(1)}, u32[]{:S(2)}, u32[]{:S(2)}) async-start(f32[4,128,256]{2,1,0:T(8,128)} %bitcast_add_fusion), calls=%async_computation.6 | async-start | bytes 1048576 | tf_op jit(solution)/shard_map/all_to_all | solution.py:69
  (40 other events, 424.4 us)

commit v3 on v1

v3 whole, which is shorter than its diff:
```python
import jax
import jax.numpy as jnp
from jax import lax
from jax.experimental import pallas as pl
from jax.experimental.pallas import tpu as pltpu
from jax.sharding import Mesh, PartitionSpec as P

S = 1024
BLOCK = 128
U1 = 512
U2 = 1024
U3 = 1536
COLS = 256
F32 = jnp.float32

CORE, PART, SLOT, PAIR, FRONT, SEL1, SEL2, SEL3 = 0, 1, 2, 3, 4, 8, 12, 20


def halves(values):
    high = values.astype(jnp.bfloat16)
    return high, (values - high.astype(F32)).astype(jnp.bfloat16)


def dot(left, right, contract=((1,), (0,))):
    left_high, left_low = halves(left)
    right_high, right_low = halves(right)

    def one(a, b):
        return lax.dot_general(a, b, (contract, ((), ())), preferred_element_type=F32)

    return one(left_high, right_high) + (one(left_high, right_low) + one(left_low, right_high))


def inner(left, right):
    return dot(left, right, ((0,), (0,)))


def times(number, unit):
    return pl.multiple_of(number * unit, unit)


def ordered(core, own, other):
    return [jnp.where(core == 0, own, other), jnp.where(core == 0, other, own)]


def call(body, micros, outs, scratch, *operands):
    spec = pl.BlockSpec(memory_space=pltpu.VMEM)
    return pl.pallas_call(
        body,
        out_shape=[jax.ShapeDtypeStruct(shape, F32) for shape in outs],
        in_specs=[pl.BlockSpec(memory_space=pltpu.SMEM)] + [spec] * (len(operands) - 1),
        out_specs=[spec] * len(outs),
        scratch_shapes=[pltpu.VMEM(shape, F32) for shape in scratch],
        cost_estimate=pl.CostEstimate(
            flops=micros * 1_100_000_000, bytes_accessed=0, transcendentals=0
        ),
        compiler_params=pltpu.CompilerParams(vmem_limit_bytes=24 * 1024 * 1024),
    )(*operands)


def place_ancestors(ids, own_1, pair_1, quad_1, own_2, pair_2, early, row_2, row_1, row_0):
    slot, pair = ids[SLOT], ids[PAIR]
    level_1 = [own_1[...], pair_1[...], quad_1[0:64, :], quad_1[64:128, :]]
    for distance in range(4):
        source = slot ^ distance
        values = level_1[distance]
        row_1[pl.ds(times(source, 32), 32), :] = values[0:32]
        row_0[pl.ds(times(source, 16), 16), :] = values[48:64]
        for copy in range(4):
            early[copy, pl.ds(times(source, 32), 32), :] = values[0:32]
            early[copy, pl.ds(256 + times(source, 16), 16), :] = values[32:48]
    for distance, ref in enumerate((own_2, pair_2)):
        start = times(pair ^ distance, 64)
        values = ref[...]
        row_2[pl.ds(start, 64), :] = values[64:128]
        row_2[pl.ds(128 + start, 64), :] = values[0:64]
        for copy in range(4):
            early[copy, pl.ds(128 + start, 64), :] = values[0:64]


def couple(ids, a0, a1, a2, a3, b0, b1, b2, b3, own_3, other_3, own, other, out):
    core, part = ids[CORE], ids[PART]
    w2 = jnp.zeros((128, COLS), F32)
    w3 = jnp.zeros((192, COLS), F32)
    for distance, (left_3, left_2) in enumerate(zip((a0, a1, a2, a3), (b0, b1, b2, b3))):
        quarter = part ^ distance
        w3 += dot(
            left_3[0:192, :], jnp.concatenate(ordered(core, own_3[quarter], other_3[quarter]), 0)
        )
        rows = []
        for step in range(2):
            y = (quarter & 1) * 2 + step
            start = 128 + times(quarter >> 1, 64)
            rows += ordered(core, own[y, pl.ds(start, 64), :], other[y, pl.ds(start, 64), :])
        w2 += dot(left_2[0:128, :], jnp.concatenate(rows, 0))
    for copy in range(4):
        out[copy, 0:128, :] = w2
        out[copy, 128:320, :] = w3


def first_half(ids, c0, c1, c2, c3, own, other, f0, y1, rows_0):
    core, part = ids[CORE], ids[PART]
    for distance, ref in enumerate((c0, c1, c2, c3)):
        rows_0[:, pl.ds(times(part ^ distance, COLS), COLS)] = ref[128:256, :]
    for block in range(4):
        f0[:, block * BLOCK : (block + 1) * BLOCK] = rows_0[
            :, pl.ds(times(ids[SEL1 + block], BLOCK), BLOCK)
        ]
    rows = []
    for slot in range(4):
        start = 256 + slot * 16
        for y in range(4):
            rows += ordered(core, own[y, start : start + 16, :], other[y, start : start + 16, :])
    y1[...] = dot(f0[...], jnp.concatenate(rows, 0))


def second_half(ids, y0, y1, y2, y3, own, other, m1):
    core, part = ids[CORE], ids[PART]
    total = jnp.zeros((128, COLS), F32)
    for distance, ref in enumerate((y0, y1, y2, y3)):
        start = times(part ^ distance, 32)
        rows = []
        for y in range(4):
            rows += ordered(core, own[y, pl.ds(start, 32), :], other[y, pl.ds(start, 32), :])
        total += dot(ref[...], jnp.concatenate(rows, 0))
    m1[...] = total


def level_two(ids, c0, c1, c2, c3, m0, m1, m2, m3, f0, own, other, x1, f1, out):
    core, part = ids[CORE], ids[PART]
    x1[0:128, S:] = jnp.zeros((128, U1), F32)
    x1[128:256, S:] = f0[...]
    for distance, (v_ref, m_ref) in enumerate(zip((c0, c1, c2, c3), (m0, m1, m2, m3))):
        place = pl.ds(times(part ^ distance, COLS), COLS)
        x1[0:128, place] = v_ref[0:128, :]
        x1[128:256, place] = -m_ref[...]
    for block in range(8):
        f1[:, block * BLOCK : (block + 1) * BLOCK] = x1[
            :, pl.ds(times(ids[SEL2 + block], BLOCK), BLOCK)
        ]
    total = jnp.zeros((256, COLS), F32)
    for pair in range(2):
        rows = []
        for y in range(4):
            start = pair * 64
            rows += ordered(core, own[y, start : start + 64, :], other[y, start : start + 64, :])
        total += dot(f1[:, pair * 512 : (pair + 1) * 512], jnp.concatenate(rows, 0))
    out[...] = total


def put(core, keep, send, values, start, rows):
    for y in range(4):
        first = values[2 * y * rows : (2 * y + 1) * rows]
        second = values[(2 * y + 1) * rows : (2 * y + 2) * rows]
        keep[y, start : start + rows, :] = jnp.where(core == 0, first, second)
        send[y, start : start + rows, :] = jnp.where(core == 0, second, first)


def early_sums(ids, c0, c1, c2, c3, f0, m1, x1, f1, m2, keep, send, piece):
    core, part = ids[CORE], ids[PART]
    front, slot, pair = ids[FRONT], ids[SLOT], ids[PAIR]
    for distance, ref in enumerate((c0, c1, c2, c3)):

        @pl.when((part ^ distance) == front >> 1)
        def _():
            piece[...] = ref[128:256, pl.ds(times(front & 1, BLOCK), BLOCK)]

    v = c0[...]
    put(core, keep, send, inner(piece[...], v[128:256]), 0, 16)
    m = m1[...]
    d1 = inner(x1[:, pl.ds(times(slot, 256), 256)], jnp.concatenate([v[0:128], -m], 0))
    put(core, keep, send, d1, 16, 32)
    put(core, keep, send, inner(f0[:, pl.ds(times(slot, 128), 128)], -m), 48, 16)
    put(core, keep, send, inner(f1[:, pl.ds(times(pair, 512), 512)], -m2[...]), 64, 64)


def level_three(ids, b0, b1, b2, b3, m0, m1, m2, m3, f1, own, other, keep_1, send_1, keep, send, x2, f2):
    core, part, pair = ids[CORE], ids[PART], ids[PAIR]
    x2[0:128, S:] = jnp.zeros((128, U2), F32)
    x2[128:384, S:] = f1[...]
    for distance, (v_ref, m_ref) in enumerate(zip((b0, b1, b2, b3), (m0, m1, m2, m3))):
        place = pl.ds(times(part ^ distance, COLS), COLS)
        x2[0:128, place] = v_ref[128:256, :]
        x2[128:384, place] = -m_ref[...]
    for block in range(12):
        f2[:, block * BLOCK : (block + 1) * BLOCK] = x2[
            :, pl.ds(times(ids[SEL3 + block], BLOCK), BLOCK)
        ]
    total = jnp.zeros((384, COLS), F32)
    for y in range(4):
        rows = jnp.concatenate(ordered(core, own[y, 128:320, :], other[y, 128:320, :]), 0)
        total += dot(f2[:, y * 384 : (y + 1) * 384], rows)
    for y in range(4):
        keep[y, 0:128, :] = keep_1[y]
        send[y, 0:128, :] = send_1[y]
    put(core, keep, send, inner(f2[...], -total), 192, 192)
    mine = jnp.concatenate([b0[128:256, :], -m0[...]], 0)
    put(core, keep, send, inner(x2[:, pl.ds(times(pair, 512), 512)], mine), 128, 64)


def last_level(ids, parts, a0, a1, a2, a3, w0, w1, w2, w3, early, d2, e3, keep, send):
    core, part = ids[CORE], ids[PART]
    total = (parts[0] + parts[1]) + (parts[2] + parts[3])
    early[...] = total[0:128]
    d2[...] = total[128:192]
    below = total[192:384]
    e3[...] = below
    right = jnp.concatenate([a0[192:320, :], -below], 0)
    for distance, (v_ref, w_ref) in enumerate(zip((a0, a1, a2, a3), (w0, w1, w2, w3))):
        rows = inner(jnp.concatenate([v_ref[192:320, :], w_ref[...]], 0), right)
        place = part ^ distance
        keep[place] = jnp.where(core == 0, rows[0:128], rows[128:256])
        send[place] = jnp.where(core == 0, rows[128:256], rows[0:128])


def swapped(array, axis, distance):
    return lax.ppermute(array, axis, [(i, i ^ distance) for i in range(lax.axis_size(axis))])


def around(values):
    return [values] + [swapped(values, "x", distance) for distance in (1, 2, 3)]


def exchanged(values):
    return lax.all_to_all(values, "y", 0, 0)


def spread(values):
    return jnp.broadcast_to(values[None], (4,) + values.shape)


def shards(v0, v1, b1, selector_1, v2, b2, selector_2, v3, b3, selector_3):
    half = lax.axis_index("h")
    quarter = lax.axis_index("q")
    pair = lax.axis_index("p")
    front_2 = half * 2 + quarter
    front_3 = front_2 * 2 + pair
    slot = quarter * 2 + pair
    places = jnp.stack(
        [lax.axis_index("c"), lax.axis_index("x"), slot, pair, front_3] + [jnp.int32(0)] * 3
    ).astype(jnp.int32)
    ids = jnp.concatenate(
        [
            places,
            lax.dynamic_index_in_dim(selector_1, half, 0, keepdims=False),
            lax.dynamic_index_in_dim(selector_2, front_2, 0, keepdims=False),
            lax.dynamic_index_in_dim(selector_3, front_3, 0, keepdims=False),
        ]
    )

    own_rows = around(jnp.concatenate([b3, v3], 0))
    own_1 = jnp.concatenate([v1, b1, v0], 0)
    pair_1 = swapped(own_1, "p", 1)
    own_2 = jnp.concatenate([v2, b2], 0)
    pair_2 = swapped(own_2, "p", 1)
    quad_1 = swapped(jnp.concatenate([own_1, pair_1], 0), "q", 1)
    columns_3 = exchanged(spread(v3))
    early, row_2, row_1, row_0 = call(
        place_ancestors,
        2,
        [(4, 320, COLS), (256, COLS), (128, COLS), (64, COLS)],
        [],
        ids, own_1, pair_1, quad_1, own_2, pair_2,
    )
    early, columns_3, own_rows = lax.optimization_barrier((early, columns_3, own_rows))
    other_3 = swapped(columns_3, "c", 1)
    early = exchanged(early)
    rows_2 = around(row_2)
    rows_10 = around(jnp.concatenate([row_1, row_0, swapped(row_0, "h", 1)], 0))
    early, rows_2, rows_10 = lax.optimization_barrier((early, rows_2, rows_10))
    early_other = swapped(early, "c", 1)

    (coupling,) = call(
        couple, 4, [(4, 320, COLS)], [], ids, *own_rows, *rows_2, columns_3, other_3, early, early_other
    )
    f0, y1 = call(
        first_half, 2, [(128, U1), (128, COLS)], [(128, S)], ids, *rows_10, early, early_other
    )
    w3 = coupling[0, 128:320]
    coupling = exchanged(coupling)
    y1 = around(y1)
    (m1,) = call(second_half, 2, [(128, COLS)], [], ids, *y1, early, early_other)
    m1, coupling = lax.optimization_barrier((around(m1), coupling))
    coupling_other = swapped(coupling, "c", 1)
    x1, f1, m2 = call(
        level_two,
        3,
        [(256, S + U1), (256, U2), (256, COLS)],
        [],
        ids, *rows_10, *m1, f0, coupling, coupling_other,
    )
    keep, send = call(
        early_sums,
        3,
        [(4, 128, COLS), (4, 128, COLS)],
        [(128, BLOCK)],
        ids, *rows_10, f0, m1[0], x1, f1, m2,
    )
    m2 = around(m2)
    keep, send = call(
        level_three,
        6,
        [(4, 384, COLS), (4, 384, COLS)],
        [(384, S + U2), (384, U3)],
        ids, *rows_2, *m2, f1, coupling, coupling_other, keep, send,
    )
    w3, keep, send = lax.optimization_barrier((w3, keep, send))
    w3 = around(w3)
    summed, d2, e3, keep, send = call(
        last_level,
        3,
        [(128, COLS), (64, COLS), (192, COLS), (4, 128, COLS), (4, 128, COLS)],
        [],
        ids, exchanged(keep + swapped(send, "c", 1)), *own_rows, *w3,
    )
    d3 = jnp.sum(exchanged(keep + swapped(send, "c", 1)), 0)
    return summed[:16], summed[16:48], summed[48:64], d2, summed[64:], d3, e3


def solution(mesh):
    devices = mesh.devices.reshape(2, 2, 2, 4, 2, 4)
    fine = Mesh(devices, ("h", "q", "p", "y", "c", "x"))
    tiled = P(("h", "q", "p", "y", "c"), "x")
    return jax.shard_map(
        shards,
        mesh=fine,
        in_specs=(tiled, tiled, tiled, P(), tiled, tiled, P(), tiled, tiled, P()),
        out_specs=(tiled,) * 7,
        check_vma=False,
    )
```

time: 221 us -> 188 us (0.85)
  blocking collectives: 21.1 us -> 0 us
  Pallas kernels: 0 us -> 18.2 us
  between operations: 16.9 us -> 0.92 us
  starting transfers between devices: 54 us -> 68.7 us
  other arithmetic: 16.3 us -> 2.94 us
  waiting for transfers between devices: 72.8 us -> 61.8 us
  matrix products: 10.4 us -> 0 us
  local copies, waits for them, and re-layouts: 28.1 us -> 34.1 us
    all_to_all x1 -> x0, blocking collectives: 21.1 us -> none  [gathered(): return lax.all_to_all(spread, axes, 0, 0)]
    unnamed x63 -> x80, local copies, waits for them, and re-layouts: 5.58 us -> 26.3 us
    all_to_all x5, waiting for transfers between devices: 34.6 us -> 15.2 us  [exchanged(): return lax.all_to_all(values, 'y', 0, 0)]
    pallas_call x0 -> x8, Pallas kernels: none -> 18.2 us  [call(): pl.pallas_call(body, out_shape=[jax.ShapeDtypeStruct(shape, F32) for shap...]
    ppermute x20 -> x30, starting transfers between devices: 30.8 us -> 47.8 us  [swapped(): lax.ppermute(array, axis, [(i, i ^ distance) for i in range(lax.axis_size...]
    dot_general x14 -> x0, matrix products: 10.4 us -> none  [the longest x8 6.88 us: inner_product(): lax.dot_general(left, right, (((0,), (0,)), ((), ())), precision=PRECISIO...]
    ppermute x20 -> x30, waiting for transfers between devices: 38.2 us -> 46.6 us  [swapped(): lax.ppermute(array, axis, [(i, i ^ distance) for i in range(lax.axis_size...]
    dynamic_update_slice x15 -> x0, local copies, waits for them, and re-layouts: 6.56 us -> none  [gathered_x(): out = lax.dynamic_update_slice(out, piece, (0, (me ^ distance) * COLS))]
  transfers between devices with their start and end apart: 25 -> 35, of which waited for: 16 -> 19; matrix products, arithmetic and copies ran while one was open for 12% -> 5% of each run, Pallas kernels for 0% -> 3%
where the time goes in v3:
time: 188 us; the launch traced here: 187 us
  starting transfers between devices  68.7 us (37%)
  waiting for transfers between devices  61.8 us (33%)
  local copies, waits for them, and re-layouts  34.1 us (18%)
  Pallas kernels  18.2 us (10%)
  other arithmetic  2.94 us (2%)
    ppermute x30, starting transfers between devices, swapped(): lax.ppermute(array, axis, [(i, i ^ distance) for i in range(lax.axis_size...  47.8 us
    ppermute x30, waiting for transfers between devices, swapped(): lax.ppermute(array, axis, [(i, i ^ distance) for i in range(lax.axis_size...  46.6 us
    unnamed x80, local copies, waits for them, and re-layouts  26.3 us
    all_to_all x5, starting transfers between devices, exchanged(): return lax.all_to_all(values, 'y', 0, 0)  20.9 us
    pallas_call x8, Pallas kernels, call(): pl.pallas_call(body, out_shape=[jax.ShapeDtypeStruct(shape, F32) for shap...  18.2 us
    all_to_all x5, waiting for transfers between devices, exchanged(): return lax.all_to_all(values, 'y', 0, 0)  15.2 us
  transfers between devices with their start and end apart: 35, of which 19 were waited for; matrix products, arithmetic and copies ran while one was open for 5% of the time, Pallas kernels for 3%

profile of v3, /device:TPU:1, one launch (start us, length us, event | category | flops | bytes accessed | tf_op | source)
XLA Modules:
  0.0 186.7 jit_solution(888546331574724708)
XLA Ops:
  2.6 3.4 %collective-permute-start.5 = (f32[320,256]{1,0:T(8,128)S(1)}, f32[320,256]{1,0:T(8,128)S(1)}, u32[]{:S(2)}, u32[]{:S(2)}) collective-permute-start(f32[320,256]{1,0:T(8,128)S(1)} %constant_dynamic-update-slice_fusion.5.a0), channel_id=1, source_target_pairs={{0,3},{1,2},{2,1},{3,0},{4,7},{5,6},{6,5},{7,4},{8,11},{9,10},{10,... | collective-permute-start | bytes 983048 | tf_op jit(solution)/shard_map/ppermute | solution.py:217
  8.9 1.7 collective-permute-start
  12.3 1.7 broadcast_in_dim.2
  14.0 4.2 %all-to-all-start = ((f32[4,128,256]{2,1,0:T(8,128)}), f32[4,128,256]{2,1,0:T(8,128)S(1)}, u32[]{:S(2)}, u32[]{:S(2)}) async-start(f32[4,128,256]{2,1,0:T(8,128)} %broadcast_in_dim.2), calls=%async_computation | async-start | bytes 1048576 | tf_op jit(solution)/shard_map/all_to_all | solution.py:225
  18.3 3.1 %collective-permute-start.1 = (f32[128,256]{1,0:T(8,128)S(1)}, f32[128,256]{1,0:T(8,128)S(1)}, u32[]{:S(2)}, u32[]{:S(2)}) collective-permute-start(f32[128,256]{1,0:T(8,128)S(1)} %pad_maximum_fusion), channel_id=1, source_target_pairs={{0,64},{64,0},{1,65},{65,1},{2,66},{66,2},{3,67},{67,3},{4,68},{68... | collective-permute-start | bytes 393224 | tf_op jit(solution)/shard_map/ppermute | solution.py:217
  22.2 3.0 %collective-permute-done.1.quad_1 = f32[128,256]{1,0:T(8,128)S(1)} collective-permute-done((f32[128,256]{1,0:T(8,128)S(1)}, f32[128,256]{1,0:T(8,128)S(1)}, u32[]{:S(2)}, u32[]{:S(2)}) %collective-permute-start.1) | collective-permute-done | bytes 131104 | tf_op jit(solution)/shard_map/ppermute | solution.py:217
  25.1 1.8 shard_map.153
  27.8 4.5 %all-to-all-start.1 = ((f32[4,320,256]{2,1,0:T(8,128)}), f32[4,320,256]{2,1,0:T(8,128)S(1)}, u32[]{:S(2)}, u32[]{:S(2)}) async-start(f32[4,320,256]{2,1,0:T(8,128)} %get-tuple-element.53), calls=%async_computation.1 | async-start | bytes 2621440 | tf_op jit(solution)/shard_map/all_to_all | solution.py:225
  32.3 2.5 %collective-permute-start.8 = (f32[256,256]{1,0:T(8,128)}, f32[256,256]{1,0:T(8,128)S(1)}, u32[]{:S(2)}, u32[]{:S(2)}) collective-permute-start(f32[256,256]{1,0:T(8,128)} %get-tuple-element.57.b0), channel_id=1, source_target_pairs={{0,3},{1,2},{2,1},{3,0},{4,7},{5,6},{6,5},{7,4},{8,11},{9,10},{10,... | collective-permute-start | bytes 786440 | tf_op jit(solution)/shard_map/ppermute | solution.py:217
  35.5 6.1 %collective-permute-start.9 = (f32[64,256]{1,0:T(8,128)S(1)}, f32[64,256]{1,0:T(8,128)S(1)}, u32[]{:S(2)}, u32[]{:S(2)}) collective-permute-start(f32[64,256]{1,0:T(8,128)S(1)} %get-tuple-element.56), channel_id=1, source_target_pairs={{0,128},{128,0},{1,129},{129,1},{2,130},{130,2},{3,131},{131,3},{4... | collective-permute-start | bytes 196616 | tf_op jit(solution)/shard_map/ppermute | solution.py:217
  43.3 2.5 %collective-permute-start.12 = (f32[256,256]{1,0:T(8,128)S(1)}, f32[256,256]{1,0:T(8,128)S(1)}, u32[]{:S(2)}, u32[]{:S(2)}) collective-permute-start(f32[256,256]{1,0:T(8,128)S(1)} %constant_dynamic-update-slice_fusion.7.c0), channel_id=1, source_target_pairs={{0,3},{1,2},{2,1},{3,0},{4,7},{5,6},{6,5},{7,4},{8,11},{9,10},{10,... | collective-permute-start | bytes 786440 | tf_op jit(solution)/shard_map/ppermute | solution.py:217
  48.7 3.7 %collective-permute-done.12.c3 = f32[256,256]{1,0:T(8,128)S(1)} collective-permute-done((f32[256,256]{1,0:T(8,128)S(1)}, f32[256,256]{1,0:T(8,128)S(1)}, u32[]{:S(2)}, u32[]{:S(2)}) %collective-permute-start.12) | collective-permute-done | bytes 262176 | tf_op jit(solution)/shard_map/ppermute | solution.py:217
  54.7 6.1 %collective-permute-start.14 = (f32[4,320,256]{2,1,0:T(8,128)S(1)}, f32[4,320,256]{2,1,0:T(8,128)S(1)}, u32[]{:S(2)}, u32[]{:S(2)}) collective-permute-start(f32[4,320,256]{2,1,0:T(8,128)S(1)} %all-to-all-done.1.own), channel_id=1, source_target_pairs={{0,4},{4,0},{1,5},{5,1},{2,6},{6,2},{3,7},{7,3},{8,12},{12,8},{9,1... | collective-permute-start | bytes 3932168 | tf_op jit(solution)/shard_map/ppermute | solution.py:217
  60.8 3.4 %collective-permute-done.13.other_3 = f32[4,128,256]{2,1,0:T(8,128)S(1)} collective-permute-done((f32[4,128,256]{2,1,0:T(8,128)S(1)}, f32[4,128,256]{2,1,0:T(8,128)S(1)}, u32[]{:S(2)}, u32[]{:S(2)}) %collective-permute-start.13) | collective-permute-done | bytes 524320 | tf_op jit(solution)/shard_map/ppermute | solution.py:217
  68.1 3.0 %shard_map.154 = f32[4,320,256]{2,1,0:T(8,128)} custom-call(s32[32]{0:T(128)S(1)} %concatenate.19.ids, f32[320,256]{1,0:T(8,128)S(1)} %constant_dynamic-update-slice_fusion.5.a0, f32[320,256]{1,0:T(8,128)S(1)} %copy-done.6, f32[320,256]{1,0:T(8,128)S(1)} %collective-permute-done.4.a2, f32[320,256]{1,0:T(8,128)S(1)} %collective-permute-done.5.a3, ...), custom_call_target="tpu_custom_call" | custom-call | flops 4400000000 | tf_op jit(solution)/shard_map/pallas_call | solution.py:48
  72.1 4.5 %all-to-all-start.2 = ((f32[4,320,256]{2,1,0:T(8,128)}), f32[4,320,256]{2,1,0:T(8,128)S(1)}, u32[]{:S(2)}, u32[]{:S(2)}) async-start(f32[4,320,256]{2,1,0:T(8,128)} %shard_map.154), calls=%async_computation.2 | async-start | bytes 2621440 | tf_op jit(solution)/shard_map/all_to_all | solution.py:225
  81.7 3.0 %collective-permute-start.17 = (f32[128,256]{1,0:T(8,128)S(1)}, f32[128,256]{1,0:T(8,128)S(1)}, u32[]{:S(2)}, u32[]{:S(2)}) collective-permute-start(f32[128,256]{1,0:T(8,128)S(1)} %get-tuple-element.67.y0), channel_id=1, source_target_pairs={{0,3},{1,2},{2,1},{3,0},{4,7},{5,6},{6,5},{7,4},{8,11},{9,10},{10,... | collective-permute-start | bytes 393224 | tf_op jit(solution)/shard_map/ppermute | solution.py:217
  85.4 4.8 %collective-permute-done.17.y3 = f32[128,256]{1,0:T(8,128)S(1)} collective-permute-done((f32[128,256]{1,0:T(8,128)S(1)}, f32[128,256]{1,0:T(8,128)S(1)}, u32[]{:S(2)}, u32[]{:S(2)}) %collective-permute-start.17) | collective-permute-done | bytes 131104 | tf_op jit(solution)/shard_map/ppermute | solution.py:217
  92.2 2.6 %collective-permute-start.20 = (f32[128,256]{1,0:T(8,128)S(1)}, f32[128,256]{1,0:T(8,128)S(1)}, u32[]{:S(2)}, u32[]{:S(2)}) collective-permute-start(f32[128,256]{1,0:T(8,128)S(1)} %shard_map.156.m0.m1), channel_id=1, source_target_pairs={{0,3},{1,2},{2,1},{3,0},{4,7},{5,6},{6,5},{7,4},{8,11},{9,10},{10,... | collective-permute-start | bytes 393224 | tf_op jit(solution)/shard_map/ppermute | solution.py:217
  96.2 2.8 %collective-permute-done.20.m3 = f32[128,256]{1,0:T(8,128)S(1)} collective-permute-done((f32[128,256]{1,0:T(8,128)S(1)}, f32[128,256]{1,0:T(8,128)S(1)}, u32[]{:S(2)}, u32[]{:S(2)}) %collective-permute-start.20) | collective-permute-done | bytes 131104 | tf_op jit(solution)/shard_map/ppermute | solution.py:217
  100.3 3.4 %collective-permute-start.21 = (f32[4,320,256]{2,1,0:T(8,128)S(1)}, f32[4,320,256]{2,1,0:T(8,128)S(1)}, u32[]{:S(2)}, u32[]{:S(2)}) collective-permute-start(f32[4,320,256]{2,1,0:T(8,128)S(1)} %all-to-all-done.2.own), channel_id=1, source_target_pairs={{0,4},{4,0},{1,5},{5,1},{2,6},{6,2},{3,7},{7,3},{8,12},{12,8},{9,1... | collective-permute-start | bytes 3932168 | tf_op jit(solution)/shard_map/ppermute | solution.py:217
  104.7 1.7 collective-permute-done.21.other
  112.5 1.8 collective-permute-start.24
  117.1 9.9 %collective-permute-done.24.m3 = f32[256,256]{1,0:T(8,128)S(1)} collective-permute-done((f32[256,256]{1,0:T(8,128)S(1)}, f32[256,256]{1,0:T(8,128)S(1)}, u32[]{:S(2)}, u32[]{:S(2)}) %collective-permute-start.24) | collective-permute-done | bytes 262176 | tf_op jit(solution)/shard_map/ppermute | solution.py:217
  127.3 6.7 %shard_map.159 = (f32[4,384,256]{2,1,0:T(8,128)S(1)}, f32[4,384,256]{2,1,0:T(8,128)S(1)}) custom-call(s32[32]{0:T(128)S(1)} %concatenate.19.ids, f32[256,256]{1,0:T(8,128)} %get-tuple-element.57.b0, f32[256,256]{1,0:T(8,128)S(1)} %copy-done.16, f32[256,256]{1,0:T(8,128)S(1)} %copy-done.13, f32[256,256]{1,0:T(8,128)S(1)} %copy-done.10, ...), custom_call_target="tpu_custom_call" | custom-call | flops 6600000000 | tf_op jit(solution)/shard_map/pallas_call | solution.py:48
  135.6 3.0 %collective-permute-done.25 = f32[4,384,256]{2,1,0:T(8,128)S(1)} collective-permute-done((f32[4,384,256]{2,1,0:T(8,128)S(1)}, f32[4,384,256]{2,1,0:T(8,128)S(1)}, u32[]{:S(2)}, u32[]{:S(2)}) %collective-permute-start.25) | collective-permute-done | bytes 1572896 | tf_op jit(solution)/shard_map/ppermute | solution.py:217
  140.0 4.2 %all-to-all-start.3 = ((f32[4,384,256]{2,1,0:T(8,128)}), f32[4,384,256]{2,1,0:T(8,128)S(1)}, u32[]{:S(2)}, u32[]{:S(2)}) async-start(f32[4,384,256]{2,1,0:T(8,128)} %add.33), calls=%async_computation.3 | async-start | bytes 3145728 | tf_op jit(solution)/shard_map/all_to_all | solution.py:225
  147.5 7.6 %collective-permute-done.28.w3 = f32[192,256]{1,0:T(8,128)S(1)} collective-permute-done((f32[192,256]{1,0:T(8,128)S(1)}, f32[192,256]{1,0:T(8,128)S(1)}, u32[]{:S(2)}, u32[]{:S(2)}) %collective-permute-start.28) | collective-permute-done | bytes 196640 | tf_op jit(solution)/shard_map/ppermute | solution.py:217
  156.5 7.9 %all-to-all-done.3.parts = f32[4,384,256]{2,1,0:T(8,128)S(1)} async-done(((f32[4,384,256]{2,1,0:T(8,128)}), f32[4,384,256]{2,1,0:T(8,128)S(1)}, u32[]{:S(2)}, u32[]{:S(2)}) %all-to-all-start.3) | async-done | bytes 1572896 | tf_op jit(solution)/shard_map/all_to_all | solution.py:225
  167.2 2.2 %shard_map.160 = (f32[128,256]{1,0:T(8,128)S(1)}, f32[64,256]{1,0:T(8,128)}, f32[192,256]{1,0:T(8,128)}, f32[4,128,256]{2,1,0:T(8,128)S(1)}, f32[4,128,256]{2,1,0:T(8,128)S(1)}) custom-call(s32[32]{0:T(128)S(1)} %concatenate.19.ids, f32[4,384,256]{2,1,0:T(8,128)S(1)} %all-to-all-done.3.parts, f32[320,256]{1,0:T(8,128)S(1)} %constant_dynamic-update-slice_fusion.5.a0, ...), custom_call_target="tpu_custom_call" | custom-call | flops 3300000000 | tf_op jit(solution)/shard_map/pallas_call | solution.py:48
  173.4 3.5 %all-to-all-start.4 = ((f32[4,128,256]{2,1,0:T(8,128)}), f32[4,128,256]{2,1,0:T(8,128)S(1)}, u32[]{:S(2)}, u32[]{:S(2)}) async-start(f32[4,128,256]{2,1,0:T(8,128)} %add.34), calls=%async_computation.4 | async-start | bytes 1048576 | tf_op jit(solution)/shard_map/all_to_all | solution.py:225
  178.7 7.3 %all-to-all-done.4 = f32[4,128,256]{2,1,0:T(8,128)S(1)} async-done(((f32[4,128,256]{2,1,0:T(8,128)}), f32[4,128,256]{2,1,0:T(8,128)S(1)}, u32[]{:S(2)}, u32[]{:S(2)}) %all-to-all-start.4) | async-done | bytes 524320 | tf_op jit(solution)/shard_map/all_to_all | solution.py:225
  (144 shorter events, 58.0 us)
Async XLA Ops:
  2.6 24.4 %collective-permute-start.5 = (f32[320,256]{1,0:T(8,128)S(1)}, f32[320,256]{1,0:T(8,128)S(1)}, u32[]{:S(2)}, u32[]{:S(2)}) collective-permute-start(f32[320,256]{1,0:T(8,128)S(1)} %constant_dynamic-update-slice_fusion.5.a0), channel_id=1, source_target_pairs={{0,3},{1,2},{2,1},{3,0},{4,7},{5,6},{6,5},{7,4},{8,11},{9,10},{10,... | collective-permute-start | bytes 983048 | tf_op jit(solution)/shard_map/ppermute | solution.py:217
  6.0 21.0 %collective-permute-start.4 = (f32[320,256]{1,0:T(8,128)S(1)}, f32[320,256]{1,0:T(8,128)S(1)}, u32[]{:S(2)}, u32[]{:S(2)}) collective-permute-start(f32[320,256]{1,0:T(8,128)S(1)} %constant_dynamic-update-slice_fusion.5.a0), channel_id=1, source_target_pairs={{0,2},{1,3},{2,0},{3,1},{4,6},{5,7},{6,4},{7,5},{8,10},{9,11},{10,... | collective-permute-start | bytes 983048 | tf_op jit(solution)/shard_map/ppermute | solution.py:217
  6.5 20.5 %collective-permute-start.3 = (f32[320,256]{1,0:T(8,128)S(1)}, f32[320,256]{1,0:T(8,128)S(1)}, u32[]{:S(2)}, u32[]{:S(2)}) collective-permute-start(f32[320,256]{1,0:T(8,128)S(1)} %constant_dynamic-update-slice_fusion.5.a0), channel_id=1, source_target_pairs={{0,1},{1,0},{2,3},{3,2},{4,5},{5,4},{6,7},{7,6},{8,9},{9,8},{10,11... | collective-permute-start | bytes 983048 | tf_op jit(solution)/shard_map/ppermute | solution.py:217
  8.9 9.4 %collective-permute-start = (f32[64,256]{1,0:T(8,128)S(1)}, f32[64,256]{1,0:T(8,128)S(1)}, u32[]{:S(2)}, u32[]{:S(2)}) collective-permute-start(f32[64,256]{1,0:T(8,128)S(1)} %constant_dynamic-update-slice_fusion.own_1), channel_id=1, source_target_pairs={{0,32},{32,0},{1,33},{33,1},{2,34},{34,2},{3,35},{35,3},{4,36},{36... | collective-permute-start | bytes 196616 | tf_op jit(solution)/shard_map/ppermute | solution.py:217
  12.3 9.9 %collective-permute-start.2 = (f32[128,256]{1,0:T(8,128)S(1)}, f32[128,256]{1,0:T(8,128)S(1)}, u32[]{:S(2)}, u32[]{:S(2)}) collective-permute-start(f32[128,256]{1,0:T(8,128)S(1)} %constant_dynamic-update-slice_fusion.3.own_2), channel_id=1, source_target_pairs={{0,32},{32,0},{1,33},{33,1},{2,34},{34,2},{3,35},{35,3},{4,36},{36... | collective-permute-start | bytes 393224 | tf_op jit(solution)/shard_map/ppermute | solution.py:217
  14.0 13.7 %all-to-all-start = ((f32[4,128,256]{2,1,0:T(8,128)}), f32[4,128,256]{2,1,0:T(8,128)S(1)}, u32[]{:S(2)}, u32[]{:S(2)}) async-start(f32[4,128,256]{2,1,0:T(8,128)} %broadcast_in_dim.2), calls=%async_computation | async-start | bytes 1048576 | tf_op jit(solution)/shard_map/all_to_all | solution.py:225
  18.3 6.8 %collective-permute-start.1 = (f32[128,256]{1,0:T(8,128)S(1)}, f32[128,256]{1,0:T(8,128)S(1)}, u32[]{:S(2)}, u32[]{:S(2)}) collective-permute-start(f32[128,256]{1,0:T(8,128)S(1)} %pad_maximum_fusion), channel_id=1, source_target_pairs={{0,64},{64,0},{1,65},{65,1},{2,66},{66,2},{3,67},{67,3},{4,68},{68... | collective-permute-start | bytes 393224 | tf_op jit(solution)/shard_map/ppermute | solution.py:217
  27.8 26.9 %all-to-all-start.1 = ((f32[4,320,256]{2,1,0:T(8,128)}), f32[4,320,256]{2,1,0:T(8,128)S(1)}, u32[]{:S(2)}, u32[]{:S(2)}) async-start(f32[4,320,256]{2,1,0:T(8,128)} %get-tuple-element.53), calls=%async_computation.1 | async-start | bytes 2621440 | tf_op jit(solution)/shard_map/all_to_all | solution.py:225
  32.3 14.0 %collective-permute-start.8 = (f32[256,256]{1,0:T(8,128)}, f32[256,256]{1,0:T(8,128)S(1)}, u32[]{:S(2)}, u32[]{:S(2)}) collective-permute-start(f32[256,256]{1,0:T(8,128)} %get-tuple-element.57.b0), channel_id=1, source_target_pairs={{0,3},{1,2},{2,1},{3,0},{4,7},{5,6},{6,5},{7,4},{8,11},{9,10},{10,... | collective-permute-start | bytes 786440 | tf_op jit(solution)/shard_map/ppermute | solution.py:217
  34.8 12.5 %collective-permute-start.7 = (f32[256,256]{1,0:T(8,128)}, f32[256,256]{1,0:T(8,128)S(1)}, u32[]{:S(2)}, u32[]{:S(2)}) collective-permute-start(f32[256,256]{1,0:T(8,128)} %get-tuple-element.57.b0), channel_id=1, source_target_pairs={{0,2},{1,3},{2,0},{3,1},{4,6},{5,7},{6,4},{7,5},{8,10},{9,11},{10,... | collective-permute-start | bytes 786440 | tf_op jit(solution)/shard_map/ppermute | solution.py:217
  35.3 12.6 %collective-permute-start.6 = (f32[256,256]{1,0:T(8,128)}, f32[256,256]{1,0:T(8,128)S(1)}, u32[]{:S(2)}, u32[]{:S(2)}) collective-permute-start(f32[256,256]{1,0:T(8,128)} %get-tuple-element.57.b0), channel_id=1, source_target_pairs={{0,1},{1,0},{2,3},{3,2},{4,5},{5,4},{6,7},{7,6},{8,9},{9,8},{10,11... | collective-permute-start | bytes 786440 | tf_op jit(solution)/shard_map/ppermute | solution.py:217
  35.5 7.8 %collective-permute-start.9 = (f32[64,256]{1,0:T(8,128)S(1)}, f32[64,256]{1,0:T(8,128)S(1)}, u32[]{:S(2)}, u32[]{:S(2)}) collective-permute-start(f32[64,256]{1,0:T(8,128)S(1)} %get-tuple-element.56), channel_id=1, source_target_pairs={{0,128},{128,0},{1,129},{129,1},{2,130},{130,2},{3,131},{131,3},{4... | collective-permute-start | bytes 196616 | tf_op jit(solution)/shard_map/ppermute | solution.py:217
  43.3 9.1 %collective-permute-start.12 = (f32[256,256]{1,0:T(8,128)S(1)}, f32[256,256]{1,0:T(8,128)S(1)}, u32[]{:S(2)}, u32[]{:S(2)}) collective-permute-start(f32[256,256]{1,0:T(8,128)S(1)} %constant_dynamic-update-slice_fusion.7.c0), channel_id=1, source_target_pairs={{0,3},{1,2},{2,1},{3,0},{4,7},{5,6},{6,5},{7,4},{8,11},{9,10},{10,... | collective-permute-start | bytes 786440 | tf_op jit(solution)/shard_map/ppermute | solution.py:217
  45.8 7.3 %collective-permute-start.11 = (f32[256,256]{1,0:T(8,128)S(1)}, f32[256,256]{1,0:T(8,128)S(1)}, u32[]{:S(2)}, u32[]{:S(2)}) collective-permute-start(f32[256,256]{1,0:T(8,128)S(1)} %constant_dynamic-update-slice_fusion.7.c0), channel_id=1, source_target_pairs={{0,2},{1,3},{2,0},{3,1},{4,6},{5,7},{6,4},{7,5},{8,10},{9,11},{10,... | collective-permute-start | bytes 786440 | tf_op jit(solution)/shard_map/ppermute | solution.py:217
  47.0 6.9 %collective-permute-start.10 = (f32[256,256]{1,0:T(8,128)S(1)}, f32[256,256]{1,0:T(8,128)S(1)}, u32[]{:S(2)}, u32[]{:S(2)}) collective-permute-start(f32[256,256]{1,0:T(8,128)S(1)} %constant_dynamic-update-slice_fusion.7.c0), channel_id=1, source_target_pairs={{0,1},{1,0},{2,3},{3,2},{4,5},{5,4},{6,7},{7,6},{8,9},{9,8},{10,11... | collective-permute-start | bytes 786440 | tf_op jit(solution)/shard_map/ppermute | solution.py:217
  54.7 9.6 %collective-permute-start.14 = (f32[4,320,256]{2,1,0:T(8,128)S(1)}, f32[4,320,256]{2,1,0:T(8,128)S(1)}, u32[]{:S(2)}, u32[]{:S(2)}) collective-permute-start(f32[4,320,256]{2,1,0:T(8,128)S(1)} %all-to-all-done.1.own), channel_id=1, source_target_pairs={{0,4},{4,0},{1,5},{5,1},{2,6},{6,2},{3,7},{7,3},{8,12},{12,8},{9,1... | collective-permute-start | bytes 3932168 | tf_op jit(solution)/shard_map/ppermute | solution.py:217
  72.1 28.2 %all-to-all-start.2 = ((f32[4,320,256]{2,1,0:T(8,128)}), f32[4,320,256]{2,1,0:T(8,128)S(1)}, u32[]{:S(2)}, u32[]{:S(2)}) async-start(f32[4,320,256]{2,1,0:T(8,128)} %shard_map.154), calls=%async_computation.2 | async-start | bytes 2621440 | tf_op jit(solution)/shard_map/all_to_all | solution.py:225
  81.7 8.5 %collective-permute-start.17 = (f32[128,256]{1,0:T(8,128)S(1)}, f32[128,256]{1,0:T(8,128)S(1)}, u32[]{:S(2)}, u32[]{:S(2)}) collective-permute-start(f32[128,256]{1,0:T(8,128)S(1)} %get-tuple-element.67.y0), channel_id=1, source_target_pairs={{0,3},{1,2},{2,1},{3,0},{4,7},{5,6},{6,5},{7,4},{8,11},{9,10},{10,... | collective-permute-start | bytes 393224 | tf_op jit(solution)/shard_map/ppermute | solution.py:217
  84.7 5.6 %collective-permute-start.16 = (f32[128,256]{1,0:T(8,128)S(1)}, f32[128,256]{1,0:T(8,128)S(1)}, u32[]{:S(2)}, u32[]{:S(2)}) collective-permute-start(f32[128,256]{1,0:T(8,128)S(1)} %get-tuple-element.67.y0), channel_id=1, source_target_pairs={{0,2},{1,3},{2,0},{3,1},{4,6},{5,7},{6,4},{7,5},{8,10},{9,11},{10,... | collective-permute-start | bytes 393224 | tf_op jit(solution)/shard_map/ppermute | solution.py:217
  84.7 6.5 %collective-permute-start.15 = (f32[128,256]{1,0:T(8,128)S(1)}, f32[128,256]{1,0:T(8,128)S(1)}, u32[]{:S(2)}, u32[]{:S(2)}) collective-permute-start(f32[128,256]{1,0:T(8,128)S(1)} %get-tuple-element.67.y0), channel_id=1, source_target_pairs={{0,1},{1,0},{2,3},{3,2},{4,5},{5,4},{6,7},{7,6},{8,9},{9,8},{10,11... | collective-permute-start | bytes 393224 | tf_op jit(solution)/shard_map/ppermute | solution.py:217
  92.2 6.8 %collective-permute-start.20 = (f32[128,256]{1,0:T(8,128)S(1)}, f32[128,256]{1,0:T(8,128)S(1)}, u32[]{:S(2)}, u32[]{:S(2)}) collective-permute-start(f32[128,256]{1,0:T(8,128)S(1)} %shard_map.156.m0.m1), channel_id=1, source_target_pairs={{0,3},{1,2},{2,1},{3,0},{4,7},{5,6},{6,5},{7,4},{8,11},{9,10},{10,... | collective-permute-start | bytes 393224 | tf_op jit(solution)/shard_map/ppermute | solution.py:217
  94.9 5.4 %collective-permute-start.19 = (f32[128,256]{1,0:T(8,128)S(1)}, f32[128,256]{1,0:T(8,128)S(1)}, u32[]{:S(2)}, u32[]{:S(2)}) collective-permute-start(f32[128,256]{1,0:T(8,128)S(1)} %shard_map.156.m0.m1), channel_id=1, source_target_pairs={{0,2},{1,3},{2,0},{3,1},{4,6},{5,7},{6,4},{7,5},{8,10},{9,11},{10,... | collective-permute-start | bytes 393224 | tf_op jit(solution)/shard_map/ppermute | solution.py:217
  94.9 5.4 %collective-permute-start.18 = (f32[128,256]{1,0:T(8,128)S(1)}, f32[128,256]{1,0:T(8,128)S(1)}, u32[]{:S(2)}, u32[]{:S(2)}) collective-permute-start(f32[128,256]{1,0:T(8,128)S(1)} %shard_map.156.m0.m1), channel_id=1, source_target_pairs={{0,1},{1,0},{2,3},{3,2},{4,5},{5,4},{6,7},{7,6},{8,9},{9,8},{10,11... | collective-permute-start | bytes 393224 | tf_op jit(solution)/shard_map/ppermute | solution.py:217
  100.3 6.1 %collective-permute-start.21 = (f32[4,320,256]{2,1,0:T(8,128)S(1)}, f32[4,320,256]{2,1,0:T(8,128)S(1)}, u32[]{:S(2)}, u32[]{:S(2)}) collective-permute-start(f32[4,320,256]{2,1,0:T(8,128)S(1)} %all-to-all-done.2.own), channel_id=1, source_target_pairs={{0,4},{4,0},{1,5},{5,1},{2,6},{6,2},{3,7},{7,3},{8,12},{12,8},{9,1... | collective-permute-start | bytes 3932168 | tf_op jit(solution)/shard_map/ppermute | solution.py:217
  112.5 14.4 %collective-permute-start.24 = (f32[256,256]{1,0:T(8,128)S(1)}, f32[256,256]{1,0:T(8,128)S(1)}, u32[]{:S(2)}, u32[]{:S(2)}) collective-permute-start(f32[256,256]{1,0:T(8,128)S(1)} %get-tuple-element.74.m2.m0), channel_id=1, source_target_pairs={{0,3},{1,2},{2,1},{3,0},{4,7},{5,6},{6,5},{7,4},{8,11},{9,10},{10,... | collective-permute-start | bytes 786440 | tf_op jit(solution)/shard_map/ppermute | solution.py:217
  114.3 12.7 %collective-permute-start.23 = (f32[256,256]{1,0:T(8,128)S(1)}, f32[256,256]{1,0:T(8,128)S(1)}, u32[]{:S(2)}, u32[]{:S(2)}) collective-permute-start(f32[256,256]{1,0:T(8,128)S(1)} %get-tuple-element.74.m2.m0), channel_id=1, source_target_pairs={{0,2},{1,3},{2,0},{3,1},{4,6},{5,7},{6,4},{7,5},{8,10},{9,11},{10,... | collective-permute-start | bytes 786440 | tf_op jit(solution)/shard_map/ppermute | solution.py:217
  114.3 13.0 %collective-permute-start.22 = (f32[256,256]{1,0:T(8,128)S(1)}, f32[256,256]{1,0:T(8,128)S(1)}, u32[]{:S(2)}, u32[]{:S(2)}) collective-permute-start(f32[256,256]{1,0:T(8,128)S(1)} %get-tuple-element.74.m2.m0), channel_id=1, source_target_pairs={{0,1},{1,0},{2,3},{3,2},{4,5},{5,4},{6,7},{7,6},{8,9},{9,8},{10,11... | collective-permute-start | bytes 786440 | tf_op jit(solution)/shard_map/ppermute | solution.py:217
  140.0 24.3 %all-to-all-start.3 = ((f32[4,384,256]{2,1,0:T(8,128)}), f32[4,384,256]{2,1,0:T(8,128)S(1)}, u32[]{:S(2)}, u32[]{:S(2)}) async-start(f32[4,384,256]{2,1,0:T(8,128)} %add.33), calls=%async_computation.3 | async-start | bytes 3145728 | tf_op jit(solution)/shard_map/all_to_all | solution.py:225
  144.2 10.9 %collective-permute-start.28 = (f32[192,256]{1,0:T(8,128)S(1)}, f32[192,256]{1,0:T(8,128)S(1)}, u32[]{:S(2)}, u32[]{:S(2)}) collective-permute-start(f32[192,256]{1,0:T(8,128)S(1)} %slice_bitcast_fusion.w0), channel_id=1, source_target_pairs={{0,3},{1,2},{2,1},{3,0},{4,7},{5,6},{6,5},{7,4},{8,11},{9,10},{10,... | collective-permute-start | bytes 589832 | tf_op jit(solution)/shard_map/ppermute | solution.py:217
  145.9 9.2 %collective-permute-start.27 = (f32[192,256]{1,0:T(8,128)S(1)}, f32[192,256]{1,0:T(8,128)S(1)}, u32[]{:S(2)}, u32[]{:S(2)}) collective-permute-start(f32[192,256]{1,0:T(8,128)S(1)} %slice_bitcast_fusion.w0), channel_id=1, source_target_pairs={{0,2},{1,3},{2,0},{3,1},{4,6},{5,7},{6,4},{7,5},{8,10},{9,11},{10,... | collective-permute-start | bytes 589832 | tf_op jit(solution)/shard_map/ppermute | solution.py:217
  145.9 9.9 %collective-permute-start.26 = (f32[192,256]{1,0:T(8,128)S(1)}, f32[192,256]{1,0:T(8,128)S(1)}, u32[]{:S(2)}, u32[]{:S(2)}) collective-permute-start(f32[192,256]{1,0:T(8,128)S(1)} %slice_bitcast_fusion.w0), channel_id=1, source_target_pairs={{0,1},{1,0},{2,3},{3,2},{4,5},{5,4},{6,7},{7,6},{8,9},{9,8},{10,11... | collective-permute-start | bytes 589832 | tf_op jit(solution)/shard_map/ppermute | solution.py:217
  173.4 12.7 %all-to-all-start.4 = ((f32[4,128,256]{2,1,0:T(8,128)}), f32[4,128,256]{2,1,0:T(8,128)S(1)}, u32[]{:S(2)}, u32[]{:S(2)}) async-start(f32[4,128,256]{2,1,0:T(8,128)} %add.34), calls=%async_computation.4 | async-start | bytes 1048576 | tf_op jit(solution)/shard_map/all_to_all | solution.py:225
  (40 other events, 211.7 us)

commit v4 on v3

v4 whole, which is shorter than its diff:
```python
import jax
import jax.numpy as jnp
from jax import lax
from jax.experimental import pallas as pl
from jax.experimental.pallas import tpu as pltpu
from jax.sharding import Mesh, PartitionSpec as P

S = 1024
BLOCK = 128
U1 = 512
U2 = 1024
U3 = 1536
COLS = 256
F32 = jnp.float32

CORE, PART, SLOT, PAIR, FRONT = 0, 1, 2, 3, 4


def halves(values):
    high = values.astype(jnp.bfloat16)
    return high, (values - high.astype(F32)).astype(jnp.bfloat16)


def dot(left, right, contract=((1,), (0,))):
    left_high, left_low = halves(left)
    right_high, right_low = halves(right)

    def one(a, b):
        return lax.dot_general(a, b, (contract, ((), ())), preferred_element_type=F32)

    return one(left_high, right_high) + (one(left_high, right_low) + one(left_low, right_high))


def inner(left, right):
    return dot(left, right, ((0,), (0,)))


def times(number, unit):
    return pl.multiple_of(number * unit, unit)


def ordered(core, own, other):
    return [jnp.where(core == 0, own, other), jnp.where(core == 0, other, own)]


class Far:

    def __init__(self, value, start=0, rows=None):
        self.value = value
        self.start = start
        self.shape = value if isinstance(value, tuple) else value.shape
        self.shape = (rows or self.shape[0],) + tuple(self.shape[1:])


def call(body, micros, outs, scratch, *operands):
    away_in = [at for at, operand in enumerate(operands) if isinstance(operand, Far)]
    away_out = [at for at, out in enumerate(outs) if isinstance(out, Far)]
    values = [operand.value if isinstance(operand, Far) else operand for operand in operands]
    shapes = [out.value if isinstance(out, Far) else out for out in outs]
    fetched = [operands[at].shape for at in away_in]
    returned = [shapes[at] for at in away_out]
    near = pl.BlockSpec(memory_space=pltpu.VMEM)
    distant = pl.BlockSpec(memory_space=pltpu.HBM)

    def place(at, value):
        if at in away_in:
            return distant
        return near if value.dtype == F32 else pl.BlockSpec(memory_space=pltpu.SMEM)

    def kernel(*refs):
        inputs = list(refs[: len(values)])
        results = list(refs[len(values) : len(values) + len(outs)])
        own = list(refs[len(values) + len(outs) :])
        held = own[: len(scratch)]
        buffers = own[len(scratch) :]
        copies = []
        for number, at in enumerate(away_in):
            rows = pl.ds(operands[at].start, fetched[number][0])
            copy = pltpu.make_async_copy(
                inputs[at].at[rows], buffers[number], buffers[-1].at[number]
            )
            copy.start()
            copies.append(copy)
            inputs[at] = buffers[number]
        for copy in copies:
            copy.wait()
        copies = []
        for number, at in enumerate(away_out):
            number += len(away_in)
            copies.append(
                pltpu.make_async_copy(buffers[number], results[at], buffers[-1].at[number])
            )
            results[at] = buffers[number]
        body(*inputs, *results, *held)
        for copy in copies:
            copy.start()
        for copy in copies:
            copy.wait()

    count = len(fetched) + len(returned)
    return pl.pallas_call(
        kernel,
        out_shape=[jax.ShapeDtypeStruct(shape, F32) for shape in shapes],
        in_specs=[place(at, value) for at, value in enumerate(values)],
        out_specs=[distant if at in away_out else near for at in range(len(outs))],
        scratch_shapes=[pltpu.VMEM(shape, F32) for shape in scratch + fetched + returned]
        + ([pltpu.SemaphoreType.DMA((count,))] if count else []),
        cost_estimate=pl.CostEstimate(
            flops=micros * 1_100_000_000, bytes_accessed=0, transcendentals=0
        ),
        compiler_params=pltpu.CompilerParams(vmem_limit_bytes=28 * 1024 * 1024),
    )(*values)


def pack(v0, v1, b1, v2, b2, v3, b3, own_1, own_2, own_3, columns_3):
    own_1[0:32, :] = v1[...]
    own_1[32:48, :] = b1[...]
    own_1[48:64, :] = v0[...]
    own_2[0:64, :] = v2[...]
    own_2[64:128, :] = b2[...]
    own_3[0:192, :] = b3[...]
    own_3[192:320, :] = v3[...]
    for copy in range(4):
        columns_3[copy] = v3[...]


def place_ancestors(ids, p0, p1, p2, p3, own_2, pair_2, early, rows, row_0):
    slot, pair = ids[SLOT], ids[PAIR]
    for distance, ref in enumerate((p0, p1, p2, p3)):
        source = slot ^ distance
        values = ref[...]
        rows[pl.ds(256 + times(source, 32), 32), :] = values[0:32]
        rows[pl.ds(384 + times(source, 16), 16), :] = values[48:64]
        row_0[pl.ds(times(source, 16), 16), :] = values[48:64]
        for copy in range(4):
            early[copy, pl.ds(times(source, 32), 32), :] = values[0:32]
            early[copy, pl.ds(256 + times(source, 16), 16), :] = values[32:48]
    for distance, ref in enumerate((own_2, pair_2)):
        start = times(pair ^ distance, 64)
        values = ref[...]
        rows[pl.ds(start, 64), :] = values[64:128]
        rows[pl.ds(128 + start, 64), :] = values[0:64]
        for copy in range(4):
            early[copy, pl.ds(128 + start, 64), :] = values[0:64]


def add(left, right, out):
    out[...] = left[...] + right[...]


def add_four(parts, out):
    out[...] = (parts[0] + parts[1]) + (parts[2] + parts[3])


def couple_front(ids, a0, a1, a2, a3, own, other, w3, v3):
    core, part = ids[CORE], ids[PART]
    total = jnp.zeros((192, COLS), F32)
    for distance, ref in enumerate((a0, a1, a2, a3)):
        quarter = part ^ distance
        total += dot(ref[0:192, :], jnp.concatenate(ordered(core, own[quarter], other[quarter]), 0))
        v3[:, pl.ds(times(quarter, COLS), COLS)] = ref[192:320, :]
    w3[...] = total


def shelve(ids, r0, r1, r2, r3, held):
    for distance, ref in enumerate((r0, r1, r2, r3)):
        held[:, pl.ds(times(ids[PART] ^ distance, COLS), COLS)] = ref[...]


def middle(
    ids, sel, b2, v0_top, h0, h1, h2, h3, own, other, w3, coupling, y1, f0, v0, v1_columns
):
    core, part = ids[CORE], ids[PART]
    v0[0:64, :] = v0_top[...]
    for distance, ref in enumerate((h0, h1, h2, h3)):
        v0[64:128, pl.ds(times(part ^ distance, COLS), COLS)] = ref[...]
    for block in range(4):
        f0[:, block * BLOCK : (block + 1) * BLOCK] = v0[
            :, pl.ds(times(sel[ids[FRONT] >> 2, block], BLOCK), BLOCK)
        ]
    rows = []
    for slot in range(4):
        start = 256 + slot * 16
        for y in range(4):
            rows += ordered(core, own[y, start : start + 16, :], other[y, start : start + 16, :])
    y1[...] = dot(f0[...], jnp.concatenate(rows, 0))
    w2 = jnp.zeros((128, COLS), F32)
    for pair in range(2):
        rows = []
        start = 128 + pair * 64
        for y in range(4):
            rows += ordered(core, own[y, start : start + 64, :], other[y, start : start + 64, :])
        w2 += dot(b2[:, pair * 512 : (pair + 1) * 512], jnp.concatenate(rows, 0))
    for copy in range(4):
        coupling[copy, 0:128, :] = w2
        coupling[copy, 128:320, :] = w3[...]
    for slot in range(4):
        start = slot * 32
        for y in range(4):
            place = slot * 256 + y * 64
            first, second = ordered(
                core, own[y, start : start + 32, :], other[y, start : start + 32, :]
            )
            v1_columns[place : place + 32, :] = first
            v1_columns[place + 32 : place + 64, :] = second


def second_half(ids, y0, y1, y2, y3, v1_columns, m1):
    part = ids[PART]
    total = jnp.zeros((128, COLS), F32)
    for distance, ref in enumerate((y0, y1, y2, y3)):
        total += dot(ref[...], v1_columns[pl.ds(times(part ^ distance, COLS), COLS), :])
    m1[...] = total


def level_two(
    ids, sel, v1, f0, m0, m1, m2, m3, own, other, out, f1, w3_columns, x1_part, mine, x1
):
    core, part, slot = ids[CORE], ids[PART], ids[SLOT]
    x1[0:128, 0:S] = v1[...]
    x1[0:128, S:] = jnp.zeros((128, U1), F32)
    x1[128:256, S:] = f0[...]
    for distance, ref in enumerate((m0, m1, m2, m3)):
        x1[128:256, pl.ds(times(part ^ distance, COLS), COLS)] = -ref[...]
    for block in range(8):
        f1[:, block * BLOCK : (block + 1) * BLOCK] = x1[
            :, pl.ds(times(sel[ids[FRONT] >> 1, block], BLOCK), BLOCK)
        ]
    total = jnp.zeros((256, COLS), F32)
    for pair in range(2):
        rows = []
        for y in range(4):
            start = pair * 64
            rows += ordered(core, own[y, start : start + 64, :], other[y, start : start + 64, :])
        total += dot(f1[:, pair * 512 : (pair + 1) * 512], jnp.concatenate(rows, 0))
    out[...] = total
    for y in range(4):
        first, second = ordered(core, own[y, 128:320, :], other[y, 128:320, :])
        w3_columns[y * 384 : y * 384 + 192, :] = first
        w3_columns[y * 384 + 192 : y * 384 + 384, :] = second
    x1_part[...] = x1[:, pl.ds(times(slot, 256), 256)]
    mine[...] = x1[:, pl.ds(times(part, COLS), COLS)]


def put(core, keep, send, values, start, rows):
    for y in range(4):
        first = values[2 * y * rows : (2 * y + 1) * rows]
        second = values[(2 * y + 1) * rows : (2 * y + 2) * rows]
        keep[y, start : start + rows, :] = jnp.where(core == 0, first, second)
        send[y, start : start + rows, :] = jnp.where(core == 0, second, first)


def early_sums(ids, v0, f0, x1_part, mine, f1, m2, keep, send):
    core, part = ids[CORE], ids[PART]
    front, slot, pair = ids[FRONT], ids[SLOT], ids[PAIR]
    d0 = inner(v0[:, pl.ds(times(front, BLOCK), BLOCK)], v0[:, pl.ds(times(part, COLS), COLS)])
    put(core, keep, send, d0, 0, 16)
    put(core, keep, send, inner(x1_part[...], mine[...]), 16, 32)
    e1 = inner(f0[:, pl.ds(times(slot, BLOCK), BLOCK)], mine[128:256, :])
    put(core, keep, send, e1, 48, 16)
    put(core, keep, send, inner(f1[:, pl.ds(times(pair, 512), 512)], -m2[...]), 64, 64)


def level_three(
    ids, sel, v2, f1, w3_columns, keep_1, send_1, m0, m1, m2, m3, keep, send, x2, f2
):
    core, part, pair = ids[CORE], ids[PART], ids[PAIR]
    x2[0:128, 0:S] = v2[...]
    x2[0:128, S:] = jnp.zeros((128, U2), F32)
    x2[128:384, S:] = f1[...]
    for distance, ref in enumerate((m0, m1, m2, m3)):
        x2[128:384, pl.ds(times(part ^ distance, COLS), COLS)] = -ref[...]
    for block in range(12):
        f2[:, block * BLOCK : (block + 1) * BLOCK] = x2[
            :, pl.ds(times(sel[ids[FRONT], block], BLOCK), BLOCK)
        ]
    total = dot(f2[...], w3_columns[...])
    for y in range(4):
        keep[y, 0:128, :] = keep_1[y]
        send[y, 0:128, :] = send_1[y]
    put(core, keep, send, inner(f2[...], -total), 192, 192)
    mine = x2[:, pl.ds(times(part, COLS), COLS)]
    put(core, keep, send, inner(x2[:, pl.ds(times(pair, 512), 512)], mine), 128, 64)


def last_level(
    ids, parts, v3, w0, w1, w2, w3, d0, d1, e1, e2, d2, e3, keep, send
):
    core, part = ids[CORE], ids[PART]
    total = (parts[0] + parts[1]) + (parts[2] + parts[3])
    d0[...] = total[0:16]
    d1[...] = total[16:48]
    e1[...] = total[48:64]
    e2[...] = total[64:128]
    d2[...] = total[128:192]
    below = total[192:384]
    e3[...] = below
    right = jnp.concatenate([v3[:, pl.ds(times(part, COLS), COLS)], -below], 0)
    for distance, ref in enumerate((w0, w1, w2, w3)):
        place = part ^ distance
        left = jnp.concatenate([v3[:, pl.ds(times(place, COLS), COLS)], ref[...]], 0)
        rows = inner(left, right)
        keep[place] = jnp.where(core == 0, rows[0:128], rows[128:256])
        send[place] = jnp.where(core == 0, rows[128:256], rows[0:128])


def swapped(array, axis, distance, parts=2):
    return lax.ppermute(array, axis, [(i, i ^ distance) for i in range(parts)])


def around(values, axis="x"):
    return [values] + [swapped(values, axis, distance, 4) for distance in (1, 2, 3)]


def exchanged(values):
    return lax.all_to_all(values, "y", 0, 0)


def core_sum(keep, send):
    (total,) = call(add, 1, [keep.shape], [], keep, swapped(send, "c", 1))
    return exchanged(total)


def shards(v0, v1, b1, selector_1, v2, b2, selector_2, v3, b3, selector_3):
    half = lax.axis_index("h")
    quarter = lax.axis_index("q")
    pair = lax.axis_index("p")
    slot = quarter * 2 + pair
    ids = jnp.stack(
        [lax.axis_index("c"), lax.axis_index("x"), slot, pair, half * 4 + slot]
    ).astype(jnp.int32)

    own_1, own_2, own_3, columns_3 = call(
        pack,
        1,
        [(64, COLS), (128, COLS), (320, COLS), (4, 128, COLS)],
        [],
        *[Far(value) for value in (v0, v1, b1, v2, b2, v3, b3)],
    )
    ancestors = around(own_1, ("q", "p"))
    pair_2 = swapped(own_2, "p", 1)
    own_rows = around(own_3)
    columns_3 = exchanged(columns_3)
    early, rows, row_0 = call(
        place_ancestors,
        2,
        [(4, 320, COLS), (448, COLS), (64, COLS)],
        [],
        ids, *ancestors, own_2, pair_2,
    )
    early, columns_3 = lax.optimization_barrier((early, columns_3))
    early = exchanged(early)
    row_0 = around(swapped(row_0, "h", 1))
    w3, v3_rows = call(
        couple_front,
        2,
        [(192, COLS), Far((128, S))],
        [],
        ids, *own_rows, columns_3, swapped(columns_3, "c", 1),
    )
    (held,) = call(shelve, 1, [Far((448, S))], [], ids, *around(rows))
    early, row_0, w3, v3_rows, held = lax.optimization_barrier(
        (early, row_0, w3, v3_rows, held)
    )

    coupling, y1, f0, v0_rows, v1_columns = call(
        middle,
        4,
        [(4, 320, COLS), (128, COLS), Far((128, U1)), Far((128, S)), Far((S, COLS))],
        [],
        ids, selector_1, Far(held, 0, 128), Far(held, 384, 64), *row_0,
        early, swapped(early, "c", 1), w3,
    )
    coupling = exchanged(coupling)
    (m1,) = call(second_half, 2, [(128, COLS)], [], ids, *around(y1), Far(v1_columns))
    m1, coupling = lax.optimization_barrier((around(m1), coupling))
    m2, f1, w3_columns, x1_part, mine = call(
        level_two,
        3,
        [(256, COLS), Far((256, U2)), Far((U3, COLS)), Far((256, 256)), Far((256, COLS))],
        [(256, S + U1)],
        ids, selector_2, Far(held, 256, 128), Far(f0), *m1,
        coupling, swapped(coupling, "c", 1),
    )
    keep, send = call(
        early_sums,
        3,
        [Far((4, 128, COLS)), Far((4, 128, COLS))],
        [],
        ids, *[Far(value) for value in (v0_rows, f0, x1_part, mine, f1)], m2,
    )
    keep, send = call(
        level_three,
        6,
        [(4, 384, COLS), (4, 384, COLS)],
        [(384, S + U2), (384, U3)],
        ids, selector_3, Far(held, 128, 128), Far(f1), Far(w3_columns), Far(keep), Far(send),
        *around(m2),
    )
    w3, keep, send = lax.optimization_barrier((w3, keep, send))
    w3 = around(w3)
    d0, d1, e1, e2, d2, e3, keep, send = call(
        last_level,
        3,
        [(16, COLS), (32, COLS), (16, COLS), (64, COLS), (64, COLS), (192, COLS)]
        + [(4, 128, COLS)] * 2,
        [],
        ids, core_sum(keep, send), Far(v3_rows), *w3,
    )
    (d3,) = call(add_four, 1, [(128, COLS)], [], core_sum(keep, send))
    return d0, d1, e1, d2, e2, d3, e3


def solution(mesh):
    devices = mesh.devices.reshape(2, 2, 2, 4, 2, 4)
    fine = Mesh(devices, ("h", "q", "p", "y", "c", "x"))
    tiled = P(("h", "q", "p", "y", "c"), "x")
    return jax.shard_map(
        shards,
        mesh=fine,
        in_specs=(tiled, tiled, tiled, P(), tiled, tiled, P(), tiled, tiled, P()),
        out_specs=(tiled,) * 7,
        check_vma=False,
    )
```

time: 188 us -> 180 us (0.957)
  local copies, waits for them, and re-layouts: 34.1 us -> 14.7 us
  blocking collectives: 0 us -> 11.6 us
  Pallas kernels: 18.2 us -> 22.4 us
  other arithmetic: 2.94 us -> 0 us
  starting transfers between devices: 68.7 us -> 66.2 us
    unnamed x80 -> x50, local copies, waits for them, and re-layouts: 26.3 us -> 14.6 us
    all_to_all x0 -> x1, blocking collectives: none -> 11.6 us  [exchanged(): return lax.all_to_all(values, 'y', 0, 0)]
    ppermute x30 -> x31, waiting for transfers between devices: 46.6 us -> 54.9 us  [swapped(): return lax.ppermute(array, axis, [(i, i ^ distance) for i in range(parts)])]
    all_to_all x5 -> x4, waiting for transfers between devices: 15.2 us -> 8.59 us  [exchanged(): return lax.all_to_all(values, 'y', 0, 0)]
    pallas_call x8 -> x13, Pallas kernels: 18.2 us -> 22.4 us  [call(): pl.pallas_call(kernel, out_shape=[jax.ShapeDtypeStruct(shape, F32) for sh...]
    all_to_all x5 -> x4, starting transfers between devices: 20.9 us -> 16.7 us  [exchanged(): return lax.all_to_all(values, 'y', 0, 0)]
    concatenate x5 -> x0, local copies, waits for them, and re-layouts: 2.57 us -> none  [the longest x1 0.92 us: shards(): own_rows = around(jnp.concatenate([b3, v3], 0))]
    add x2 -> x0, other arithmetic: 2.24 us -> none  [the longest x1 1.36 us: shards(): keep + swapped(send, 'c', 1)]
  transfers between devices with their start and end apart: 35 -> 35, of which waited for: 19 -> 20; matrix products, arithmetic and copies ran while one was open for 5% -> 0% of each run, Pallas kernels for 3% -> 4%
where the time goes in v4:
time: 180 us; the launch traced here: 179 us
  starting transfers between devices  66.2 us (37%)
  waiting for transfers between devices  63.5 us (35%)
  Pallas kernels  22.4 us (12%)
  local copies, waits for them, and re-layouts  14.7 us (8%)
  blocking collectives  11.6 us (6%)
    ppermute x31, waiting for transfers between devices, swapped(): return lax.ppermute(array, axis, [(i, i ^ distance) for i in range(parts)])  54.9 us
    ppermute x31, starting transfers between devices, swapped(): return lax.ppermute(array, axis, [(i, i ^ distance) for i in range(parts)])  49.5 us
    pallas_call x13, Pallas kernels, call(): pl.pallas_call(kernel, out_shape=[jax.ShapeDtypeStruct(shape, F32) for sh...  22.4 us
    all_to_all x4, starting transfers between devices, exchanged(): return lax.all_to_all(values, 'y', 0, 0)  16.7 us
    unnamed x50, local copies, waits for them, and re-layouts  14.6 us
    all_to_all x1, blocking collectives, exchanged(): return lax.all_to_all(values, 'y', 0, 0)  11.6 us
    all_to_all x4, waiting for transfers between devices, exchanged(): return lax.all_to_all(values, 'y', 0, 0)  8.59 us
  transfers between devices with their start and end apart: 35, of which 20 were waited for; matrix products, arithmetic and copies ran while one was open for 0% of the time, Pallas kernels for 4%

profile of v4, /device:TPU:1, one launch (start us, length us, event | category | flops | bytes accessed | tf_op | source)
XLA Modules:
  0.0 179.3 jit_solution(7633100019060366791)
XLA Ops:
  7.9 5.0 %all-to-all-start = ((f32[4,128,256]{2,1,0:T(8,128)}), f32[4,128,256]{2,1,0:T(8,128)S(1)}, u32[]{:S(2)}, u32[]{:S(2)}) async-start(f32[4,128,256]{2,1,0:T(8,128)} %get-tuple-element.59), calls=%async_computation | async-start | bytes 1048576 | tf_op jit(solution)/shard_map/all_to_all | solution.py:316
  14.6 2.7 %collective-permute-start.2 = (f32[64,256]{1,0:T(8,128)S(1)}, f32[64,256]{1,0:T(8,128)S(1)}, u32[]{:S(2)}, u32[]{:S(2)}) collective-permute-start(f32[64,256]{1,0:T(8,128)S(1)} %get-tuple-element.56.refs_1_), channel_id=1, source_target_pairs={{0,96},{32,64},{64,32},{96,0},{1,97},{33,65},{65,33},{97,1},{2,98}... | collective-permute-start | bytes 196616 | tf_op jit(solution)/shard_map/ppermute | solution.py:308
  18.2 3.0 %collective-permute-done.2.refs_4_ = f32[64,256]{1,0:T(8,128)S(1)} collective-permute-done((f32[64,256]{1,0:T(8,128)S(1)}, f32[64,256]{1,0:T(8,128)S(1)}, u32[]{:S(2)}, u32[]{:S(2)}) %collective-permute-start.2) | collective-permute-done | bytes 65568 | tf_op jit(solution)/shard_map/ppermute | solution.py:308
  21.2 2.3 %collective-permute-done.1.refs_3_ = f32[64,256]{1,0:T(8,128)S(1)} collective-permute-done((f32[64,256]{1,0:T(8,128)S(1)}, f32[64,256]{1,0:T(8,128)S(1)}, u32[]{:S(2)}, u32[]{:S(2)}) %collective-permute-start.1) | collective-permute-done | bytes 65568 | tf_op jit(solution)/shard_map/ppermute | solution.py:308
  25.8 2.5 %collective-permute-start.14 = (f32[448,256]{1,0:T(8,128)S(1)}, f32[448,256]{1,0:T(8,128)S(1)}, u32[]{:S(2)}, u32[]{:S(2)}) collective-permute-start(f32[448,256]{1,0:T(8,128)S(1)} %get-tuple-element.66.refs_1_), channel_id=1, source_target_pairs={{0,3},{1,2},{2,1},{3,0},{4,7},{5,6},{6,5},{7,4},{8,11},{9,10},{10,... | collective-permute-start | bytes 1376264 | tf_op jit(solution)/shard_map/ppermute | solution.py:308
  28.8 3.8 %all-to-all-start.1 = ((f32[4,320,256]{2,1,0:T(8,128)}), f32[4,320,256]{2,1,0:T(8,128)S(1)}, u32[]{:S(2)}, u32[]{:S(2)}) async-start(f32[4,320,256]{2,1,0:T(8,128)} %get-tuple-element.60), calls=%async_computation.1 | async-start | bytes 2621440 | tf_op jit(solution)/shard_map/all_to_all | solution.py:316
  32.9 3.6 %collective-permute-start.11 = (f32[4,128,256]{2,1,0:T(8,128)S(1)}, f32[4,128,256]{2,1,0:T(8,128)S(1)}, u32[]{:S(2)}, u32[]{:S(2)}) collective-permute-start(f32[4,128,256]{2,1,0:T(8,128)S(1)} %all-to-all-done.refs_5_), channel_id=1, source_target_pairs={{0,4},{4,0},{1,5},{5,1},{2,6},{6,2},{3,7},{7,3},{8,12},{12,8},{9,1... | collective-permute-start | bytes 1572872 | tf_op jit(solution)/shard_map/ppermute | solution.py:308
  36.4 5.2 %collective-permute-start.4 = (f32[64,256]{1,0:T(8,128)}, f32[64,256]{1,0:T(8,128)S(1)}, u32[]{:S(2)}, u32[]{:S(2)}) collective-permute-start(f32[64,256]{1,0:T(8,128)} %copy-done.8), channel_id=1, source_target_pairs={{0,128},{128,0},{1,129},{129,1},{2,130},{130,2},{3,131},{131,3},{4... | collective-permute-start | bytes 196616 | tf_op jit(solution)/shard_map/ppermute | solution.py:308
  41.7 2.6 %collective-permute-done.4.refs_4_ = f32[64,256]{1,0:T(8,128)S(1)} collective-permute-done((f32[64,256]{1,0:T(8,128)}, f32[64,256]{1,0:T(8,128)S(1)}, u32[]{:S(2)}, u32[]{:S(2)}) %collective-permute-start.4) | collective-permute-done | bytes 65568 | tf_op jit(solution)/shard_map/ppermute | solution.py:308
  44.3 2.5 %collective-permute-start.10 = (f32[320,256]{1,0:T(8,128)S(1)}, f32[320,256]{1,0:T(8,128)S(1)}, u32[]{:S(2)}, u32[]{:S(2)}) collective-permute-start(f32[320,256]{1,0:T(8,128)S(1)} %get-tuple-element.62.refs_1_), channel_id=1, source_target_pairs={{0,3},{1,2},{2,1},{3,0},{4,7},{5,6},{6,5},{7,4},{8,11},{9,10},{10,... | collective-permute-start | bytes 983048 | tf_op jit(solution)/shard_map/ppermute | solution.py:308
  49.0 2.8 %collective-permute-start.8 = (f32[320,256]{1,0:T(8,128)S(1)}, f32[320,256]{1,0:T(8,128)S(1)}, u32[]{:S(2)}, u32[]{:S(2)}) collective-permute-start(f32[320,256]{1,0:T(8,128)S(1)} %get-tuple-element.62.refs_1_), channel_id=1, source_target_pairs={{0,1},{1,0},{2,3},{3,2},{4,5},{5,4},{6,7},{7,6},{8,9},{9,8},{10,11... | collective-permute-start | bytes 983048 | tf_op jit(solution)/shard_map/ppermute | solution.py:308
  53.9 8.0 %collective-permute-done.10.refs_4_ = f32[320,256]{1,0:T(8,128)S(1)} collective-permute-done((f32[320,256]{1,0:T(8,128)S(1)}, f32[320,256]{1,0:T(8,128)S(1)}, u32[]{:S(2)}, u32[]{:S(2)}) %collective-permute-start.10) | collective-permute-done | bytes 327712 | tf_op jit(solution)/shard_map/ppermute | solution.py:308
  61.9 1.9 %collective-permute-start.6 = (f32[64,256]{1,0:T(8,128)S(1)}, f32[64,256]{1,0:T(8,128)S(1)}, u32[]{:S(2)}, u32[]{:S(2)}) collective-permute-start(f32[64,256]{1,0:T(8,128)S(1)} %collective-permute-done.4.refs_4_), channel_id=1, source_target_pairs={{0,2},{1,3},{2,0},{3,1},{4,6},{5,7},{6,4},{7,5},{8,10},{9,11},{10,... | collective-permute-start | bytes 196616 | tf_op jit(solution)/shard_map/ppermute | solution.py:308
  63.8 2.0 %collective-permute-start.5 = (f32[64,256]{1,0:T(8,128)S(1)}, f32[64,256]{1,0:T(8,128)S(1)}, u32[]{:S(2)}, u32[]{:S(2)}) collective-permute-start(f32[64,256]{1,0:T(8,128)S(1)} %collective-permute-done.4.refs_4_), channel_id=1, source_target_pairs={{0,1},{1,0},{2,3},{3,2},{4,5},{5,4},{6,7},{7,6},{8,9},{9,8},{10,11... | collective-permute-start | bytes 196616 | tf_op jit(solution)/shard_map/ppermute | solution.py:308
  68.6 2.5 %collective-permute-start.15 = (f32[4,320,256]{2,1,0:T(8,128)S(1)}, f32[4,320,256]{2,1,0:T(8,128)S(1)}, u32[]{:S(2)}, u32[]{:S(2)}) collective-permute-start(f32[4,320,256]{2,1,0:T(8,128)S(1)} %all-to-all-done.1.refs_8_), channel_id=1, source_target_pairs={{0,4},{4,0},{1,5},{5,1},{2,6},{6,2},{3,7},{7,3},{8,12},{12,8},{9,1... | collective-permute-start | bytes 3932168 | tf_op jit(solution)/shard_map/ppermute | solution.py:308
  71.1 2.7 %collective-permute-done.15.refs_9_ = f32[4,320,256]{2,1,0:T(8,128)S(1)} collective-permute-done((f32[4,320,256]{2,1,0:T(8,128)S(1)}, f32[4,320,256]{2,1,0:T(8,128)S(1)}, u32[]{:S(2)}, u32[]{:S(2)}) %collective-permute-start.15) | collective-permute-done | bytes 1310752 | tf_op jit(solution)/shard_map/ppermute | solution.py:308
  76.1 2.6 %shard_map.157 = (f32[4,320,256]{2,1,0:T(8,128)}, f32[128,256]{1,0:T(8,128)S(1)}, f32[128,512]{1,0:T(8,128)S(1)}, f32[128,1024]{1,0:T(8,128)S(1)}, f32[1024,256]{1,0:T(8,128)S(1)}) custom-call(s32[5]{0:T(128)S(1)} %stack.23.refs_0_, s32[2,4]{1,0:T(2,128)S(1)} %copy-done.14, f32[448,1024]{1,0:T(8,128)S(1)} %copy-done.16, f32[448,1024]{1,0:T(8,128)S(1)} %copy-done.16, ...), custom_call_target="tpu_custom_call" | custom-call | flops 4400000000 | tf_op jit(solution)/shard_map/pallas_call | solution.py:101
  79.4 3.8 %all-to-all-start.2 = ((f32[4,320,256]{2,1,0:T(8,128)}), f32[4,320,256]{2,1,0:T(8,128)S(1)}, u32[]{:S(2)}, u32[]{:S(2)}) async-start(f32[4,320,256]{2,1,0:T(8,128)} %get-tuple-element.77), calls=%async_computation.2 | async-start | bytes 2621440 | tf_op jit(solution)/shard_map/all_to_all | solution.py:316
  86.5 2.3 %collective-permute-done.18.refs_4_ = f32[128,256]{1,0:T(8,128)S(1)} collective-permute-done((f32[128,256]{1,0:T(8,128)S(1)}, f32[128,256]{1,0:T(8,128)S(1)}, u32[]{:S(2)}, u32[]{:S(2)}) %collective-permute-start.18) | collective-permute-done | bytes 131104 | tf_op jit(solution)/shard_map/ppermute | solution.py:308
  96.5 2.1 %collective-permute-done.21.refs_7_ = f32[128,256]{1,0:T(8,128)S(1)} collective-permute-done((f32[128,256]{1,0:T(8,128)S(1)}, f32[128,256]{1,0:T(8,128)S(1)}, u32[]{:S(2)}, u32[]{:S(2)}) %collective-permute-start.21) | collective-permute-done | bytes 131104 | tf_op jit(solution)/shard_map/ppermute | solution.py:308
  98.5 2.0 %collective-permute-done.20.refs_6_ = f32[128,256]{1,0:T(8,128)S(1)} collective-permute-done((f32[128,256]{1,0:T(8,128)S(1)}, f32[128,256]{1,0:T(8,128)S(1)}, u32[]{:S(2)}, u32[]{:S(2)}) %collective-permute-start.20) | collective-permute-done | bytes 131104 | tf_op jit(solution)/shard_map/ppermute | solution.py:308
  100.8 3.0 %collective-permute-start.22 = (f32[4,320,256]{2,1,0:T(8,128)S(1)}, f32[4,320,256]{2,1,0:T(8,128)S(1)}, u32[]{:S(2)}, u32[]{:S(2)}) collective-permute-start(f32[4,320,256]{2,1,0:T(8,128)S(1)} %all-to-all-done.2.refs_8_), channel_id=1, source_target_pairs={{0,4},{4,0},{1,5},{5,1},{2,6},{6,2},{3,7},{7,3},{8,12},{12,8},{9,1... | collective-permute-start | bytes 3932168 | tf_op jit(solution)/shard_map/ppermute | solution.py:308
  103.8 2.7 %collective-permute-done.22.refs_9_ = f32[4,320,256]{2,1,0:T(8,128)S(1)} collective-permute-done((f32[4,320,256]{2,1,0:T(8,128)S(1)}, f32[4,320,256]{2,1,0:T(8,128)S(1)}, u32[]{:S(2)}, u32[]{:S(2)}) %collective-permute-start.22) | collective-permute-done | bytes 1310752 | tf_op jit(solution)/shard_map/ppermute | solution.py:308
  108.9 1.9 %shard_map.159 = (f32[256,256]{1,0:T(8,128)S(1)}, f32[256,1024]{1,0:T(8,128)S(1)}, f32[1536,256]{1,0:T(8,128)S(1)}, f32[256,256]{1,0:T(8,128)S(1)}, f32[256,256]{1,0:T(8,128)S(1)}) custom-call(s32[5]{0:T(128)S(1)} %stack.23.refs_0_, s32[4,8]{1,0:T(4,128)S(1)} %copy-done.13, f32[448,1024]{1,0:T(8,128)S(1)} %copy-done.17, f32[128,512]{1,0:T(8,128)S(1)} %copy-done.24, ...), custom_call_target="tpu_custom_call" | custom-call | flops 3300000000 | tf_op jit(solution)/shard_map/pallas_call | solution.py:101
  115.7 9.6 %collective-permute-done.25.refs_10_ = f32[256,256]{1,0:T(8,128)S(1)} collective-permute-done((f32[256,256]{1,0:T(8,128)S(1)}, f32[256,256]{1,0:T(8,128)S(1)}, u32[]{:S(2)}, u32[]{:S(2)}) %collective-permute-start.25) | collective-permute-done | bytes 262176 | tf_op jit(solution)/shard_map/ppermute | solution.py:308
  125.6 5.6 %shard_map.161 = (f32[4,384,256]{2,1,0:T(8,128)S(1)}, f32[4,384,256]{2,1,0:T(8,128)S(1)}) custom-call(s32[5]{0:T(128)S(1)} %stack.23.refs_0_, s32[8,12]{1,0:T(8,128)S(1)} %copy-done.12, f32[448,1024]{1,0:T(8,128)S(1)} %copy-done.18, f32[256,1024]{1,0:T(8,128)S(1)} %get-tuple-element.83.refs_5_.refs_3_, f32[1536,256]{1,0:T(8,128)S(1)} %get-tuple-element.84.refs_4_, ...), custom_call_target="tpu_custom_call" | custom-call | flops 6600000000 | tf_op jit(solution)/shard_map/pallas_call | solution.py:101
  132.8 3.0 %collective-permute-done.26.refs_1_ = f32[4,384,256]{2,1,0:T(8,128)S(1)} collective-permute-done((f32[4,384,256]{2,1,0:T(8,128)S(1)}, f32[4,384,256]{2,1,0:T(8,128)S(1)}, u32[]{:S(2)}, u32[]{:S(2)}) %collective-permute-start.26) | collective-permute-done | bytes 1572896 | tf_op jit(solution)/shard_map/ppermute | solution.py:308
  137.3 4.1 %all-to-all-start.3 = ((f32[4,384,256]{2,1,0:T(8,128)}), f32[4,384,256]{2,1,0:T(8,128)S(1)}, u32[]{:S(2)}, u32[]{:S(2)}) async-start(f32[4,384,256]{2,1,0:T(8,128)} %shard_map.162), calls=%async_computation.3 | async-start | bytes 3145728 | tf_op jit(solution)/shard_map/all_to_all | solution.py:316
  144.6 7.6 %collective-permute-done.29.refs_6_ = f32[192,256]{1,0:T(8,128)S(1)} collective-permute-done((f32[192,256]{1,0:T(8,128)S(1)}, f32[192,256]{1,0:T(8,128)S(1)}, u32[]{:S(2)}, u32[]{:S(2)}) %collective-permute-start.29) | collective-permute-done | bytes 196640 | tf_op jit(solution)/shard_map/ppermute | solution.py:308
  152.9 8.6 %all-to-all-done.3.refs_1_ = f32[4,384,256]{2,1,0:T(8,128)S(1)} async-done(((f32[4,384,256]{2,1,0:T(8,128)}), f32[4,384,256]{2,1,0:T(8,128)S(1)}, u32[]{:S(2)}, u32[]{:S(2)}) %all-to-all-start.3) | async-done | bytes 1572896 | tf_op jit(solution)/shard_map/all_to_all | solution.py:316
  161.5 2.3 %shard_map.163 = (f32[16,256]{1,0:T(8,128)}, f32[32,256]{1,0:T(8,128)}, f32[16,256]{1,0:T(8,128)}, f32[64,256]{1,0:T(8,128)}, f32[64,256]{1,0:T(8,128)}, /*index...) custom-call(s32[5]{0:T(128)S(1)} %stack.23.refs_0_, ...), custom_call_target="tpu_custom_call" | custom-call | flops 3300000000 | tf_op jit(solution)/shard_map/pallas_call | solution.py:101
  167.0 11.6 %all_to_all.25.refs_0_ = f32[4,128,256]{2,1,0:T(8,128)S(1)} all-to-all(f32[4,128,256]{2,1,0:T(8,128)S(1)} %shard_map.164), channel_id=1, replica_groups=mesh['h'=2,'q'=2,'p'=2,'y'=4,'c'=2,'x'=4] {'y'}, dimensions={0} | all-to-all | bytes 1048576 | tf_op jit(solution)/shard_map/all_to_all | solution.py:316
  (103 shorter events, 52.6 us)
Async XLA Ops:
  7.9 20.9 %all-to-all-start = ((f32[4,128,256]{2,1,0:T(8,128)}), f32[4,128,256]{2,1,0:T(8,128)S(1)}, u32[]{:S(2)}, u32[]{:S(2)}) async-start(f32[4,128,256]{2,1,0:T(8,128)} %get-tuple-element.59), calls=%async_computation | async-start | bytes 1048576 | tf_op jit(solution)/shard_map/all_to_all | solution.py:316
  12.9 10.5 %collective-permute-start.3 = (f32[128,256]{1,0:T(8,128)S(1)}, f32[128,256]{1,0:T(8,128)S(1)}, u32[]{:S(2)}, u32[]{:S(2)}) collective-permute-start(f32[128,256]{1,0:T(8,128)S(1)} %get-tuple-element.57.refs_5_), channel_id=1, source_target_pairs={{0,32},{32,0},{1,33},{33,1},{2,34},{34,2},{3,35},{35,3},{4,36},{36... | collective-permute-start | bytes 393224 | tf_op jit(solution)/shard_map/ppermute | solution.py:308
  14.6 6.6 %collective-permute-start.2 = (f32[64,256]{1,0:T(8,128)S(1)}, f32[64,256]{1,0:T(8,128)S(1)}, u32[]{:S(2)}, u32[]{:S(2)}) collective-permute-start(f32[64,256]{1,0:T(8,128)S(1)} %get-tuple-element.56.refs_1_), channel_id=1, source_target_pairs={{0,96},{32,64},{64,32},{96,0},{1,97},{33,65},{65,33},{97,1},{2,98}... | collective-permute-start | bytes 196616 | tf_op jit(solution)/shard_map/ppermute | solution.py:308
  17.3 6.1 %collective-permute-start.1 = (f32[64,256]{1,0:T(8,128)S(1)}, f32[64,256]{1,0:T(8,128)S(1)}, u32[]{:S(2)}, u32[]{:S(2)}) collective-permute-start(f32[64,256]{1,0:T(8,128)S(1)} %get-tuple-element.56.refs_1_), channel_id=1, source_target_pairs={{0,64},{32,96},{64,0},{96,32},{1,65},{33,97},{65,1},{97,33},{2,66}... | collective-permute-start | bytes 196616 | tf_op jit(solution)/shard_map/ppermute | solution.py:308
  17.6 5.9 %collective-permute-start = (f32[64,256]{1,0:T(8,128)S(1)}, f32[64,256]{1,0:T(8,128)S(1)}, u32[]{:S(2)}, u32[]{:S(2)}) collective-permute-start(f32[64,256]{1,0:T(8,128)S(1)} %get-tuple-element.56.refs_1_), channel_id=1, source_target_pairs={{0,32},{32,0},{64,96},{96,64},{1,33},{33,1},{65,97},{97,65},{2,34}... | collective-permute-start | bytes 196616 | tf_op jit(solution)/shard_map/ppermute | solution.py:308
  25.8 22.0 %collective-permute-start.14 = (f32[448,256]{1,0:T(8,128)S(1)}, f32[448,256]{1,0:T(8,128)S(1)}, u32[]{:S(2)}, u32[]{:S(2)}) collective-permute-start(f32[448,256]{1,0:T(8,128)S(1)} %get-tuple-element.66.refs_1_), channel_id=1, source_target_pairs={{0,3},{1,2},{2,1},{3,0},{4,7},{5,6},{6,5},{7,4},{8,11},{9,10},{10,... | collective-permute-start | bytes 1376264 | tf_op jit(solution)/shard_map/ppermute | solution.py:308
  28.3 20.7 %collective-permute-start.13 = (f32[448,256]{1,0:T(8,128)S(1)}, f32[448,256]{1,0:T(8,128)S(1)}, u32[]{:S(2)}, u32[]{:S(2)}) collective-permute-start(f32[448,256]{1,0:T(8,128)S(1)} %get-tuple-element.66.refs_1_), channel_id=1, source_target_pairs={{0,2},{1,3},{2,0},{3,1},{4,6},{5,7},{6,4},{7,5},{8,10},{9,11},{10,... | collective-permute-start | bytes 1376264 | tf_op jit(solution)/shard_map/ppermute | solution.py:308
  28.8 39.7 %all-to-all-start.1 = ((f32[4,320,256]{2,1,0:T(8,128)}), f32[4,320,256]{2,1,0:T(8,128)S(1)}, u32[]{:S(2)}, u32[]{:S(2)}) async-start(f32[4,320,256]{2,1,0:T(8,128)} %get-tuple-element.60), calls=%async_computation.1 | async-start | bytes 2621440 | tf_op jit(solution)/shard_map/all_to_all | solution.py:316
  32.6 19.2 %collective-permute-start.12 = (f32[448,256]{1,0:T(8,128)S(1)}, f32[448,256]{1,0:T(8,128)S(1)}, u32[]{:S(2)}, u32[]{:S(2)}) collective-permute-start(f32[448,256]{1,0:T(8,128)S(1)} %get-tuple-element.66.refs_1_), channel_id=1, source_target_pairs={{0,1},{1,0},{2,3},{3,2},{4,5},{5,4},{6,7},{7,6},{8,9},{9,8},{10,11... | collective-permute-start | bytes 1376264 | tf_op jit(solution)/shard_map/ppermute | solution.py:308
  32.9 33.0 %collective-permute-start.11 = (f32[4,128,256]{2,1,0:T(8,128)S(1)}, f32[4,128,256]{2,1,0:T(8,128)S(1)}, u32[]{:S(2)}, u32[]{:S(2)}) collective-permute-start(f32[4,128,256]{2,1,0:T(8,128)S(1)} %all-to-all-done.refs_5_), channel_id=1, source_target_pairs={{0,4},{4,0},{1,5},{5,1},{2,6},{6,2},{3,7},{7,3},{8,12},{12,8},{9,1... | collective-permute-start | bytes 1572872 | tf_op jit(solution)/shard_map/ppermute | solution.py:308
  36.4 7.8 %collective-permute-start.4 = (f32[64,256]{1,0:T(8,128)}, f32[64,256]{1,0:T(8,128)S(1)}, u32[]{:S(2)}, u32[]{:S(2)}) collective-permute-start(f32[64,256]{1,0:T(8,128)} %copy-done.8), channel_id=1, source_target_pairs={{0,128},{128,0},{1,129},{129,1},{2,130},{130,2},{3,131},{131,3},{4... | collective-permute-start | bytes 196616 | tf_op jit(solution)/shard_map/ppermute | solution.py:308
  44.3 17.7 %collective-permute-start.10 = (f32[320,256]{1,0:T(8,128)S(1)}, f32[320,256]{1,0:T(8,128)S(1)}, u32[]{:S(2)}, u32[]{:S(2)}) collective-permute-start(f32[320,256]{1,0:T(8,128)S(1)} %get-tuple-element.62.refs_1_), channel_id=1, source_target_pairs={{0,3},{1,2},{2,1},{3,0},{4,7},{5,6},{6,5},{7,4},{8,11},{9,10},{10,... | collective-permute-start | bytes 983048 | tf_op jit(solution)/shard_map/ppermute | solution.py:308
  47.8 16.0 %collective-permute-start.9 = (f32[320,256]{1,0:T(8,128)S(1)}, f32[320,256]{1,0:T(8,128)S(1)}, u32[]{:S(2)}, u32[]{:S(2)}) collective-permute-start(f32[320,256]{1,0:T(8,128)S(1)} %get-tuple-element.62.refs_1_), channel_id=1, source_target_pairs={{0,2},{1,3},{2,0},{3,1},{4,6},{5,7},{6,4},{7,5},{8,10},{9,11},{10,... | collective-permute-start | bytes 983048 | tf_op jit(solution)/shard_map/ppermute | solution.py:308
  49.0 16.8 %collective-permute-start.8 = (f32[320,256]{1,0:T(8,128)S(1)}, f32[320,256]{1,0:T(8,128)S(1)}, u32[]{:S(2)}, u32[]{:S(2)}) collective-permute-start(f32[320,256]{1,0:T(8,128)S(1)} %get-tuple-element.62.refs_1_), channel_id=1, source_target_pairs={{0,1},{1,0},{2,3},{3,2},{4,5},{5,4},{6,7},{7,6},{8,9},{9,8},{10,11... | collective-permute-start | bytes 983048 | tf_op jit(solution)/shard_map/ppermute | solution.py:308
  51.8 16.1 %collective-permute-start.7 = (f32[64,256]{1,0:T(8,128)S(1)}, f32[64,256]{1,0:T(8,128)S(1)}, u32[]{:S(2)}, u32[]{:S(2)}) collective-permute-start(f32[64,256]{1,0:T(8,128)S(1)} %collective-permute-done.4.refs_4_), channel_id=1, source_target_pairs={{0,3},{1,2},{2,1},{3,0},{4,7},{5,6},{6,5},{7,4},{8,11},{9,10},{10,... | collective-permute-start | bytes 196616 | tf_op jit(solution)/shard_map/ppermute | solution.py:308
  61.9 6.6 %collective-permute-start.6 = (f32[64,256]{1,0:T(8,128)S(1)}, f32[64,256]{1,0:T(8,128)S(1)}, u32[]{:S(2)}, u32[]{:S(2)}) collective-permute-start(f32[64,256]{1,0:T(8,128)S(1)} %collective-permute-done.4.refs_4_), channel_id=1, source_target_pairs={{0,2},{1,3},{2,0},{3,1},{4,6},{5,7},{6,4},{7,5},{8,10},{9,11},{10,... | collective-permute-start | bytes 196616 | tf_op jit(solution)/shard_map/ppermute | solution.py:308
  68.6 5.2 %collective-permute-start.15 = (f32[4,320,256]{2,1,0:T(8,128)S(1)}, f32[4,320,256]{2,1,0:T(8,128)S(1)}, u32[]{:S(2)}, u32[]{:S(2)}) collective-permute-start(f32[4,320,256]{2,1,0:T(8,128)S(1)} %all-to-all-done.1.refs_8_), channel_id=1, source_target_pairs={{0,4},{4,0},{1,5},{5,1},{2,6},{6,2},{3,7},{7,3},{8,12},{12,8},{9,1... | collective-permute-start | bytes 3932168 | tf_op jit(solution)/shard_map/ppermute | solution.py:308
  79.4 21.4 %all-to-all-start.2 = ((f32[4,320,256]{2,1,0:T(8,128)}), f32[4,320,256]{2,1,0:T(8,128)S(1)}, u32[]{:S(2)}, u32[]{:S(2)}) async-start(f32[4,320,256]{2,1,0:T(8,128)} %get-tuple-element.77), calls=%async_computation.2 | async-start | bytes 2621440 | tf_op jit(solution)/shard_map/all_to_all | solution.py:316
  83.3 5.6 %collective-permute-start.18 = (f32[128,256]{1,0:T(8,128)S(1)}, f32[128,256]{1,0:T(8,128)S(1)}, u32[]{:S(2)}, u32[]{:S(2)}) collective-permute-start(f32[128,256]{1,0:T(8,128)S(1)} %get-tuple-element.75.refs_1_), channel_id=1, source_target_pairs={{0,3},{1,2},{2,1},{3,0},{4,7},{5,6},{6,5},{7,4},{8,11},{9,10},{10,... | collective-permute-start | bytes 393224 | tf_op jit(solution)/shard_map/ppermute | solution.py:308
  85.0 5.4 %collective-permute-start.17 = (f32[128,256]{1,0:T(8,128)S(1)}, f32[128,256]{1,0:T(8,128)S(1)}, u32[]{:S(2)}, u32[]{:S(2)}) collective-permute-start(f32[128,256]{1,0:T(8,128)S(1)} %get-tuple-element.75.refs_1_), channel_id=1, source_target_pairs={{0,2},{1,3},{2,0},{3,1},{4,6},{5,7},{6,4},{7,5},{8,10},{9,11},{10,... | collective-permute-start | bytes 393224 | tf_op jit(solution)/shard_map/ppermute | solution.py:308
  86.1 5.9 %collective-permute-start.16 = (f32[128,256]{1,0:T(8,128)S(1)}, f32[128,256]{1,0:T(8,128)S(1)}, u32[]{:S(2)}, u32[]{:S(2)}) collective-permute-start(f32[128,256]{1,0:T(8,128)S(1)} %get-tuple-element.75.refs_1_), channel_id=1, source_target_pairs={{0,1},{1,0},{2,3},{3,2},{4,5},{5,4},{6,7},{7,6},{8,9},{9,8},{10,11... | collective-permute-start | bytes 393224 | tf_op jit(solution)/shard_map/ppermute | solution.py:308
  93.1 5.4 %collective-permute-start.21 = (f32[128,256]{1,0:T(8,128)S(1)}, f32[128,256]{1,0:T(8,128)S(1)}, u32[]{:S(2)}, u32[]{:S(2)}) collective-permute-start(f32[128,256]{1,0:T(8,128)S(1)} %shard_map.158.refs_4_), channel_id=1, source_target_pairs={{0,3},{1,2},{2,1},{3,0},{4,7},{5,6},{6,5},{7,4},{8,11},{9,10},{10,... | collective-permute-start | bytes 393224 | tf_op jit(solution)/shard_map/ppermute | solution.py:308
  94.9 5.6 %collective-permute-start.20 = (f32[128,256]{1,0:T(8,128)S(1)}, f32[128,256]{1,0:T(8,128)S(1)}, u32[]{:S(2)}, u32[]{:S(2)}) collective-permute-start(f32[128,256]{1,0:T(8,128)S(1)} %shard_map.158.refs_4_), channel_id=1, source_target_pairs={{0,2},{1,3},{2,0},{3,1},{4,6},{5,7},{6,4},{7,5},{8,10},{9,11},{10,... | collective-permute-start | bytes 393224 | tf_op jit(solution)/shard_map/ppermute | solution.py:308
  95.9 4.8 %collective-permute-start.19 = (f32[128,256]{1,0:T(8,128)S(1)}, f32[128,256]{1,0:T(8,128)S(1)}, u32[]{:S(2)}, u32[]{:S(2)}) collective-permute-start(f32[128,256]{1,0:T(8,128)S(1)} %shard_map.158.refs_4_), channel_id=1, source_target_pairs={{0,1},{1,0},{2,3},{3,2},{4,5},{5,4},{6,7},{7,6},{8,9},{9,8},{10,11... | collective-permute-start | bytes 393224 | tf_op jit(solution)/shard_map/ppermute | solution.py:308
  100.8 5.6 %collective-permute-start.22 = (f32[4,320,256]{2,1,0:T(8,128)S(1)}, f32[4,320,256]{2,1,0:T(8,128)S(1)}, u32[]{:S(2)}, u32[]{:S(2)}) collective-permute-start(f32[4,320,256]{2,1,0:T(8,128)S(1)} %all-to-all-done.2.refs_8_), channel_id=1, source_target_pairs={{0,4},{4,0},{1,5},{5,1},{2,6},{6,2},{3,7},{7,3},{8,12},{12,8},{9,1... | collective-permute-start | bytes 3932168 | tf_op jit(solution)/shard_map/ppermute | solution.py:308
  110.8 14.4 %collective-permute-start.25 = (f32[256,256]{1,0:T(8,128)S(1)}, f32[256,256]{1,0:T(8,128)S(1)}, u32[]{:S(2)}, u32[]{:S(2)}) collective-permute-start(f32[256,256]{1,0:T(8,128)S(1)} %get-tuple-element.88.refs_6_.refs_7_), channel_id=1, source_target_pairs={{0,3},{1,2},{2,1},{3,0},{4,7},{5,6},{6,5},{7,4},{8,11},{9,10},{10,... | collective-permute-start | bytes 786440 | tf_op jit(solution)/shard_map/ppermute | solution.py:308
  112.5 12.7 %collective-permute-start.24 = (f32[256,256]{1,0:T(8,128)S(1)}, f32[256,256]{1,0:T(8,128)S(1)}, u32[]{:S(2)}, u32[]{:S(2)}) collective-permute-start(f32[256,256]{1,0:T(8,128)S(1)} %get-tuple-element.88.refs_6_.refs_7_), channel_id=1, source_target_pairs={{0,2},{1,3},{2,0},{3,1},{4,6},{5,7},{6,4},{7,5},{8,10},{9,11},{10,... | collective-permute-start | bytes 786440 | tf_op jit(solution)/shard_map/ppermute | solution.py:308
  113.6 12.0 %collective-permute-start.23 = (f32[256,256]{1,0:T(8,128)S(1)}, f32[256,256]{1,0:T(8,128)S(1)}, u32[]{:S(2)}, u32[]{:S(2)}) collective-permute-start(f32[256,256]{1,0:T(8,128)S(1)} %get-tuple-element.88.refs_6_.refs_7_), channel_id=1, source_target_pairs={{0,1},{1,0},{2,3},{3,2},{4,5},{5,4},{6,7},{7,6},{8,9},{9,8},{10,11... | collective-permute-start | bytes 786440 | tf_op jit(solution)/shard_map/ppermute | solution.py:308
  137.3 24.2 %all-to-all-start.3 = ((f32[4,384,256]{2,1,0:T(8,128)}), f32[4,384,256]{2,1,0:T(8,128)S(1)}, u32[]{:S(2)}, u32[]{:S(2)}) async-start(f32[4,384,256]{2,1,0:T(8,128)} %shard_map.162), calls=%async_computation.3 | async-start | bytes 3145728 | tf_op jit(solution)/shard_map/all_to_all | solution.py:316
  141.3 10.9 %collective-permute-start.29 = (f32[192,256]{1,0:T(8,128)S(1)}, f32[192,256]{1,0:T(8,128)S(1)}, u32[]{:S(2)}, u32[]{:S(2)}) collective-permute-start(f32[192,256]{1,0:T(8,128)S(1)} %get-tuple-element.96.refs_10_.refs_3_), channel_id=1, source_target_pairs={{0,3},{1,2},{2,1},{3,0},{4,7},{5,6},{6,5},{7,4},{8,11},{9,10},{10,... | collective-permute-start | bytes 589832 | tf_op jit(solution)/shard_map/ppermute | solution.py:308
  143.0 9.2 %collective-permute-start.28 = (f32[192,256]{1,0:T(8,128)S(1)}, f32[192,256]{1,0:T(8,128)S(1)}, u32[]{:S(2)}, u32[]{:S(2)}) collective-permute-start(f32[192,256]{1,0:T(8,128)S(1)} %get-tuple-element.96.refs_10_.refs_3_), channel_id=1, source_target_pairs={{0,2},{1,3},{2,0},{3,1},{4,6},{5,7},{6,4},{7,5},{8,10},{9,11},{10,... | collective-permute-start | bytes 589832 | tf_op jit(solution)/shard_map/ppermute | solution.py:308
  144.1 8.8 %collective-permute-start.27 = (f32[192,256]{1,0:T(8,128)S(1)}, f32[192,256]{1,0:T(8,128)S(1)}, u32[]{:S(2)}, u32[]{:S(2)}) collective-permute-start(f32[192,256]{1,0:T(8,128)S(1)} %get-tuple-element.96.refs_10_.refs_3_), channel_id=1, source_target_pairs={{0,1},{1,0},{2,3},{3,2},{4,5},{5,4},{6,7},{7,6},{8,9},{9,8},{10,11... | collective-permute-start | bytes 589832 | tf_op jit(solution)/shard_map/ppermute | solution.py:308
  (28 other events, 145.0 us)

commit v5 on v4

--- a/solution.py
+++ b/solution.py
@@ -108,7 +108,7 @@
         cost_estimate=pl.CostEstimate(
             flops=micros * 1_100_000_000, bytes_accessed=0, transcendentals=0
         ),
-        compiler_params=pltpu.CompilerParams(vmem_limit_bytes=28 * 1024 * 1024),
+        compiler_params=pltpu.CompilerParams(vmem_limit_bytes=(60 if body in (pack,) else 28) * 1024 * 1024),
     )(*values)
 
 
@@ -339,7 +339,6 @@
     )
     ancestors = around(own_1, ("q", "p"))
     pair_2 = swapped(own_2, "p", 1)
-    own_rows = around(own_3)
     columns_3 = exchanged(columns_3)
     early, rows, row_0 = call(
         place_ancestors,
@@ -349,6 +348,8 @@
         ids, *ancestors, own_2, pair_2,
     )
     early, columns_3 = lax.optimization_barrier((early, columns_3))
+    own_rows = around(own_3)
+    own_rows, rows = lax.optimization_barrier((own_rows, rows))
     early = exchanged(early)
     row_0 = around(swapped(row_0, "h", 1))
     w3, v3_rows = call(

time: 180 us -> 171 us (0.950)
  local copies, waits for them, and re-layouts: 14.7 us -> 8.93 us
  starting transfers between devices: 66.2 us -> 62.7 us
    unnamed x50 -> x36, local copies, waits for them, and re-layouts: 14.6 us -> 8.84 us
    ppermute x31, starting transfers between devices: 49.5 us -> 46.5 us  [swapped(): return lax.ppermute(array, axis, [(i, i ^ distance) for i in range(parts)])]
  transfers between devices with their start and end apart: 35 -> 35, of which waited for: 20 -> 19; matrix products, arithmetic and copies ran while one was open for 0% -> 0% of each run, Pallas kernels for 4% -> 4%
where the time goes in v5:
time: 171 us; the launch traced here: 170 us
  waiting for transfers between devices  63.1 us (37%)
  starting transfers between devices  62.7 us (37%)
  Pallas kernels  23 us (13%)
  blocking collectives  11.6 us (7%)
  local copies, waits for them, and re-layouts  8.93 us (5%)
    ppermute x31, waiting for transfers between devices, swapped(): return lax.ppermute(array, axis, [(i, i ^ distance) for i in range(parts)])  54.6 us
    ppermute x31, starting transfers between devices, swapped(): return lax.ppermute(array, axis, [(i, i ^ distance) for i in range(parts)])  46.5 us
    pallas_call x13, Pallas kernels, call(): pl.pallas_call(kernel, out_shape=[jax.ShapeDtypeStruct(shape, F32) for sh...  23 us
    all_to_all x4, starting transfers between devices, exchanged(): return lax.all_to_all(values, 'y', 0, 0)  16.2 us
    all_to_all x1, blocking collectives, exchanged(): return lax.all_to_all(values, 'y', 0, 0)  11.6 us
    unnamed x36, local copies, waits for them, and re-layouts  8.84 us
    all_to_all x4, waiting for transfers between devices, exchanged(): return lax.all_to_all(values, 'y', 0, 0)  8.58 us
  transfers between devices with their start and end apart: 35, of which 19 were waited for; matrix products, arithmetic and copies ran while one was open for 0% of the time, Pallas kernels for 4%

profile of v5, /device:TPU:1, one launch (start us, length us, event | category | flops | bytes accessed | tf_op | source)
XLA Modules:
  0.0 170.3 jit_solution(12542750717421202577)
XLA Ops:
  0.6 2.2 %shard_map.153 = (f32[64,256]{1,0:T(8,128)}, f32[128,256]{1,0:T(8,128)}, f32[320,256]{1,0:T(8,128)}, f32[4,128,256]{2,1,0:T(8,128)}) custom-call(f32[16,256]{1,0:T(8,128)} %refs_0_.1, f32[32,256]{1,0:T(8,128)} %refs_1_.4, f32[16,256]{1,0:T(8,128)} %refs_2_.1, f32[64,256]{1,0:T(8,128)} %refs_3_.1, f32[64,256]{1,0:T(8,128)} %refs_4_.1, f32[128,256]{1,0:T(8,128)} %refs_5_.1, ...), custom_call_target="tpu_custom_call" | custom-call | flops 1100000000 | tf_op jit(solution)/shard_map/pallas_call | solution.py:101
  2.8 5.0 %all-to-all-start = ((f32[4,128,256]{2,1,0:T(8,128)}), f32[4,128,256]{2,1,0:T(8,128)S(1)}, u32[]{:S(2)}, u32[]{:S(2)}) async-start(f32[4,128,256]{2,1,0:T(8,128)} %get-tuple-element.64), calls=%async_computation | async-start | bytes 1048576 | tf_op jit(solution)/shard_map/all_to_all | solution.py:316
  9.5 2.7 %collective-permute-start.2 = (f32[64,256]{1,0:T(8,128)}, f32[64,256]{1,0:T(8,128)S(1)}, u32[]{:S(2)}, u32[]{:S(2)}) collective-permute-start(f32[64,256]{1,0:T(8,128)} %get-tuple-element.61.refs_1_), channel_id=1, source_target_pairs={{0,96},{32,64},{64,32},{96,0},{1,97},{33,65},{65,33},{97,1},{2,98}... | collective-permute-start | bytes 196616 | tf_op jit(solution)/shard_map/ppermute | solution.py:308
  13.0 2.5 %collective-permute-start.10 = (f32[320,256]{1,0:T(8,128)}, f32[320,256]{1,0:T(8,128)S(1)}, u32[]{:S(2)}, u32[]{:S(2)}) collective-permute-start(f32[320,256]{1,0:T(8,128)} %get-tuple-element.69.refs_1_), channel_id=1, source_target_pairs={{0,3},{1,2},{2,1},{3,0},{4,7},{5,6},{6,5},{7,4},{8,11},{9,10},{10,... | collective-permute-start | bytes 983048 | tf_op jit(solution)/shard_map/ppermute | solution.py:308
  16.6 2.7 %collective-permute-start.9 = (f32[320,256]{1,0:T(8,128)}, f32[320,256]{1,0:T(8,128)S(1)}, u32[]{:S(2)}, u32[]{:S(2)}) collective-permute-start(f32[320,256]{1,0:T(8,128)} %get-tuple-element.69.refs_1_), channel_id=1, source_target_pairs={{0,2},{1,3},{2,0},{3,1},{4,6},{5,7},{6,4},{7,5},{8,10},{9,11},{10,... | collective-permute-start | bytes 983048 | tf_op jit(solution)/shard_map/ppermute | solution.py:308
  23.2 3.8 %all-to-all-start.1 = ((f32[4,320,256]{2,1,0:T(8,128)}), f32[4,320,256]{2,1,0:T(8,128)S(1)}, u32[]{:S(2)}, u32[]{:S(2)}) async-start(f32[4,320,256]{2,1,0:T(8,128)} %get-tuple-element.65), calls=%async_computation.1 | async-start | bytes 2621440 | tf_op jit(solution)/shard_map/all_to_all | solution.py:316
  27.0 4.6 %collective-permute-done.8.refs_2_ = f32[320,256]{1,0:T(8,128)S(1)} collective-permute-done((f32[320,256]{1,0:T(8,128)}, f32[320,256]{1,0:T(8,128)S(1)}, u32[]{:S(2)}, u32[]{:S(2)}) %collective-permute-start.8) | collective-permute-done | bytes 327712 | tf_op jit(solution)/shard_map/ppermute | solution.py:308
  31.9 2.7 %collective-permute-start.13 = (f32[448,256]{1,0:T(8,128)S(1)}, f32[448,256]{1,0:T(8,128)S(1)}, u32[]{:S(2)}, u32[]{:S(2)}) collective-permute-start(f32[448,256]{1,0:T(8,128)S(1)} %get-tuple-element.76.refs_1_), channel_id=1, source_target_pairs={{0,2},{1,3},{2,0},{3,1},{4,6},{5,7},{6,4},{7,5},{8,10},{9,11},{10,... | collective-permute-start | bytes 1376264 | tf_op jit(solution)/shard_map/ppermute | solution.py:308
  34.9 4.7 %collective-permute-start.11 = (f32[4,128,256]{2,1,0:T(8,128)S(1)}, f32[4,128,256]{2,1,0:T(8,128)S(1)}, u32[]{:S(2)}, u32[]{:S(2)}) collective-permute-start(f32[4,128,256]{2,1,0:T(8,128)S(1)} %all-to-all-done.refs_5_), channel_id=1, source_target_pairs={{0,4},{4,0},{1,5},{5,1},{2,6},{6,2},{3,7},{7,3},{8,12},{12,8},{9,1... | collective-permute-start | bytes 1572872 | tf_op jit(solution)/shard_map/ppermute | solution.py:308
  39.7 4.7 %collective-permute-start.4 = (f32[64,256]{1,0:T(8,128)S(1)}, f32[64,256]{1,0:T(8,128)S(1)}, u32[]{:S(2)}, u32[]{:S(2)}) collective-permute-start(f32[64,256]{1,0:T(8,128)S(1)} %get-tuple-element.66), channel_id=1, source_target_pairs={{0,128},{128,0},{1,129},{129,1},{2,130},{130,2},{3,131},{131,3},{4... | collective-permute-start | bytes 196616 | tf_op jit(solution)/shard_map/ppermute | solution.py:308
  44.4 2.9 %collective-permute-done.4.refs_4_ = f32[64,256]{1,0:T(8,128)S(1)} collective-permute-done((f32[64,256]{1,0:T(8,128)S(1)}, f32[64,256]{1,0:T(8,128)S(1)}, u32[]{:S(2)}, u32[]{:S(2)}) %collective-permute-start.4) | collective-permute-done | bytes 65568 | tf_op jit(solution)/shard_map/ppermute | solution.py:308
  47.5 7.1 %collective-permute-done.14.refs_4_ = f32[448,256]{1,0:T(8,128)S(1)} collective-permute-done((f32[448,256]{1,0:T(8,128)S(1)}, f32[448,256]{1,0:T(8,128)S(1)}, u32[]{:S(2)}, u32[]{:S(2)}) %collective-permute-start.14) | collective-permute-done | bytes 458784 | tf_op jit(solution)/shard_map/ppermute | solution.py:308
  59.2 2.9 %collective-permute-start.15 = (f32[4,320,256]{2,1,0:T(8,128)S(1)}, f32[4,320,256]{2,1,0:T(8,128)S(1)}, u32[]{:S(2)}, u32[]{:S(2)}) collective-permute-start(f32[4,320,256]{2,1,0:T(8,128)S(1)} %all-to-all-done.1.refs_8_), channel_id=1, source_target_pairs={{0,4},{4,0},{1,5},{5,1},{2,6},{6,2},{3,7},{7,3},{8,12},{12,8},{9,1... | collective-permute-start | bytes 3932168 | tf_op jit(solution)/shard_map/ppermute | solution.py:308
  62.1 2.7 %collective-permute-done.15.refs_9_ = f32[4,320,256]{2,1,0:T(8,128)S(1)} collective-permute-done((f32[4,320,256]{2,1,0:T(8,128)S(1)}, f32[4,320,256]{2,1,0:T(8,128)S(1)}, u32[]{:S(2)}, u32[]{:S(2)}) %collective-permute-start.15) | collective-permute-done | bytes 1310752 | tf_op jit(solution)/shard_map/ppermute | solution.py:308
  66.3 2.6 %shard_map.157 = (f32[4,320,256]{2,1,0:T(8,128)}, f32[128,256]{1,0:T(8,128)S(1)}, f32[128,512]{1,0:T(8,128)S(1)}, f32[128,1024]{1,0:T(8,128)S(1)}, f32[1024,256]{1,0:T(8,128)S(1)}) custom-call(s32[5]{0:T(128)S(1)} %stack.23.refs_0_, s32[2,4]{1,0:T(2,128)S(1)} %copy-done.5, f32[448,1024]{1,0:T(8,128)S(1)} %copy-done.7, f32[448,1024]{1,0:T(8,128)S(1)} %copy-done.7, ...), custom_call_target="tpu_custom_call" | custom-call | flops 4400000000 | tf_op jit(solution)/shard_map/pallas_call | solution.py:101
  69.6 3.5 %all-to-all-start.2 = ((f32[4,320,256]{2,1,0:T(8,128)}), f32[4,320,256]{2,1,0:T(8,128)S(1)}, u32[]{:S(2)}, u32[]{:S(2)}) async-start(f32[4,320,256]{2,1,0:T(8,128)} %get-tuple-element.87), calls=%async_computation.2 | async-start | bytes 2621440 | tf_op jit(solution)/shard_map/all_to_all | solution.py:316
  73.2 2.4 %collective-permute-start.18 = (f32[128,256]{1,0:T(8,128)S(1)}, f32[128,256]{1,0:T(8,128)S(1)}, u32[]{:S(2)}, u32[]{:S(2)}) collective-permute-start(f32[128,256]{1,0:T(8,128)S(1)} %get-tuple-element.85.refs_1_), channel_id=1, source_target_pairs={{0,3},{1,2},{2,1},{3,0},{4,7},{5,6},{6,5},{7,4},{8,11},{9,10},{10,... | collective-permute-start | bytes 393224 | tf_op jit(solution)/shard_map/ppermute | solution.py:308
  76.5 4.2 %collective-permute-done.18.refs_4_ = f32[128,256]{1,0:T(8,128)S(1)} collective-permute-done((f32[128,256]{1,0:T(8,128)S(1)}, f32[128,256]{1,0:T(8,128)S(1)}, u32[]{:S(2)}, u32[]{:S(2)}) %collective-permute-start.18) | collective-permute-done | bytes 131104 | tf_op jit(solution)/shard_map/ppermute | solution.py:308
  84.7 2.4 %collective-permute-start.21 = (f32[128,256]{1,0:T(8,128)S(1)}, f32[128,256]{1,0:T(8,128)S(1)}, u32[]{:S(2)}, u32[]{:S(2)}) collective-permute-start(f32[128,256]{1,0:T(8,128)S(1)} %shard_map.158.refs_4_), channel_id=1, source_target_pairs={{0,3},{1,2},{2,1},{3,0},{4,7},{5,6},{6,5},{7,4},{8,11},{9,10},{10,... | collective-permute-start | bytes 393224 | tf_op jit(solution)/shard_map/ppermute | solution.py:308
  88.0 2.8 %collective-permute-done.21.refs_7_ = f32[128,256]{1,0:T(8,128)S(1)} collective-permute-done((f32[128,256]{1,0:T(8,128)S(1)}, f32[128,256]{1,0:T(8,128)S(1)}, u32[]{:S(2)}, u32[]{:S(2)}) %collective-permute-start.21) | collective-permute-done | bytes 131104 | tf_op jit(solution)/shard_map/ppermute | solution.py:308
  92.5 3.4 %collective-permute-start.22 = (f32[4,320,256]{2,1,0:T(8,128)S(1)}, f32[4,320,256]{2,1,0:T(8,128)S(1)}, u32[]{:S(2)}, u32[]{:S(2)}) collective-permute-start(f32[4,320,256]{2,1,0:T(8,128)S(1)} %all-to-all-done.2.refs_8_), channel_id=1, source_target_pairs={{0,4},{4,0},{1,5},{5,1},{2,6},{6,2},{3,7},{7,3},{8,12},{12,8},{9,1... | collective-permute-start | bytes 3932168 | tf_op jit(solution)/shard_map/ppermute | solution.py:308
  95.9 2.7 %collective-permute-done.22.refs_9_ = f32[4,320,256]{2,1,0:T(8,128)S(1)} collective-permute-done((f32[4,320,256]{2,1,0:T(8,128)S(1)}, f32[4,320,256]{2,1,0:T(8,128)S(1)}, u32[]{:S(2)}, u32[]{:S(2)}) %collective-permute-start.22) | collective-permute-done | bytes 1310752 | tf_op jit(solution)/shard_map/ppermute | solution.py:308
  100.1 1.9 %shard_map.159 = (f32[256,256]{1,0:T(8,128)S(1)}, f32[256,1024]{1,0:T(8,128)S(1)}, f32[1536,256]{1,0:T(8,128)S(1)}, f32[256,256]{1,0:T(8,128)S(1)}, f32[256,256]{1,0:T(8,128)S(1)}) custom-call(s32[5]{0:T(128)S(1)} %stack.23.refs_0_, s32[4,8]{1,0:T(4,128)S(1)} %copy-done.4, f32[448,1024]{1,0:T(8,128)S(1)} %copy-done.8, f32[128,512]{1,0:T(8,128)S(1)} %copy-done.17, ...), custom_call_target="tpu_custom_call" | custom-call | flops 3300000000 | tf_op jit(solution)/shard_map/pallas_call | solution.py:101
  102.0 1.8 %collective-permute-start.25 = (f32[256,256]{1,0:T(8,128)S(1)}, f32[256,256]{1,0:T(8,128)S(1)}, u32[]{:S(2)}, u32[]{:S(2)}) collective-permute-start(f32[256,256]{1,0:T(8,128)S(1)} %get-tuple-element.98.refs_6_.refs_7_), channel_id=1, source_target_pairs={{0,3},{1,2},{2,1},{3,0},{4,7},{5,6},{6,5},{7,4},{8,11},{9,10},{10,... | collective-permute-start | bytes 786440 | tf_op jit(solution)/shard_map/ppermute | solution.py:308
  106.9 9.6 %collective-permute-done.25.refs_10_ = f32[256,256]{1,0:T(8,128)S(1)} collective-permute-done((f32[256,256]{1,0:T(8,128)S(1)}, f32[256,256]{1,0:T(8,128)S(1)}, u32[]{:S(2)}, u32[]{:S(2)}) %collective-permute-start.25) | collective-permute-done | bytes 262176 | tf_op jit(solution)/shard_map/ppermute | solution.py:308
  116.8 5.6 %shard_map.161 = (f32[4,384,256]{2,1,0:T(8,128)S(1)}, f32[4,384,256]{2,1,0:T(8,128)S(1)}) custom-call(s32[5]{0:T(128)S(1)} %stack.23.refs_0_, s32[8,12]{1,0:T(8,128)S(1)} %copy-done.3, f32[448,1024]{1,0:T(8,128)S(1)} %copy-done.9, f32[256,1024]{1,0:T(8,128)S(1)} %get-tuple-element.93.refs_5_.refs_3_, f32[1536,256]{1,0:T(8,128)S(1)} %get-tuple-element.94.refs_4_, ...), custom_call_target="tpu_custom_call" | custom-call | flops 6600000000 | tf_op jit(solution)/shard_map/pallas_call | solution.py:101
  124.0 3.0 %collective-permute-done.26.refs_1_ = f32[4,384,256]{2,1,0:T(8,128)S(1)} collective-permute-done((f32[4,384,256]{2,1,0:T(8,128)S(1)}, f32[4,384,256]{2,1,0:T(8,128)S(1)}, u32[]{:S(2)}, u32[]{:S(2)}) %collective-permute-start.26) | collective-permute-done | bytes 1572896 | tf_op jit(solution)/shard_map/ppermute | solution.py:308
  128.5 3.9 %all-to-all-start.3 = ((f32[4,384,256]{2,1,0:T(8,128)}), f32[4,384,256]{2,1,0:T(8,128)S(1)}, u32[]{:S(2)}, u32[]{:S(2)}) async-start(f32[4,384,256]{2,1,0:T(8,128)} %shard_map.162), calls=%async_computation.3 | async-start | bytes 3145728 | tf_op jit(solution)/shard_map/all_to_all | solution.py:316
  135.6 7.6 %collective-permute-done.29.refs_6_ = f32[192,256]{1,0:T(8,128)S(1)} collective-permute-done((f32[192,256]{1,0:T(8,128)S(1)}, f32[192,256]{1,0:T(8,128)S(1)}, u32[]{:S(2)}, u32[]{:S(2)}) %collective-permute-start.29) | collective-permute-done | bytes 196640 | tf_op jit(solution)/shard_map/ppermute | solution.py:308
  143.9 8.6 %all-to-all-done.3.refs_1_ = f32[4,384,256]{2,1,0:T(8,128)S(1)} async-done(((f32[4,384,256]{2,1,0:T(8,128)}), f32[4,384,256]{2,1,0:T(8,128)S(1)}, u32[]{:S(2)}, u32[]{:S(2)}) %all-to-all-start.3) | async-done | bytes 1572896 | tf_op jit(solution)/shard_map/all_to_all | solution.py:316
  152.5 2.3 %shard_map.163 = (f32[16,256]{1,0:T(8,128)}, f32[32,256]{1,0:T(8,128)}, f32[16,256]{1,0:T(8,128)}, f32[64,256]{1,0:T(8,128)}, f32[64,256]{1,0:T(8,128)}, /*index...) custom-call(s32[5]{0:T(128)S(1)} %stack.23.refs_0_, ...), custom_call_target="tpu_custom_call" | custom-call | flops 3300000000 | tf_op jit(solution)/shard_map/pallas_call | solution.py:101
  158.0 11.6 %all_to_all.25.refs_0_ = f32[4,128,256]{2,1,0:T(8,128)S(1)} all-to-all(f32[4,128,256]{2,1,0:T(8,128)S(1)} %shard_map.164), channel_id=1, replica_groups=mesh['h'=2,'q'=2,'p'=2,'y'=4,'c'=2,'x'=4] {'y'}, dimensions={0} | all-to-all | bytes 1048576 | tf_op jit(solution)/shard_map/all_to_all | solution.py:316
  (89 shorter events, 38.3 us)
Async XLA Ops:
  2.8 20.4 %all-to-all-start = ((f32[4,128,256]{2,1,0:T(8,128)}), f32[4,128,256]{2,1,0:T(8,128)S(1)}, u32[]{:S(2)}, u32[]{:S(2)}) async-start(f32[4,128,256]{2,1,0:T(8,128)} %get-tuple-element.64), calls=%async_computation | async-start | bytes 1048576 | tf_op jit(solution)/shard_map/all_to_all | solution.py:316
  7.8 11.9 %collective-permute-start.3 = (f32[128,256]{1,0:T(8,128)}, f32[128,256]{1,0:T(8,128)S(1)}, u32[]{:S(2)}, u32[]{:S(2)}) collective-permute-start(f32[128,256]{1,0:T(8,128)} %get-tuple-element.62.refs_5_), channel_id=1, source_target_pairs={{0,32},{32,0},{1,33},{33,1},{2,34},{34,2},{3,35},{35,3},{4,36},{36... | collective-permute-start | bytes 393224 | tf_op jit(solution)/shard_map/ppermute | solution.py:308
  9.5 7.1 %collective-permute-start.2 = (f32[64,256]{1,0:T(8,128)}, f32[64,256]{1,0:T(8,128)S(1)}, u32[]{:S(2)}, u32[]{:S(2)}) collective-permute-start(f32[64,256]{1,0:T(8,128)} %get-tuple-element.61.refs_1_), channel_id=1, source_target_pairs={{0,96},{32,64},{64,32},{96,0},{1,97},{33,65},{65,33},{97,1},{2,98}... | collective-permute-start | bytes 196616 | tf_op jit(solution)/shard_map/ppermute | solution.py:308
  12.2 7.1 %collective-permute-start.1 = (f32[64,256]{1,0:T(8,128)}, f32[64,256]{1,0:T(8,128)S(1)}, u32[]{:S(2)}, u32[]{:S(2)}) collective-permute-start(f32[64,256]{1,0:T(8,128)} %get-tuple-element.61.refs_1_), channel_id=1, source_target_pairs={{0,64},{32,96},{64,0},{96,32},{1,65},{33,97},{65,1},{97,33},{2,66}... | collective-permute-start | bytes 196616 | tf_op jit(solution)/shard_map/ppermute | solution.py:308
  12.5 7.3 %collective-permute-start = (f32[64,256]{1,0:T(8,128)}, f32[64,256]{1,0:T(8,128)S(1)}, u32[]{:S(2)}, u32[]{:S(2)}) collective-permute-start(f32[64,256]{1,0:T(8,128)} %get-tuple-element.61.refs_1_), channel_id=1, source_target_pairs={{0,32},{32,0},{64,96},{96,64},{1,33},{33,1},{65,97},{97,65},{2,34}... | collective-permute-start | bytes 196616 | tf_op jit(solution)/shard_map/ppermute | solution.py:308
  13.0 14.0 %collective-permute-start.10 = (f32[320,256]{1,0:T(8,128)}, f32[320,256]{1,0:T(8,128)S(1)}, u32[]{:S(2)}, u32[]{:S(2)}) collective-permute-start(f32[320,256]{1,0:T(8,128)} %get-tuple-element.69.refs_1_), channel_id=1, source_target_pairs={{0,3},{1,2},{2,1},{3,0},{4,7},{5,6},{6,5},{7,4},{8,11},{9,10},{10,... | collective-permute-start | bytes 983048 | tf_op jit(solution)/shard_map/ppermute | solution.py:308
  16.6 10.5 %collective-permute-start.9 = (f32[320,256]{1,0:T(8,128)}, f32[320,256]{1,0:T(8,128)S(1)}, u32[]{:S(2)}, u32[]{:S(2)}) collective-permute-start(f32[320,256]{1,0:T(8,128)} %get-tuple-element.69.refs_1_), channel_id=1, source_target_pairs={{0,2},{1,3},{2,0},{3,1},{4,6},{5,7},{6,4},{7,5},{8,10},{9,11},{10,... | collective-permute-start | bytes 983048 | tf_op jit(solution)/shard_map/ppermute | solution.py:308
  19.3 12.4 %collective-permute-start.8 = (f32[320,256]{1,0:T(8,128)}, f32[320,256]{1,0:T(8,128)S(1)}, u32[]{:S(2)}, u32[]{:S(2)}) collective-permute-start(f32[320,256]{1,0:T(8,128)} %get-tuple-element.69.refs_1_), channel_id=1, source_target_pairs={{0,1},{1,0},{2,3},{3,2},{4,5},{5,4},{6,7},{7,6},{8,9},{9,8},{10,11... | collective-permute-start | bytes 983048 | tf_op jit(solution)/shard_map/ppermute | solution.py:308
  23.2 36.0 %all-to-all-start.1 = ((f32[4,320,256]{2,1,0:T(8,128)}), f32[4,320,256]{2,1,0:T(8,128)S(1)}, u32[]{:S(2)}, u32[]{:S(2)}) async-start(f32[4,320,256]{2,1,0:T(8,128)} %get-tuple-element.65), calls=%async_computation.1 | async-start | bytes 2621440 | tf_op jit(solution)/shard_map/all_to_all | solution.py:316
  31.7 22.9 %collective-permute-start.14 = (f32[448,256]{1,0:T(8,128)S(1)}, f32[448,256]{1,0:T(8,128)S(1)}, u32[]{:S(2)}, u32[]{:S(2)}) collective-permute-start(f32[448,256]{1,0:T(8,128)S(1)} %get-tuple-element.76.refs_1_), channel_id=1, source_target_pairs={{0,3},{1,2},{2,1},{3,0},{4,7},{5,6},{6,5},{7,4},{8,11},{9,10},{10,... | collective-permute-start | bytes 1376264 | tf_op jit(solution)/shard_map/ppermute | solution.py:308
  31.9 22.7 %collective-permute-start.13 = (f32[448,256]{1,0:T(8,128)S(1)}, f32[448,256]{1,0:T(8,128)S(1)}, u32[]{:S(2)}, u32[]{:S(2)}) collective-permute-start(f32[448,256]{1,0:T(8,128)S(1)} %get-tuple-element.76.refs_1_), channel_id=1, source_target_pairs={{0,2},{1,3},{2,0},{3,1},{4,6},{5,7},{6,4},{7,5},{8,10},{9,11},{10,... | collective-permute-start | bytes 1376264 | tf_op jit(solution)/shard_map/ppermute | solution.py:308
  34.6 20.0 %collective-permute-start.12 = (f32[448,256]{1,0:T(8,128)S(1)}, f32[448,256]{1,0:T(8,128)S(1)}, u32[]{:S(2)}, u32[]{:S(2)}) collective-permute-start(f32[448,256]{1,0:T(8,128)S(1)} %get-tuple-element.76.refs_1_), channel_id=1, source_target_pairs={{0,1},{1,0},{2,3},{3,2},{4,5},{5,4},{6,7},{7,6},{8,9},{9,8},{10,11... | collective-permute-start | bytes 1376264 | tf_op jit(solution)/shard_map/ppermute | solution.py:308
  34.9 21.8 %collective-permute-start.11 = (f32[4,128,256]{2,1,0:T(8,128)S(1)}, f32[4,128,256]{2,1,0:T(8,128)S(1)}, u32[]{:S(2)}, u32[]{:S(2)}) collective-permute-start(f32[4,128,256]{2,1,0:T(8,128)S(1)} %all-to-all-done.refs_5_), channel_id=1, source_target_pairs={{0,4},{4,0},{1,5},{5,1},{2,6},{6,2},{3,7},{7,3},{8,12},{12,8},{9,1... | collective-permute-start | bytes 1572872 | tf_op jit(solution)/shard_map/ppermute | solution.py:308
  39.7 7.6 %collective-permute-start.4 = (f32[64,256]{1,0:T(8,128)S(1)}, f32[64,256]{1,0:T(8,128)S(1)}, u32[]{:S(2)}, u32[]{:S(2)}) collective-permute-start(f32[64,256]{1,0:T(8,128)S(1)} %get-tuple-element.66), channel_id=1, source_target_pairs={{0,128},{128,0},{1,129},{129,1},{2,130},{130,2},{3,131},{131,3},{4... | collective-permute-start | bytes 196616 | tf_op jit(solution)/shard_map/ppermute | solution.py:308
  47.3 11.5 %collective-permute-start.7 = (f32[64,256]{1,0:T(8,128)S(1)}, f32[64,256]{1,0:T(8,128)S(1)}, u32[]{:S(2)}, u32[]{:S(2)}) collective-permute-start(f32[64,256]{1,0:T(8,128)S(1)} %collective-permute-done.4.refs_4_), channel_id=1, source_target_pairs={{0,3},{1,2},{2,1},{3,0},{4,7},{5,6},{6,5},{7,4},{8,11},{9,10},{10,... | collective-permute-start | bytes 196616 | tf_op jit(solution)/shard_map/ppermute | solution.py:308
  54.6 4.6 %collective-permute-start.6 = (f32[64,256]{1,0:T(8,128)S(1)}, f32[64,256]{1,0:T(8,128)S(1)}, u32[]{:S(2)}, u32[]{:S(2)}) collective-permute-start(f32[64,256]{1,0:T(8,128)S(1)} %collective-permute-done.4.refs_4_), channel_id=1, source_target_pairs={{0,2},{1,3},{2,0},{3,1},{4,6},{5,7},{6,4},{7,5},{8,10},{9,11},{10,... | collective-permute-start | bytes 196616 | tf_op jit(solution)/shard_map/ppermute | solution.py:308
  59.2 5.5 %collective-permute-start.15 = (f32[4,320,256]{2,1,0:T(8,128)S(1)}, f32[4,320,256]{2,1,0:T(8,128)S(1)}, u32[]{:S(2)}, u32[]{:S(2)}) collective-permute-start(f32[4,320,256]{2,1,0:T(8,128)S(1)} %all-to-all-done.1.refs_8_), channel_id=1, source_target_pairs={{0,4},{4,0},{1,5},{5,1},{2,6},{6,2},{3,7},{7,3},{8,12},{12,8},{9,1... | collective-permute-start | bytes 3932168 | tf_op jit(solution)/shard_map/ppermute | solution.py:308
  69.6 22.9 %all-to-all-start.2 = ((f32[4,320,256]{2,1,0:T(8,128)}), f32[4,320,256]{2,1,0:T(8,128)S(1)}, u32[]{:S(2)}, u32[]{:S(2)}) async-start(f32[4,320,256]{2,1,0:T(8,128)} %get-tuple-element.87), calls=%async_computation.2 | async-start | bytes 2621440 | tf_op jit(solution)/shard_map/all_to_all | solution.py:316
  73.2 7.6 %collective-permute-start.18 = (f32[128,256]{1,0:T(8,128)S(1)}, f32[128,256]{1,0:T(8,128)S(1)}, u32[]{:S(2)}, u32[]{:S(2)}) collective-permute-start(f32[128,256]{1,0:T(8,128)S(1)} %get-tuple-element.85.refs_1_), channel_id=1, source_target_pairs={{0,3},{1,2},{2,1},{3,0},{4,7},{5,6},{6,5},{7,4},{8,11},{9,10},{10,... | collective-permute-start | bytes 393224 | tf_op jit(solution)/shard_map/ppermute | solution.py:308
  75.6 6.0 %collective-permute-start.17 = (f32[128,256]{1,0:T(8,128)S(1)}, f32[128,256]{1,0:T(8,128)S(1)}, u32[]{:S(2)}, u32[]{:S(2)}) collective-permute-start(f32[128,256]{1,0:T(8,128)S(1)} %get-tuple-element.85.refs_1_), channel_id=1, source_target_pairs={{0,2},{1,3},{2,0},{3,1},{4,6},{5,7},{6,4},{7,5},{8,10},{9,11},{10,... | collective-permute-start | bytes 393224 | tf_op jit(solution)/shard_map/ppermute | solution.py:308
  76.2 6.2 %collective-permute-start.16 = (f32[128,256]{1,0:T(8,128)S(1)}, f32[128,256]{1,0:T(8,128)S(1)}, u32[]{:S(2)}, u32[]{:S(2)}) collective-permute-start(f32[128,256]{1,0:T(8,128)S(1)} %get-tuple-element.85.refs_1_), channel_id=1, source_target_pairs={{0,1},{1,0},{2,3},{3,2},{4,5},{5,4},{6,7},{7,6},{8,9},{9,8},{10,11... | collective-permute-start | bytes 393224 | tf_op jit(solution)/shard_map/ppermute | solution.py:308
  84.7 6.1 %collective-permute-start.21 = (f32[128,256]{1,0:T(8,128)S(1)}, f32[128,256]{1,0:T(8,128)S(1)}, u32[]{:S(2)}, u32[]{:S(2)}) collective-permute-start(f32[128,256]{1,0:T(8,128)S(1)} %shard_map.158.refs_4_), channel_id=1, source_target_pairs={{0,3},{1,2},{2,1},{3,0},{4,7},{5,6},{6,5},{7,4},{8,11},{9,10},{10,... | collective-permute-start | bytes 393224 | tf_op jit(solution)/shard_map/ppermute | solution.py:308
  87.1 5.4 %collective-permute-start.20 = (f32[128,256]{1,0:T(8,128)S(1)}, f32[128,256]{1,0:T(8,128)S(1)}, u32[]{:S(2)}, u32[]{:S(2)}) collective-permute-start(f32[128,256]{1,0:T(8,128)S(1)} %shard_map.158.refs_4_), channel_id=1, source_target_pairs={{0,2},{1,3},{2,0},{3,1},{4,6},{5,7},{6,4},{7,5},{8,10},{9,11},{10,... | collective-permute-start | bytes 393224 | tf_op jit(solution)/shard_map/ppermute | solution.py:308
  87.6 4.9 %collective-permute-start.19 = (f32[128,256]{1,0:T(8,128)S(1)}, f32[128,256]{1,0:T(8,128)S(1)}, u32[]{:S(2)}, u32[]{:S(2)}) collective-permute-start(f32[128,256]{1,0:T(8,128)S(1)} %shard_map.158.refs_4_), channel_id=1, source_target_pairs={{0,1},{1,0},{2,3},{3,2},{4,5},{5,4},{6,7},{7,6},{8,9},{9,8},{10,11... | collective-permute-start | bytes 393224 | tf_op jit(solution)/shard_map/ppermute | solution.py:308
  92.5 6.1 %collective-permute-start.22 = (f32[4,320,256]{2,1,0:T(8,128)S(1)}, f32[4,320,256]{2,1,0:T(8,128)S(1)}, u32[]{:S(2)}, u32[]{:S(2)}) collective-permute-start(f32[4,320,256]{2,1,0:T(8,128)S(1)} %all-to-all-done.2.refs_8_), channel_id=1, source_target_pairs={{0,4},{4,0},{1,5},{5,1},{2,6},{6,2},{3,7},{7,3},{8,12},{12,8},{9,1... | collective-permute-start | bytes 3932168 | tf_op jit(solution)/shard_map/ppermute | solution.py:308
  102.0 14.4 %collective-permute-start.25 = (f32[256,256]{1,0:T(8,128)S(1)}, f32[256,256]{1,0:T(8,128)S(1)}, u32[]{:S(2)}, u32[]{:S(2)}) collective-permute-start(f32[256,256]{1,0:T(8,128)S(1)} %get-tuple-element.98.refs_6_.refs_7_), channel_id=1, source_target_pairs={{0,3},{1,2},{2,1},{3,0},{4,7},{5,6},{6,5},{7,4},{8,11},{9,10},{10,... | collective-permute-start | bytes 786440 | tf_op jit(solution)/shard_map/ppermute | solution.py:308
  103.8 12.7 %collective-permute-start.24 = (f32[256,256]{1,0:T(8,128)S(1)}, f32[256,256]{1,0:T(8,128)S(1)}, u32[]{:S(2)}, u32[]{:S(2)}) collective-permute-start(f32[256,256]{1,0:T(8,128)S(1)} %get-tuple-element.98.refs_6_.refs_7_), channel_id=1, source_target_pairs={{0,2},{1,3},{2,0},{3,1},{4,6},{5,7},{6,4},{7,5},{8,10},{9,11},{10,... | collective-permute-start | bytes 786440 | tf_op jit(solution)/shard_map/ppermute | solution.py:308
  104.3 12.5 %collective-permute-start.23 = (f32[256,256]{1,0:T(8,128)S(1)}, f32[256,256]{1,0:T(8,128)S(1)}, u32[]{:S(2)}, u32[]{:S(2)}) collective-permute-start(f32[256,256]{1,0:T(8,128)S(1)} %get-tuple-element.98.refs_6_.refs_7_), channel_id=1, source_target_pairs={{0,1},{1,0},{2,3},{3,2},{4,5},{5,4},{6,7},{7,6},{8,9},{9,8},{10,11... | collective-permute-start | bytes 786440 | tf_op jit(solution)/shard_map/ppermute | solution.py:308
  128.5 24.0 %all-to-all-start.3 = ((f32[4,384,256]{2,1,0:T(8,128)}), f32[4,384,256]{2,1,0:T(8,128)S(1)}, u32[]{:S(2)}, u32[]{:S(2)}) async-start(f32[4,384,256]{2,1,0:T(8,128)} %shard_map.162), calls=%async_computation.3 | async-start | bytes 3145728 | tf_op jit(solution)/shard_map/all_to_all | solution.py:316
  132.3 10.9 %collective-permute-start.29 = (f32[192,256]{1,0:T(8,128)S(1)}, f32[192,256]{1,0:T(8,128)S(1)}, u32[]{:S(2)}, u32[]{:S(2)}) collective-permute-start(f32[192,256]{1,0:T(8,128)S(1)} %get-tuple-element.106.refs_10_.refs_3_), channel_id=1, source_target_pairs={{0,3},{1,2},{2,1},{3,0},{4,7},{5,6},{6,5},{7,4},{8,11},{9,10},{10,... | collective-permute-start | bytes 589832 | tf_op jit(solution)/shard_map/ppermute | solution.py:308
  134.0 9.2 %collective-permute-start.28 = (f32[192,256]{1,0:T(8,128)S(1)}, f32[192,256]{1,0:T(8,128)S(1)}, u32[]{:S(2)}, u32[]{:S(2)}) collective-permute-start(f32[192,256]{1,0:T(8,128)S(1)} %get-tuple-element.106.refs_10_.refs_3_), channel_id=1, source_target_pairs={{0,2},{1,3},{2,0},{3,1},{4,6},{5,7},{6,4},{7,5},{8,10},{9,11},{10,... | collective-permute-start | bytes 589832 | tf_op jit(solution)/shard_map/ppermute | solution.py:308
  134.6 9.3 %collective-permute-start.27 = (f32[192,256]{1,0:T(8,128)S(1)}, f32[192,256]{1,0:T(8,128)S(1)}, u32[]{:S(2)}, u32[]{:S(2)}) collective-permute-start(f32[192,256]{1,0:T(8,128)S(1)} %get-tuple-element.106.refs_10_.refs_3_), channel_id=1, source_target_pairs={{0,1},{1,0},{2,3},{3,2},{4,5},{5,4},{6,7},{7,6},{8,9},{9,8},{10,11... | collective-permute-start | bytes 589832 | tf_op jit(solution)/shard_map/ppermute | solution.py:308
  (21 other events, 144.8 us)

commit v6 on v5

--- a/solution.py
+++ b/solution.py
@@ -22,8 +22,12 @@
 
 
 def dot(left, right, contract=((1,), (0,))):
-    left_high, left_low = halves(left)
-    right_high, right_low = halves(right)
+    return from_halves(halves(left), halves(right), contract)
+
+
+def from_halves(left, right, contract):
+    left_high, left_low = left
+    right_high, right_low = right
 
     def one(a, b):
         return lax.dot_general(a, b, (contract, ((), ())), preferred_element_type=F32)
@@ -118,8 +122,7 @@
     own_1[48:64, :] = v0[...]
     own_2[0:64, :] = v2[...]
     own_2[64:128, :] = b2[...]
-    own_3[0:192, :] = b3[...]
-    own_3[192:320, :] = v3[...]
+    own_3[...] = b3[...]
     for copy in range(4):
         columns_3[copy] = v3[...]
 
@@ -152,14 +155,15 @@
     out[...] = (parts[0] + parts[1]) + (parts[2] + parts[3])
 
 
-def couple_front(ids, a0, a1, a2, a3, own, other, w3, v3):
+def couple_front(ids, a0, a1, a2, a3, v3, own, other, w3, front):
     core, part = ids[CORE], ids[PART]
     total = jnp.zeros((192, COLS), F32)
     for distance, ref in enumerate((a0, a1, a2, a3)):
         quarter = part ^ distance
-        total += dot(ref[0:192, :], jnp.concatenate(ordered(core, own[quarter], other[quarter]), 0))
-        v3[:, pl.ds(times(quarter, COLS), COLS)] = ref[192:320, :]
+        total += dot(ref[...], jnp.concatenate(ordered(core, own[quarter], other[quarter]), 0))
     w3[...] = total
+    front[0:192, :] = total
+    front[192:320, :] = v3[...]
 
 
 def shelve(ids, r0, r1, r2, r3, held):
@@ -274,17 +278,18 @@
         f2[:, block * BLOCK : (block + 1) * BLOCK] = x2[
             :, pl.ds(times(sel[ids[FRONT], block], BLOCK), BLOCK)
         ]
-    total = dot(f2[...], w3_columns[...])
+    high, low = halves(f2[...])
+    total = from_halves((high, low), halves(w3_columns[...]), ((1,), (0,)))
     for y in range(4):
         keep[y, 0:128, :] = keep_1[y]
         send[y, 0:128, :] = send_1[y]
-    put(core, keep, send, inner(f2[...], -total), 192, 192)
+    put(core, keep, send, from_halves((high, low), halves(-total), ((0,), (0,))), 192, 192)
     mine = x2[:, pl.ds(times(part, COLS), COLS)]
     put(core, keep, send, inner(x2[:, pl.ds(times(pair, 512), 512)], mine), 128, 64)
 
 
 def last_level(
-    ids, parts, v3, w0, w1, w2, w3, d0, d1, e1, e2, d2, e3, keep, send
+    ids, parts, w0, w1, w2, w3, d0, d1, e1, e2, d2, e3, keep, send
 ):
     core, part = ids[CORE], ids[PART]
     total = (parts[0] + parts[1]) + (parts[2] + parts[3])
@@ -295,11 +300,10 @@
     d2[...] = total[128:192]
     below = total[192:384]
     e3[...] = below
-    right = jnp.concatenate([v3[:, pl.ds(times(part, COLS), COLS)], -below], 0)
+    right = jnp.concatenate([-below, w0[192:320, :]], 0)
     for distance, ref in enumerate((w0, w1, w2, w3)):
         place = part ^ distance
-        left = jnp.concatenate([v3[:, pl.ds(times(place, COLS), COLS)], ref[...]], 0)
-        rows = inner(left, right)
+        rows = inner(ref[...], right)
         keep[place] = jnp.where(core == 0, rows[0:128], rows[128:256])
         send[place] = jnp.where(core == 0, rows[128:256], rows[0:128])
 
@@ -333,7 +337,7 @@
     own_1, own_2, own_3, columns_3 = call(
         pack,
         1,
-        [(64, COLS), (128, COLS), (320, COLS), (4, 128, COLS)],
+        [(64, COLS), (128, COLS), (192, COLS), (4, 128, COLS)],
         [],
         *[Far(value) for value in (v0, v1, b1, v2, b2, v3, b3)],
     )
@@ -345,24 +349,23 @@
         2,
         [(4, 320, COLS), (448, COLS), (64, COLS)],
         [],
-        ids, *ancestors, own_2, pair_2,
-    )
-    early, columns_3 = lax.optimization_barrier((early, columns_3))
+        ids, Far(ancestors[0]), *ancestors[1:], Far(own_2), pair_2,
+    )
     own_rows = around(own_3)
-    own_rows, rows = lax.optimization_barrier((own_rows, rows))
+    early, columns_3, own_rows, rows = lax.optimization_barrier(
+        (early, columns_3, own_rows, rows)
+    )
     early = exchanged(early)
     row_0 = around(swapped(row_0, "h", 1))
-    w3, v3_rows = call(
+    w3, front = call(
         couple_front,
         2,
-        [(192, COLS), Far((128, S))],
-        [],
-        ids, *own_rows, columns_3, swapped(columns_3, "c", 1),
+        [(192, COLS), (320, COLS)],
+        [],
+        ids, *own_rows, Far(v3), columns_3, swapped(columns_3, "c", 1),
     )
     (held,) = call(shelve, 1, [Far((448, S))], [], ids, *around(rows))
-    early, row_0, w3, v3_rows, held = lax.optimization_barrier(
-        (early, row_0, w3, v3_rows, held)
-    )
+    early, row_0, w3, front, held = lax.optimization_barrier((early, row_0, w3, front, held))
 
     coupling, y1, f0, v0_rows, v1_columns = call(
         middle,
@@ -398,15 +401,14 @@
         ids, selector_3, Far(held, 128, 128), Far(f1), Far(w3_columns), Far(keep), Far(send),
         *around(m2),
     )
-    w3, keep, send = lax.optimization_barrier((w3, keep, send))
-    w3 = around(w3)
+    front, keep, send = lax.optimization_barrier((front, keep, send))
     d0, d1, e1, e2, d2, e3, keep, send = call(
         last_level,
         3,
         [(16, COLS), (32, COLS), (16, COLS), (64, COLS), (64, COLS), (192, COLS)]
         + [(4, 128, COLS)] * 2,
         [],
-        ids, core_sum(keep, send), Far(v3_rows), *w3,
+        ids, core_sum(keep, send), *around(front),
     )
     (d3,) = call(add_four, 1, [(128, COLS)], [], core_sum(keep, send))
     return d0, d1, e1, d2, e2, d3, e3

time: 171 us -> 170 us (level)
  waiting for transfers between devices: 63.1 us -> 57.3 us
  starting transfers between devices: 62.7 us -> 66.9 us
    all_to_all x4, waiting for transfers between devices: 8.58 us -> 2.97 us  [exchanged(): return lax.all_to_all(values, 'y', 0, 0)]
    ppermute x31, starting transfers between devices: 46.5 us -> 50.1 us  [swapped(): return lax.ppermute(array, axis, [(i, i ^ distance) for i in range(parts)])]
    unnamed x36 -> x34, local copies, waits for them, and re-layouts: 8.84 us -> 9.45 us
where the time goes in v6:
time: 170 us
  starting transfers between devices  66.9 us (39%)
  waiting for transfers between devices  57.3 us (34%)
  Pallas kernels  23.4 us (14%)
  blocking collectives  11.6 us (7%)
  local copies, waits for them, and re-layouts  9.53 us (6%)
    ppermute x31, waiting for transfers between devices, swapped(): return lax.ppermute(array, axis, [(i, i ^ distance) for i in range(parts)])  54.4 us
    ppermute x31, starting transfers between devices, swapped(): return lax.ppermute(array, axis, [(i, i ^ distance) for i in range(parts)])  50.1 us
    pallas_call x13, Pallas kernels, call(): pl.pallas_call(kernel, out_shape=[jax.ShapeDtypeStruct(shape, F32) for sh...  23.4 us
    all_to_all x4, starting transfers between devices, exchanged(): return lax.all_to_all(values, 'y', 0, 0)  16.8 us
    all_to_all x1, blocking collectives, exchanged(): return lax.all_to_all(values, 'y', 0, 0)  11.6 us
    unnamed x34, local copies, waits for them, and re-layouts  9.45 us
  transfers between devices with their start and end apart: 35, of which 19 were waited for; matrix products, arithmetic and copies ran while one was open for 0% of the time, Pallas kernels for 4%

profile of v6, /device:TPU:1, one launch (start us, length us, event | category | flops | bytes accessed | tf_op | source)
XLA Modules:
  0.0 169.6 jit_solution(4755797405671521529)
XLA Ops:
  0.6 2.1 %shard_map.153 = (f32[64,256]{1,0:T(8,128)}, f32[128,256]{1,0:T(8,128)}, f32[192,256]{1,0:T(8,128)}, f32[4,128,256]{2,1,0:T(8,128)}) custom-call(f32[16,256]{1,0:T(8,128)} %refs_0_.1, f32[32,256]{1,0:T(8,128)} %refs_1_.4, f32[16,256]{1,0:T(8,128)} %refs_2_.1, f32[64,256]{1,0:T(8,128)} %refs_3_.1, f32[64,256]{1,0:T(8,128)} %refs_4_.1, f32[128,256]{1,0:T(8,128)} %refs_5_.3, ...), custom_call_target="tpu_custom_call" | custom-call | flops 1100000000 | tf_op jit(solution)/shard_map/pallas_call | solution.py:105
  2.8 5.0 %all-to-all-start = ((f32[4,128,256]{2,1,0:T(8,128)}), f32[4,128,256]{2,1,0:T(8,128)S(1)}, u32[]{:S(2)}, u32[]{:S(2)}) async-start(f32[4,128,256]{2,1,0:T(8,128)} %get-tuple-element.64), calls=%async_computation | async-start | bytes 1048576 | tf_op jit(solution)/shard_map/all_to_all | solution.py:320
  9.4 2.7 %collective-permute-start.2 = (f32[64,256]{1,0:T(8,128)}, f32[64,256]{1,0:T(8,128)S(1)}, u32[]{:S(2)}, u32[]{:S(2)}) collective-permute-start(f32[64,256]{1,0:T(8,128)} %get-tuple-element.61.refs_1_), channel_id=1, source_target_pairs={{0,96},{32,64},{64,32},{96,0},{1,97},{33,65},{65,33},{97,1},{2,98}... | collective-permute-start | bytes 196616 | tf_op jit(solution)/shard_map/ppermute | solution.py:312
  13.0 2.5 %collective-permute-start.6 = (f32[192,256]{1,0:T(8,128)}, f32[192,256]{1,0:T(8,128)S(1)}, u32[]{:S(2)}, u32[]{:S(2)}) collective-permute-start(f32[192,256]{1,0:T(8,128)} %get-tuple-element.69.refs_1_), channel_id=1, source_target_pairs={{0,3},{1,2},{2,1},{3,0},{4,7},{5,6},{6,5},{7,4},{8,11},{9,10},{10,... | collective-permute-start | bytes 589832 | tf_op jit(solution)/shard_map/ppermute | solution.py:312
  16.5 2.7 %collective-permute-start.5 = (f32[192,256]{1,0:T(8,128)}, f32[192,256]{1,0:T(8,128)S(1)}, u32[]{:S(2)}, u32[]{:S(2)}) collective-permute-start(f32[192,256]{1,0:T(8,128)} %get-tuple-element.69.refs_1_), channel_id=1, source_target_pairs={{0,2},{1,3},{2,0},{3,1},{4,6},{5,7},{6,4},{7,5},{8,10},{9,11},{10,... | collective-permute-start | bytes 589832 | tf_op jit(solution)/shard_map/ppermute | solution.py:312
  21.5 2.0 %shard_map.154 = (f32[4,320,256]{2,1,0:T(8,128)}, f32[448,256]{1,0:T(8,128)S(1)}, f32[64,256]{1,0:T(8,128)S(1)}) custom-call(s32[5]{0:T(128)S(1)} %stack.23.refs_0_, f32[64,256]{1,0:T(8,128)S(1)} %copy-done.3, f32[64,256]{1,0:T(8,128)S(1)} %collective-permute-done.refs_2_, f32[64,256]{1,0:T(8,128)S(1)} %collective-permute-done.1.refs_3_, ...), custom_call_target="tpu_custom_call" | custom-call | flops 2200000000 | tf_op jit(solution)/shard_map/pallas_call | solution.py:105
  23.5 2.5 %collective-permute-done.4.refs_2_ = f32[192,256]{1,0:T(8,128)S(1)} collective-permute-done((f32[192,256]{1,0:T(8,128)}, f32[192,256]{1,0:T(8,128)S(1)}, u32[]{:S(2)}, u32[]{:S(2)}) %collective-permute-start.4) | collective-permute-done | bytes 196640 | tf_op jit(solution)/shard_map/ppermute | solution.py:312
  26.0 3.5 %all-to-all-start.1 = ((f32[4,320,256]{2,1,0:T(8,128)}), f32[4,320,256]{2,1,0:T(8,128)S(1)}, u32[]{:S(2)}, u32[]{:S(2)}) async-start(f32[4,320,256]{2,1,0:T(8,128)} %get-tuple-element.67), calls=%async_computation.1 | async-start | bytes 2621440 | tf_op jit(solution)/shard_map/all_to_all | solution.py:320
  32.9 5.0 %collective-permute-start.11 = (f32[4,128,256]{2,1,0:T(8,128)S(1)}, f32[4,128,256]{2,1,0:T(8,128)S(1)}, u32[]{:S(2)}, u32[]{:S(2)}) collective-permute-start(f32[4,128,256]{2,1,0:T(8,128)S(1)} %all-to-all-done.refs_6_), channel_id=1, source_target_pairs={{0,4},{4,0},{1,5},{5,1},{2,6},{6,2},{3,7},{7,3},{8,12},{12,8},{9,1... | collective-permute-start | bytes 1572872 | tf_op jit(solution)/shard_map/ppermute | solution.py:312
  38.0 5.2 %collective-permute-start.7 = (f32[64,256]{1,0:T(8,128)S(1)}, f32[64,256]{1,0:T(8,128)S(1)}, u32[]{:S(2)}, u32[]{:S(2)}) collective-permute-start(f32[64,256]{1,0:T(8,128)S(1)} %get-tuple-element.68), channel_id=1, source_target_pairs={{0,128},{128,0},{1,129},{129,1},{2,130},{130,2},{3,131},{131,3},{4... | collective-permute-start | bytes 196616 | tf_op jit(solution)/shard_map/ppermute | solution.py:312
  43.2 2.4 %collective-permute-done.7.refs_4_ = f32[64,256]{1,0:T(8,128)S(1)} collective-permute-done((f32[64,256]{1,0:T(8,128)S(1)}, f32[64,256]{1,0:T(8,128)S(1)}, u32[]{:S(2)}, u32[]{:S(2)}) %collective-permute-start.7) | collective-permute-done | bytes 65568 | tf_op jit(solution)/shard_map/ppermute | solution.py:312
  46.6 4.9 %collective-permute-done.14.refs_4_ = f32[448,256]{1,0:T(8,128)S(1)} collective-permute-done((f32[448,256]{1,0:T(8,128)S(1)}, f32[448,256]{1,0:T(8,128)S(1)}, u32[]{:S(2)}, u32[]{:S(2)}) %collective-permute-start.14) | collective-permute-done | bytes 458784 | tf_op jit(solution)/shard_map/ppermute | solution.py:312
  51.5 1.8 %collective-permute-start.8 = (f32[64,256]{1,0:T(8,128)S(1)}, f32[64,256]{1,0:T(8,128)S(1)}, u32[]{:S(2)}, u32[]{:S(2)}) collective-permute-start(f32[64,256]{1,0:T(8,128)S(1)} %collective-permute-done.7.refs_4_), channel_id=1, source_target_pairs={{0,1},{1,0},{2,3},{3,2},{4,5},{5,4},{6,7},{7,6},{8,9},{9,8},{10,11... | collective-permute-start | bytes 196616 | tf_op jit(solution)/shard_map/ppermute | solution.py:312
  56.8 3.6 %collective-permute-start.15 = (f32[4,320,256]{2,1,0:T(8,128)S(1)}, f32[4,320,256]{2,1,0:T(8,128)S(1)}, u32[]{:S(2)}, u32[]{:S(2)}) collective-permute-start(f32[4,320,256]{2,1,0:T(8,128)S(1)} %all-to-all-done.1.refs_8_), channel_id=1, source_target_pairs={{0,4},{4,0},{1,5},{5,1},{2,6},{6,2},{3,7},{7,3},{8,12},{12,8},{9,1... | collective-permute-start | bytes 3932168 | tf_op jit(solution)/shard_map/ppermute | solution.py:312
  60.4 2.7 %collective-permute-done.15.refs_9_ = f32[4,320,256]{2,1,0:T(8,128)S(1)} collective-permute-done((f32[4,320,256]{2,1,0:T(8,128)S(1)}, f32[4,320,256]{2,1,0:T(8,128)S(1)}, u32[]{:S(2)}, u32[]{:S(2)}) %collective-permute-start.15) | collective-permute-done | bytes 1310752 | tf_op jit(solution)/shard_map/ppermute | solution.py:312
  64.5 2.6 %shard_map.157 = (f32[4,320,256]{2,1,0:T(8,128)}, f32[128,256]{1,0:T(8,128)S(1)}, f32[128,512]{1,0:T(8,128)S(1)}, f32[128,1024]{1,0:T(8,128)S(1)}, f32[1024,256]{1,0:T(8,128)S(1)}) custom-call(s32[5]{0:T(128)S(1)} %stack.23.refs_0_, s32[2,4]{1,0:T(2,128)S(1)} %copy-done.6, f32[448,1024]{1,0:T(8,128)S(1)} %copy-done.8, f32[448,1024]{1,0:T(8,128)S(1)} %copy-done.8, ...), custom_call_target="tpu_custom_call" | custom-call | flops 4400000000 | tf_op jit(solution)/shard_map/pallas_call | solution.py:105
  69.6 4.2 %all-to-all-start.2 = ((f32[4,320,256]{2,1,0:T(8,128)}), f32[4,320,256]{2,1,0:T(8,128)S(1)}, u32[]{:S(2)}, u32[]{:S(2)}) async-start(f32[4,320,256]{2,1,0:T(8,128)} %get-tuple-element.88), calls=%async_computation.2 | async-start | bytes 2621440 | tf_op jit(solution)/shard_map/all_to_all | solution.py:320
  77.1 2.4 %collective-permute-done.18.refs_4_ = f32[128,256]{1,0:T(8,128)S(1)} collective-permute-done((f32[128,256]{1,0:T(8,128)S(1)}, f32[128,256]{1,0:T(8,128)S(1)}, u32[]{:S(2)}, u32[]{:S(2)}) %collective-permute-start.18) | collective-permute-done | bytes 131104 | tf_op jit(solution)/shard_map/ppermute | solution.py:312
  80.6 2.0 %collective-permute-done.16.refs_2_ = f32[128,256]{1,0:T(8,128)S(1)} collective-permute-done((f32[128,256]{1,0:T(8,128)S(1)}, f32[128,256]{1,0:T(8,128)S(1)}, u32[]{:S(2)}, u32[]{:S(2)}) %collective-permute-start.16) | collective-permute-done | bytes 131104 | tf_op jit(solution)/shard_map/ppermute | solution.py:312
  87.0 2.1 %collective-permute-done.21.refs_7_ = f32[128,256]{1,0:T(8,128)S(1)} collective-permute-done((f32[128,256]{1,0:T(8,128)S(1)}, f32[128,256]{1,0:T(8,128)S(1)}, u32[]{:S(2)}, u32[]{:S(2)}) %collective-permute-start.21) | collective-permute-done | bytes 131104 | tf_op jit(solution)/shard_map/ppermute | solution.py:312
  89.1 1.7 collective-permute-done.20.refs_6_
  91.3 3.0 %collective-permute-start.22 = (f32[4,320,256]{2,1,0:T(8,128)S(1)}, f32[4,320,256]{2,1,0:T(8,128)S(1)}, u32[]{:S(2)}, u32[]{:S(2)}) collective-permute-start(f32[4,320,256]{2,1,0:T(8,128)S(1)} %all-to-all-done.2.refs_8_), channel_id=1, source_target_pairs={{0,4},{4,0},{1,5},{5,1},{2,6},{6,2},{3,7},{7,3},{8,12},{12,8},{9,1... | collective-permute-start | bytes 3932168 | tf_op jit(solution)/shard_map/ppermute | solution.py:312
  94.3 2.7 %collective-permute-done.22.refs_9_ = f32[4,320,256]{2,1,0:T(8,128)S(1)} collective-permute-done((f32[4,320,256]{2,1,0:T(8,128)S(1)}, f32[4,320,256]{2,1,0:T(8,128)S(1)}, u32[]{:S(2)}, u32[]{:S(2)}) %collective-permute-start.22) | collective-permute-done | bytes 1310752 | tf_op jit(solution)/shard_map/ppermute | solution.py:312
  99.4 1.9 %shard_map.159 = (f32[256,256]{1,0:T(8,128)S(1)}, f32[256,1024]{1,0:T(8,128)S(1)}, f32[1536,256]{1,0:T(8,128)S(1)}, f32[256,256]{1,0:T(8,128)S(1)}, f32[256,256]{1,0:T(8,128)S(1)}) custom-call(s32[5]{0:T(128)S(1)} %stack.23.refs_0_, s32[4,8]{1,0:T(4,128)S(1)} %copy-done.5, f32[448,1024]{1,0:T(8,128)S(1)} %copy-done.9, f32[128,512]{1,0:T(8,128)S(1)} %copy-done.16, ...), custom_call_target="tpu_custom_call" | custom-call | flops 3300000000 | tf_op jit(solution)/shard_map/pallas_call | solution.py:105
  106.2 9.6 %collective-permute-done.25.refs_10_ = f32[256,256]{1,0:T(8,128)S(1)} collective-permute-done((f32[256,256]{1,0:T(8,128)S(1)}, f32[256,256]{1,0:T(8,128)S(1)}, u32[]{:S(2)}, u32[]{:S(2)}) %collective-permute-start.25) | collective-permute-done | bytes 262176 | tf_op jit(solution)/shard_map/ppermute | solution.py:312
  116.1 5.6 %shard_map.161 = (f32[4,384,256]{2,1,0:T(8,128)S(1)}, f32[4,384,256]{2,1,0:T(8,128)S(1)}) custom-call(s32[5]{0:T(128)S(1)} %stack.23.refs_0_, s32[8,12]{1,0:T(8,128)S(1)} %copy-done.4, f32[448,1024]{1,0:T(8,128)S(1)} %copy-done.10, f32[256,1024]{1,0:T(8,128)S(1)} %get-tuple-element.94.refs_5_.refs_3_, f32[1536,256]{1,0:T(8,128)S(1)} %get-tuple-element.95.refs_4_, ...), custom_call_target="tpu_custom_call" | custom-call | flops 6600000000 | tf_op jit(solution)/shard_map/pallas_call | solution.py:105
  123.3 3.0 %collective-permute-done.26.refs_1_ = f32[4,384,256]{2,1,0:T(8,128)S(1)} collective-permute-done((f32[4,384,256]{2,1,0:T(8,128)S(1)}, f32[4,384,256]{2,1,0:T(8,128)S(1)}, u32[]{:S(2)}, u32[]{:S(2)}) %collective-permute-start.26) | collective-permute-done | bytes 1572896 | tf_op jit(solution)/shard_map/ppermute | solution.py:312
  127.8 4.0 %all-to-all-start.3 = ((f32[4,384,256]{2,1,0:T(8,128)}), f32[4,384,256]{2,1,0:T(8,128)S(1)}, u32[]{:S(2)}, u32[]{:S(2)}) async-start(f32[4,384,256]{2,1,0:T(8,128)} %shard_map.162), calls=%async_computation.3 | async-start | bytes 3145728 | tf_op jit(solution)/shard_map/all_to_all | solution.py:320
  135.0 13.6 %collective-permute-done.29.refs_5_ = f32[320,256]{1,0:T(8,128)S(1)} collective-permute-done((f32[320,256]{1,0:T(8,128)S(1)}, f32[320,256]{1,0:T(8,128)S(1)}, u32[]{:S(2)}, u32[]{:S(2)}) %collective-permute-start.29) | collective-permute-done | bytes 327712 | tf_op jit(solution)/shard_map/ppermute | solution.py:312
  148.9 3.0 %all-to-all-done.3.refs_1_ = f32[4,384,256]{2,1,0:T(8,128)S(1)} async-done(((f32[4,384,256]{2,1,0:T(8,128)}), f32[4,384,256]{2,1,0:T(8,128)S(1)}, u32[]{:S(2)}, u32[]{:S(2)}) %all-to-all-start.3) | async-done | bytes 1572896 | tf_op jit(solution)/shard_map/all_to_all | solution.py:320
  151.9 2.3 %shard_map.163 = (f32[16,256]{1,0:T(8,128)}, f32[32,256]{1,0:T(8,128)}, f32[16,256]{1,0:T(8,128)}, f32[64,256]{1,0:T(8,128)}, f32[64,256]{1,0:T(8,128)}, /*index...) custom-call(s32[5]{0:T(128)S(1)} %stack.23.refs_0_, ...), custom_call_target="tpu_custom_call" | custom-call | flops 3300000000 | tf_op jit(solution)/shard_map/pallas_call | solution.py:105
  157.3 11.6 %all_to_all.25.refs_0_ = f32[4,128,256]{2,1,0:T(8,128)S(1)} all-to-all(f32[4,128,256]{2,1,0:T(8,128)S(1)} %shard_map.164), channel_id=1, replica_groups=mesh['h'=2,'q'=2,'p'=2,'y'=4,'c'=2,'x'=4] {'y'}, dimensions={0} | all-to-all | bytes 1048576 | tf_op jit(solution)/shard_map/all_to_all | solution.py:320
  (87 shorter events, 44.9 us)
Async XLA Ops:
  2.8 23.3 %all-to-all-start = ((f32[4,128,256]{2,1,0:T(8,128)}), f32[4,128,256]{2,1,0:T(8,128)S(1)}, u32[]{:S(2)}, u32[]{:S(2)}) async-start(f32[4,128,256]{2,1,0:T(8,128)} %get-tuple-element.64), calls=%async_computation | async-start | bytes 1048576 | tf_op jit(solution)/shard_map/all_to_all | solution.py:320
  7.8 11.9 %collective-permute-start.3 = (f32[128,256]{1,0:T(8,128)}, f32[128,256]{1,0:T(8,128)S(1)}, u32[]{:S(2)}, u32[]{:S(2)}) collective-permute-start(f32[128,256]{1,0:T(8,128)} %get-tuple-element.62.refs_5_), channel_id=1, source_target_pairs={{0,32},{32,0},{1,33},{33,1},{2,34},{34,2},{3,35},{35,3},{4,36},{36... | collective-permute-start | bytes 393224 | tf_op jit(solution)/shard_map/ppermute | solution.py:312
  9.4 7.1 %collective-permute-start.2 = (f32[64,256]{1,0:T(8,128)}, f32[64,256]{1,0:T(8,128)S(1)}, u32[]{:S(2)}, u32[]{:S(2)}) collective-permute-start(f32[64,256]{1,0:T(8,128)} %get-tuple-element.61.refs_1_), channel_id=1, source_target_pairs={{0,96},{32,64},{64,32},{96,0},{1,97},{33,65},{65,33},{97,1},{2,98}... | collective-permute-start | bytes 196616 | tf_op jit(solution)/shard_map/ppermute | solution.py:312
  12.1 7.1 %collective-permute-start.1 = (f32[64,256]{1,0:T(8,128)}, f32[64,256]{1,0:T(8,128)S(1)}, u32[]{:S(2)}, u32[]{:S(2)}) collective-permute-start(f32[64,256]{1,0:T(8,128)} %get-tuple-element.61.refs_1_), channel_id=1, source_target_pairs={{0,64},{32,96},{64,0},{96,32},{1,65},{33,97},{65,1},{97,33},{2,66}... | collective-permute-start | bytes 196616 | tf_op jit(solution)/shard_map/ppermute | solution.py:312
  12.4 7.3 %collective-permute-start = (f32[64,256]{1,0:T(8,128)}, f32[64,256]{1,0:T(8,128)S(1)}, u32[]{:S(2)}, u32[]{:S(2)}) collective-permute-start(f32[64,256]{1,0:T(8,128)} %get-tuple-element.61.refs_1_), channel_id=1, source_target_pairs={{0,32},{32,0},{64,96},{96,64},{1,33},{33,1},{65,97},{97,65},{2,34}... | collective-permute-start | bytes 196616 | tf_op jit(solution)/shard_map/ppermute | solution.py:312
  13.0 10.5 %collective-permute-start.6 = (f32[192,256]{1,0:T(8,128)}, f32[192,256]{1,0:T(8,128)S(1)}, u32[]{:S(2)}, u32[]{:S(2)}) collective-permute-start(f32[192,256]{1,0:T(8,128)} %get-tuple-element.69.refs_1_), channel_id=1, source_target_pairs={{0,3},{1,2},{2,1},{3,0},{4,7},{5,6},{6,5},{7,4},{8,11},{9,10},{10,... | collective-permute-start | bytes 589832 | tf_op jit(solution)/shard_map/ppermute | solution.py:312
  16.5 7.0 %collective-permute-start.5 = (f32[192,256]{1,0:T(8,128)}, f32[192,256]{1,0:T(8,128)S(1)}, u32[]{:S(2)}, u32[]{:S(2)}) collective-permute-start(f32[192,256]{1,0:T(8,128)} %get-tuple-element.69.refs_1_), channel_id=1, source_target_pairs={{0,2},{1,3},{2,0},{3,1},{4,6},{5,7},{6,4},{7,5},{8,10},{9,11},{10,... | collective-permute-start | bytes 589832 | tf_op jit(solution)/shard_map/ppermute | solution.py:312
  19.3 6.8 %collective-permute-start.4 = (f32[192,256]{1,0:T(8,128)}, f32[192,256]{1,0:T(8,128)S(1)}, u32[]{:S(2)}, u32[]{:S(2)}) collective-permute-start(f32[192,256]{1,0:T(8,128)} %get-tuple-element.69.refs_1_), channel_id=1, source_target_pairs={{0,1},{1,0},{2,3},{3,2},{4,5},{5,4},{6,7},{7,6},{8,9},{9,8},{10,11... | collective-permute-start | bytes 589832 | tf_op jit(solution)/shard_map/ppermute | solution.py:312
  26.0 30.8 %all-to-all-start.1 = ((f32[4,320,256]{2,1,0:T(8,128)}), f32[4,320,256]{2,1,0:T(8,128)S(1)}, u32[]{:S(2)}, u32[]{:S(2)}) async-start(f32[4,320,256]{2,1,0:T(8,128)} %get-tuple-element.67), calls=%async_computation.1 | async-start | bytes 2621440 | tf_op jit(solution)/shard_map/all_to_all | solution.py:320
  29.6 21.9 %collective-permute-start.14 = (f32[448,256]{1,0:T(8,128)S(1)}, f32[448,256]{1,0:T(8,128)S(1)}, u32[]{:S(2)}, u32[]{:S(2)}) collective-permute-start(f32[448,256]{1,0:T(8,128)S(1)} %get-tuple-element.76.refs_1_), channel_id=1, source_target_pairs={{0,3},{1,2},{2,1},{3,0},{4,7},{5,6},{6,5},{7,4},{8,11},{9,10},{10,... | collective-permute-start | bytes 1376264 | tf_op jit(solution)/shard_map/ppermute | solution.py:312
  31.0 20.5 %collective-permute-start.13 = (f32[448,256]{1,0:T(8,128)S(1)}, f32[448,256]{1,0:T(8,128)S(1)}, u32[]{:S(2)}, u32[]{:S(2)}) collective-permute-start(f32[448,256]{1,0:T(8,128)S(1)} %get-tuple-element.76.refs_1_), channel_id=1, source_target_pairs={{0,2},{1,3},{2,0},{3,1},{4,6},{5,7},{6,4},{7,5},{8,10},{9,11},{10,... | collective-permute-start | bytes 1376264 | tf_op jit(solution)/shard_map/ppermute | solution.py:312
  32.5 20.8 %collective-permute-start.12 = (f32[448,256]{1,0:T(8,128)S(1)}, f32[448,256]{1,0:T(8,128)S(1)}, u32[]{:S(2)}, u32[]{:S(2)}) collective-permute-start(f32[448,256]{1,0:T(8,128)S(1)} %get-tuple-element.76.refs_1_), channel_id=1, source_target_pairs={{0,1},{1,0},{2,3},{3,2},{4,5},{5,4},{6,7},{7,6},{8,9},{9,8},{10,11... | collective-permute-start | bytes 1376264 | tf_op jit(solution)/shard_map/ppermute | solution.py:312
  32.9 22.5 %collective-permute-start.11 = (f32[4,128,256]{2,1,0:T(8,128)S(1)}, f32[4,128,256]{2,1,0:T(8,128)S(1)}, u32[]{:S(2)}, u32[]{:S(2)}) collective-permute-start(f32[4,128,256]{2,1,0:T(8,128)S(1)} %all-to-all-done.refs_6_), channel_id=1, source_target_pairs={{0,4},{4,0},{1,5},{5,1},{2,6},{6,2},{3,7},{7,3},{8,12},{12,8},{9,1... | collective-permute-start | bytes 1572872 | tf_op jit(solution)/shard_map/ppermute | solution.py:312
  38.0 7.6 %collective-permute-start.7 = (f32[64,256]{1,0:T(8,128)S(1)}, f32[64,256]{1,0:T(8,128)S(1)}, u32[]{:S(2)}, u32[]{:S(2)}) collective-permute-start(f32[64,256]{1,0:T(8,128)S(1)} %get-tuple-element.68), channel_id=1, source_target_pairs={{0,128},{128,0},{1,129},{129,1},{2,130},{130,2},{3,131},{131,3},{4... | collective-permute-start | bytes 196616 | tf_op jit(solution)/shard_map/ppermute | solution.py:312
  45.6 11.2 %collective-permute-start.10 = (f32[64,256]{1,0:T(8,128)S(1)}, f32[64,256]{1,0:T(8,128)S(1)}, u32[]{:S(2)}, u32[]{:S(2)}) collective-permute-start(f32[64,256]{1,0:T(8,128)S(1)} %collective-permute-done.7.refs_4_), channel_id=1, source_target_pairs={{0,3},{1,2},{2,1},{3,0},{4,7},{5,6},{6,5},{7,4},{8,11},{9,10},{10,... | collective-permute-start | bytes 196616 | tf_op jit(solution)/shard_map/ppermute | solution.py:312
  51.5 5.3 %collective-permute-start.8 = (f32[64,256]{1,0:T(8,128)S(1)}, f32[64,256]{1,0:T(8,128)S(1)}, u32[]{:S(2)}, u32[]{:S(2)}) collective-permute-start(f32[64,256]{1,0:T(8,128)S(1)} %collective-permute-done.7.refs_4_), channel_id=1, source_target_pairs={{0,1},{1,0},{2,3},{3,2},{4,5},{5,4},{6,7},{7,6},{8,9},{9,8},{10,11... | collective-permute-start | bytes 196616 | tf_op jit(solution)/shard_map/ppermute | solution.py:312
  56.8 6.2 %collective-permute-start.15 = (f32[4,320,256]{2,1,0:T(8,128)S(1)}, f32[4,320,256]{2,1,0:T(8,128)S(1)}, u32[]{:S(2)}, u32[]{:S(2)}) collective-permute-start(f32[4,320,256]{2,1,0:T(8,128)S(1)} %all-to-all-done.1.refs_8_), channel_id=1, source_target_pairs={{0,4},{4,0},{1,5},{5,1},{2,6},{6,2},{3,7},{7,3},{8,12},{12,8},{9,1... | collective-permute-start | bytes 3932168 | tf_op jit(solution)/shard_map/ppermute | solution.py:312
  69.6 21.7 %all-to-all-start.2 = ((f32[4,320,256]{2,1,0:T(8,128)}), f32[4,320,256]{2,1,0:T(8,128)S(1)}, u32[]{:S(2)}, u32[]{:S(2)}) async-start(f32[4,320,256]{2,1,0:T(8,128)} %get-tuple-element.88), calls=%async_computation.2 | async-start | bytes 2621440 | tf_op jit(solution)/shard_map/all_to_all | solution.py:320
  73.8 5.6 %collective-permute-start.18 = (f32[128,256]{1,0:T(8,128)S(1)}, f32[128,256]{1,0:T(8,128)S(1)}, u32[]{:S(2)}, u32[]{:S(2)}) collective-permute-start(f32[128,256]{1,0:T(8,128)S(1)} %get-tuple-element.86.refs_1_), channel_id=1, source_target_pairs={{0,3},{1,2},{2,1},{3,0},{4,7},{5,6},{6,5},{7,4},{8,11},{9,10},{10,... | collective-permute-start | bytes 393224 | tf_op jit(solution)/shard_map/ppermute | solution.py:312
  75.2 5.4 %collective-permute-start.17 = (f32[128,256]{1,0:T(8,128)S(1)}, f32[128,256]{1,0:T(8,128)S(1)}, u32[]{:S(2)}, u32[]{:S(2)}) collective-permute-start(f32[128,256]{1,0:T(8,128)S(1)} %get-tuple-element.86.refs_1_), channel_id=1, source_target_pairs={{0,2},{1,3},{2,0},{3,1},{4,6},{5,7},{6,4},{7,5},{8,10},{9,11},{10,... | collective-permute-start | bytes 393224 | tf_op jit(solution)/shard_map/ppermute | solution.py:312
  76.0 6.6 %collective-permute-start.16 = (f32[128,256]{1,0:T(8,128)S(1)}, f32[128,256]{1,0:T(8,128)S(1)}, u32[]{:S(2)}, u32[]{:S(2)}) collective-permute-start(f32[128,256]{1,0:T(8,128)S(1)} %get-tuple-element.86.refs_1_), channel_id=1, source_target_pairs={{0,1},{1,0},{2,3},{3,2},{4,5},{5,4},{6,7},{7,6},{8,9},{9,8},{10,11... | collective-permute-start | bytes 393224 | tf_op jit(solution)/shard_map/ppermute | solution.py:312
  83.7 5.4 %collective-permute-start.21 = (f32[128,256]{1,0:T(8,128)S(1)}, f32[128,256]{1,0:T(8,128)S(1)}, u32[]{:S(2)}, u32[]{:S(2)}) collective-permute-start(f32[128,256]{1,0:T(8,128)S(1)} %shard_map.158.refs_4_), channel_id=1, source_target_pairs={{0,3},{1,2},{2,1},{3,0},{4,7},{5,6},{6,5},{7,4},{8,11},{9,10},{10,... | collective-permute-start | bytes 393224 | tf_op jit(solution)/shard_map/ppermute | solution.py:312
  85.1 5.6 %collective-permute-start.20 = (f32[128,256]{1,0:T(8,128)S(1)}, f32[128,256]{1,0:T(8,128)S(1)}, u32[]{:S(2)}, u32[]{:S(2)}) collective-permute-start(f32[128,256]{1,0:T(8,128)S(1)} %shard_map.158.refs_4_), channel_id=1, source_target_pairs={{0,2},{1,3},{2,0},{3,1},{4,6},{5,7},{6,4},{7,5},{8,10},{9,11},{10,... | collective-permute-start | bytes 393224 | tf_op jit(solution)/shard_map/ppermute | solution.py:312
  86.0 5.3 %collective-permute-start.19 = (f32[128,256]{1,0:T(8,128)S(1)}, f32[128,256]{1,0:T(8,128)S(1)}, u32[]{:S(2)}, u32[]{:S(2)}) collective-permute-start(f32[128,256]{1,0:T(8,128)S(1)} %shard_map.158.refs_4_), channel_id=1, source_target_pairs={{0,1},{1,0},{2,3},{3,2},{4,5},{5,4},{6,7},{7,6},{8,9},{9,8},{10,11... | collective-permute-start | bytes 393224 | tf_op jit(solution)/shard_map/ppermute | solution.py:312
  91.3 5.7 %collective-permute-start.22 = (f32[4,320,256]{2,1,0:T(8,128)S(1)}, f32[4,320,256]{2,1,0:T(8,128)S(1)}, u32[]{:S(2)}, u32[]{:S(2)}) collective-permute-start(f32[4,320,256]{2,1,0:T(8,128)S(1)} %all-to-all-done.2.refs_8_), channel_id=1, source_target_pairs={{0,4},{4,0},{1,5},{5,1},{2,6},{6,2},{3,7},{7,3},{8,12},{12,8},{9,1... | collective-permute-start | bytes 3932168 | tf_op jit(solution)/shard_map/ppermute | solution.py:312
  101.3 14.4 %collective-permute-start.25 = (f32[256,256]{1,0:T(8,128)S(1)}, f32[256,256]{1,0:T(8,128)S(1)}, u32[]{:S(2)}, u32[]{:S(2)}) collective-permute-start(f32[256,256]{1,0:T(8,128)S(1)} %get-tuple-element.99.refs_6_.refs_7_), channel_id=1, source_target_pairs={{0,3},{1,2},{2,1},{3,0},{4,7},{5,6},{6,5},{7,4},{8,11},{9,10},{10,... | collective-permute-start | bytes 786440 | tf_op jit(solution)/shard_map/ppermute | solution.py:312
  102.8 13.0 %collective-permute-start.24 = (f32[256,256]{1,0:T(8,128)S(1)}, f32[256,256]{1,0:T(8,128)S(1)}, u32[]{:S(2)}, u32[]{:S(2)}) collective-permute-start(f32[256,256]{1,0:T(8,128)S(1)} %get-tuple-element.99.refs_6_.refs_7_), channel_id=1, source_target_pairs={{0,2},{1,3},{2,0},{3,1},{4,6},{5,7},{6,4},{7,5},{8,10},{9,11},{10,... | collective-permute-start | bytes 786440 | tf_op jit(solution)/shard_map/ppermute | solution.py:312
  103.6 12.5 %collective-permute-start.23 = (f32[256,256]{1,0:T(8,128)S(1)}, f32[256,256]{1,0:T(8,128)S(1)}, u32[]{:S(2)}, u32[]{:S(2)}) collective-permute-start(f32[256,256]{1,0:T(8,128)S(1)} %get-tuple-element.99.refs_6_.refs_7_), channel_id=1, source_target_pairs={{0,1},{1,0},{2,3},{3,2},{4,5},{5,4},{6,7},{7,6},{8,9},{9,8},{10,11... | collective-permute-start | bytes 786440 | tf_op jit(solution)/shard_map/ppermute | solution.py:312
  127.8 24.1 %all-to-all-start.3 = ((f32[4,384,256]{2,1,0:T(8,128)}), f32[4,384,256]{2,1,0:T(8,128)S(1)}, u32[]{:S(2)}, u32[]{:S(2)}) async-start(f32[4,384,256]{2,1,0:T(8,128)} %shard_map.162), calls=%async_computation.3 | async-start | bytes 3145728 | tf_op jit(solution)/shard_map/all_to_all | solution.py:320
  131.7 16.8 %collective-permute-start.29 = (f32[320,256]{1,0:T(8,128)S(1)}, f32[320,256]{1,0:T(8,128)S(1)}, u32[]{:S(2)}, u32[]{:S(2)}) collective-permute-start(f32[320,256]{1,0:T(8,128)S(1)} %get-tuple-element.106.refs_2_), channel_id=1, source_target_pairs={{0,3},{1,2},{2,1},{3,0},{4,7},{5,6},{6,5},{7,4},{8,11},{9,10},{10,... | collective-permute-start | bytes 983048 | tf_op jit(solution)/shard_map/ppermute | solution.py:312
  133.1 15.5 %collective-permute-start.28 = (f32[320,256]{1,0:T(8,128)S(1)}, f32[320,256]{1,0:T(8,128)S(1)}, u32[]{:S(2)}, u32[]{:S(2)}) collective-permute-start(f32[320,256]{1,0:T(8,128)S(1)} %get-tuple-element.106.refs_2_), channel_id=1, source_target_pairs={{0,2},{1,3},{2,0},{3,1},{4,6},{5,7},{6,4},{7,5},{8,10},{9,11},{10,... | collective-permute-start | bytes 983048 | tf_op jit(solution)/shard_map/ppermute | solution.py:312
  133.9 15.0 %collective-permute-start.27 = (f32[320,256]{1,0:T(8,128)S(1)}, f32[320,256]{1,0:T(8,128)S(1)}, u32[]{:S(2)}, u32[]{:S(2)}) collective-permute-start(f32[320,256]{1,0:T(8,128)S(1)} %get-tuple-element.106.refs_2_), channel_id=1, source_target_pairs={{0,1},{1,0},{2,3},{3,2},{4,5},{5,4},{6,7},{7,6},{8,9},{9,8},{10,11... | collective-permute-start | bytes 983048 | tf_op jit(solution)/shard_map/ppermute | solution.py:312
  (20 other events, 120.4 us)

commit v7 on v6

--- a/solution.py
+++ b/solution.py
@@ -381,7 +381,7 @@
     m2, f1, w3_columns, x1_part, mine = call(
         level_two,
         3,
-        [(256, COLS), Far((256, U2)), Far((U3, COLS)), Far((256, 256)), Far((256, COLS))],
+        [(256, COLS), Far((256, U2)), Far((U3, COLS)), (256, 256), (256, COLS)],
         [(256, S + U1)],
         ids, selector_2, Far(held, 256, 128), Far(f0), *m1,
         coupling, swapped(coupling, "c", 1),
@@ -389,16 +389,16 @@
     keep, send = call(
         early_sums,
         3,
-        [Far((4, 128, COLS)), Far((4, 128, COLS))],
-        [],
-        ids, *[Far(value) for value in (v0_rows, f0, x1_part, mine, f1)], m2,
+        [(4, 128, COLS), (4, 128, COLS)],
+        [],
+        ids, Far(v0_rows), Far(f0), x1_part, mine, Far(f1), m2,
     )
     keep, send = call(
         level_three,
         6,
         [(4, 384, COLS), (4, 384, COLS)],
         [(384, S + U2), (384, U3)],
-        ids, selector_3, Far(held, 128, 128), Far(f1), Far(w3_columns), Far(keep), Far(send),
+        ids, selector_3, Far(held, 128, 128), Far(f1), Far(w3_columns), keep, send,
         *around(m2),
     )
     front, keep, send = lax.optimization_barrier((front, keep, send))

time: 170 us -> 170 us (level)
  no operation moved by 1% of the time
where the time goes in v7:
time: 170 us; the launch traced here: 169 us
  starting transfers between devices  66.9 us (39%)
  waiting for transfers between devices  57.5 us (34%)
  Pallas kernels  23.1 us (14%)
  blocking collectives  11.6 us (7%)
  local copies, waits for them, and re-layouts  9.53 us (6%)
    ppermute x31, waiting for transfers between devices, swapped(): return lax.ppermute(array, axis, [(i, i ^ distance) for i in range(parts)])  54.5 us
    ppermute x31, starting transfers between devices, swapped(): return lax.ppermute(array, axis, [(i, i ^ distance) for i in range(parts)])  50.1 us
    pallas_call x13, Pallas kernels, call(): pl.pallas_call(kernel, out_shape=[jax.ShapeDtypeStruct(shape, F32) for sh...  23.1 us
    all_to_all x4, starting transfers between devices, exchanged(): return lax.all_to_all(values, 'y', 0, 0)  16.8 us
    all_to_all x1, blocking collectives, exchanged(): return lax.all_to_all(values, 'y', 0, 0)  11.6 us
    unnamed x34, local copies, waits for them, and re-layouts  9.45 us
  transfers between devices with their start and end apart: 35, of which 19 were waited for; matrix products, arithmetic and copies ran while one was open for 0% of the time, Pallas kernels for 4%

profile of v7, /device:TPU:1, one launch (start us, length us, event | category | flops | bytes accessed | tf_op | source)
XLA Modules:
  0.0 169.5 jit_solution(9602903506857245289)
XLA Ops:
  0.6 2.1 %shard_map.153 = (f32[64,256]{1,0:T(8,128)}, f32[128,256]{1,0:T(8,128)}, f32[192,256]{1,0:T(8,128)}, f32[4,128,256]{2,1,0:T(8,128)}) custom-call(f32[16,256]{1,0:T(8,128)} %refs_0_.1, f32[32,256]{1,0:T(8,128)} %refs_1_.4, f32[16,256]{1,0:T(8,128)} %refs_2_.1, f32[64,256]{1,0:T(8,128)} %refs_3_.1, f32[64,256]{1,0:T(8,128)} %refs_4_.1, f32[128,256]{1,0:T(8,128)} %refs_5_.3, ...), custom_call_target="tpu_custom_call" | custom-call | flops 1100000000 | tf_op jit(solution)/shard_map/pallas_call | solution.py:105
  2.8 5.0 %all-to-all-start = ((f32[4,128,256]{2,1,0:T(8,128)}), f32[4,128,256]{2,1,0:T(8,128)S(1)}, u32[]{:S(2)}, u32[]{:S(2)}) async-start(f32[4,128,256]{2,1,0:T(8,128)} %get-tuple-element.64), calls=%async_computation | async-start | bytes 1048576 | tf_op jit(solution)/shard_map/all_to_all | solution.py:320
  9.4 2.7 %collective-permute-start.2 = (f32[64,256]{1,0:T(8,128)}, f32[64,256]{1,0:T(8,128)S(1)}, u32[]{:S(2)}, u32[]{:S(2)}) collective-permute-start(f32[64,256]{1,0:T(8,128)} %get-tuple-element.61.refs_1_), channel_id=1, source_target_pairs={{0,96},{32,64},{64,32},{96,0},{1,97},{33,65},{65,33},{97,1},{2,98}... | collective-permute-start | bytes 196616 | tf_op jit(solution)/shard_map/ppermute | solution.py:312
  13.0 2.5 %collective-permute-start.6 = (f32[192,256]{1,0:T(8,128)}, f32[192,256]{1,0:T(8,128)S(1)}, u32[]{:S(2)}, u32[]{:S(2)}) collective-permute-start(f32[192,256]{1,0:T(8,128)} %get-tuple-element.69.refs_1_), channel_id=1, source_target_pairs={{0,3},{1,2},{2,1},{3,0},{4,7},{5,6},{6,5},{7,4},{8,11},{9,10},{10,... | collective-permute-start | bytes 589832 | tf_op jit(solution)/shard_map/ppermute | solution.py:312
  16.5 2.7 %collective-permute-start.5 = (f32[192,256]{1,0:T(8,128)}, f32[192,256]{1,0:T(8,128)S(1)}, u32[]{:S(2)}, u32[]{:S(2)}) collective-permute-start(f32[192,256]{1,0:T(8,128)} %get-tuple-element.69.refs_1_), channel_id=1, source_target_pairs={{0,2},{1,3},{2,0},{3,1},{4,6},{5,7},{6,4},{7,5},{8,10},{9,11},{10,... | collective-permute-start | bytes 589832 | tf_op jit(solution)/shard_map/ppermute | solution.py:312
  21.5 2.0 %shard_map.154 = (f32[4,320,256]{2,1,0:T(8,128)}, f32[448,256]{1,0:T(8,128)S(1)}, f32[64,256]{1,0:T(8,128)S(1)}) custom-call(s32[5]{0:T(128)S(1)} %stack.23.refs_0_, f32[64,256]{1,0:T(8,128)S(1)} %copy-done.3, f32[64,256]{1,0:T(8,128)S(1)} %collective-permute-done.refs_2_, f32[64,256]{1,0:T(8,128)S(1)} %collective-permute-done.1.refs_3_, ...), custom_call_target="tpu_custom_call" | custom-call | flops 2200000000 | tf_op jit(solution)/shard_map/pallas_call | solution.py:105
  23.5 2.5 %collective-permute-done.4.refs_2_ = f32[192,256]{1,0:T(8,128)S(1)} collective-permute-done((f32[192,256]{1,0:T(8,128)}, f32[192,256]{1,0:T(8,128)S(1)}, u32[]{:S(2)}, u32[]{:S(2)}) %collective-permute-start.4) | collective-permute-done | bytes 196640 | tf_op jit(solution)/shard_map/ppermute | solution.py:312
  26.0 3.5 %all-to-all-start.1 = ((f32[4,320,256]{2,1,0:T(8,128)}), f32[4,320,256]{2,1,0:T(8,128)S(1)}, u32[]{:S(2)}, u32[]{:S(2)}) async-start(f32[4,320,256]{2,1,0:T(8,128)} %get-tuple-element.67), calls=%async_computation.1 | async-start | bytes 2621440 | tf_op jit(solution)/shard_map/all_to_all | solution.py:320
  32.9 5.0 %collective-permute-start.11 = (f32[4,128,256]{2,1,0:T(8,128)S(1)}, f32[4,128,256]{2,1,0:T(8,128)S(1)}, u32[]{:S(2)}, u32[]{:S(2)}) collective-permute-start(f32[4,128,256]{2,1,0:T(8,128)S(1)} %all-to-all-done.refs_6_), channel_id=1, source_target_pairs={{0,4},{4,0},{1,5},{5,1},{2,6},{6,2},{3,7},{7,3},{8,12},{12,8},{9,1... | collective-permute-start | bytes 1572872 | tf_op jit(solution)/shard_map/ppermute | solution.py:312
  38.0 5.2 %collective-permute-start.7 = (f32[64,256]{1,0:T(8,128)S(1)}, f32[64,256]{1,0:T(8,128)S(1)}, u32[]{:S(2)}, u32[]{:S(2)}) collective-permute-start(f32[64,256]{1,0:T(8,128)S(1)} %get-tuple-element.68), channel_id=1, source_target_pairs={{0,128},{128,0},{1,129},{129,1},{2,130},{130,2},{3,131},{131,3},{4... | collective-permute-start | bytes 196616 | tf_op jit(solution)/shard_map/ppermute | solution.py:312
  43.2 2.4 %collective-permute-done.7.refs_4_ = f32[64,256]{1,0:T(8,128)S(1)} collective-permute-done((f32[64,256]{1,0:T(8,128)S(1)}, f32[64,256]{1,0:T(8,128)S(1)}, u32[]{:S(2)}, u32[]{:S(2)}) %collective-permute-start.7) | collective-permute-done | bytes 65568 | tf_op jit(solution)/shard_map/ppermute | solution.py:312
  46.6 4.9 %collective-permute-done.14.refs_4_ = f32[448,256]{1,0:T(8,128)S(1)} collective-permute-done((f32[448,256]{1,0:T(8,128)S(1)}, f32[448,256]{1,0:T(8,128)S(1)}, u32[]{:S(2)}, u32[]{:S(2)}) %collective-permute-start.14) | collective-permute-done | bytes 458784 | tf_op jit(solution)/shard_map/ppermute | solution.py:312
  51.5 1.8 %collective-permute-start.8 = (f32[64,256]{1,0:T(8,128)S(1)}, f32[64,256]{1,0:T(8,128)S(1)}, u32[]{:S(2)}, u32[]{:S(2)}) collective-permute-start(f32[64,256]{1,0:T(8,128)S(1)} %collective-permute-done.7.refs_4_), channel_id=1, source_target_pairs={{0,1},{1,0},{2,3},{3,2},{4,5},{5,4},{6,7},{7,6},{8,9},{9,8},{10,11... | collective-permute-start | bytes 196616 | tf_op jit(solution)/shard_map/ppermute | solution.py:312
  56.8 3.6 %collective-permute-start.15 = (f32[4,320,256]{2,1,0:T(8,128)S(1)}, f32[4,320,256]{2,1,0:T(8,128)S(1)}, u32[]{:S(2)}, u32[]{:S(2)}) collective-permute-start(f32[4,320,256]{2,1,0:T(8,128)S(1)} %all-to-all-done.1.refs_8_), channel_id=1, source_target_pairs={{0,4},{4,0},{1,5},{5,1},{2,6},{6,2},{3,7},{7,3},{8,12},{12,8},{9,1... | collective-permute-start | bytes 3932168 | tf_op jit(solution)/shard_map/ppermute | solution.py:312
  60.4 2.7 %collective-permute-done.15.refs_9_ = f32[4,320,256]{2,1,0:T(8,128)S(1)} collective-permute-done((f32[4,320,256]{2,1,0:T(8,128)S(1)}, f32[4,320,256]{2,1,0:T(8,128)S(1)}, u32[]{:S(2)}, u32[]{:S(2)}) %collective-permute-start.15) | collective-permute-done | bytes 1310752 | tf_op jit(solution)/shard_map/ppermute | solution.py:312
  64.5 2.6 %shard_map.157 = (f32[4,320,256]{2,1,0:T(8,128)}, f32[128,256]{1,0:T(8,128)S(1)}, f32[128,512]{1,0:T(8,128)S(1)}, f32[128,1024]{1,0:T(8,128)S(1)}, f32[1024,256]{1,0:T(8,128)S(1)}) custom-call(s32[5]{0:T(128)S(1)} %stack.23.refs_0_, s32[2,4]{1,0:T(2,128)S(1)} %copy-done.6, f32[448,1024]{1,0:T(8,128)S(1)} %copy-done.8, f32[448,1024]{1,0:T(8,128)S(1)} %copy-done.8, ...), custom_call_target="tpu_custom_call" | custom-call | flops 4400000000 | tf_op jit(solution)/shard_map/pallas_call | solution.py:105
  69.6 4.2 %all-to-all-start.2 = ((f32[4,320,256]{2,1,0:T(8,128)}), f32[4,320,256]{2,1,0:T(8,128)S(1)}, u32[]{:S(2)}, u32[]{:S(2)}) async-start(f32[4,320,256]{2,1,0:T(8,128)} %get-tuple-element.88), calls=%async_computation.2 | async-start | bytes 2621440 | tf_op jit(solution)/shard_map/all_to_all | solution.py:320
  77.1 2.4 %collective-permute-done.18.refs_4_ = f32[128,256]{1,0:T(8,128)S(1)} collective-permute-done((f32[128,256]{1,0:T(8,128)S(1)}, f32[128,256]{1,0:T(8,128)S(1)}, u32[]{:S(2)}, u32[]{:S(2)}) %collective-permute-start.18) | collective-permute-done | bytes 131104 | tf_op jit(solution)/shard_map/ppermute | solution.py:312
  80.6 2.0 %collective-permute-done.16.refs_2_ = f32[128,256]{1,0:T(8,128)S(1)} collective-permute-done((f32[128,256]{1,0:T(8,128)S(1)}, f32[128,256]{1,0:T(8,128)S(1)}, u32[]{:S(2)}, u32[]{:S(2)}) %collective-permute-start.16) | collective-permute-done | bytes 131104 | tf_op jit(solution)/shard_map/ppermute | solution.py:312
  87.0 2.1 %collective-permute-done.21.refs_7_ = f32[128,256]{1,0:T(8,128)S(1)} collective-permute-done((f32[128,256]{1,0:T(8,128)S(1)}, f32[128,256]{1,0:T(8,128)S(1)}, u32[]{:S(2)}, u32[]{:S(2)}) %collective-permute-start.21) | collective-permute-done | bytes 131104 | tf_op jit(solution)/shard_map/ppermute | solution.py:312
  89.1 1.7 collective-permute-done.20.refs_6_
  91.3 3.0 %collective-permute-start.22 = (f32[4,320,256]{2,1,0:T(8,128)S(1)}, f32[4,320,256]{2,1,0:T(8,128)S(1)}, u32[]{:S(2)}, u32[]{:S(2)}) collective-permute-start(f32[4,320,256]{2,1,0:T(8,128)S(1)} %all-to-all-done.2.refs_8_), channel_id=1, source_target_pairs={{0,4},{4,0},{1,5},{5,1},{2,6},{6,2},{3,7},{7,3},{8,12},{12,8},{9,1... | collective-permute-start | bytes 3932168 | tf_op jit(solution)/shard_map/ppermute | solution.py:312
  94.3 2.7 %collective-permute-done.22.refs_9_ = f32[4,320,256]{2,1,0:T(8,128)S(1)} collective-permute-done((f32[4,320,256]{2,1,0:T(8,128)S(1)}, f32[4,320,256]{2,1,0:T(8,128)S(1)}, u32[]{:S(2)}, u32[]{:S(2)}) %collective-permute-start.22) | collective-permute-done | bytes 1310752 | tf_op jit(solution)/shard_map/ppermute | solution.py:312
  99.4 1.9 %shard_map.159 = (f32[256,256]{1,0:T(8,128)S(1)}, f32[256,1024]{1,0:T(8,128)S(1)}, f32[1536,256]{1,0:T(8,128)S(1)}, f32[256,256]{1,0:T(8,128)S(1)}, f32[256,256]{1,0:T(8,128)S(1)}) custom-call(s32[5]{0:T(128)S(1)} %stack.23.refs_0_, s32[4,8]{1,0:T(4,128)S(1)} %copy-done.5, f32[448,1024]{1,0:T(8,128)S(1)} %copy-done.9, f32[128,512]{1,0:T(8,128)S(1)} %copy-done.16, ...), custom_call_target="tpu_custom_call" | custom-call | flops 3300000000 | tf_op jit(solution)/shard_map/pallas_call | solution.py:105
  106.0 9.8 %collective-permute-done.25.refs_10_ = f32[256,256]{1,0:T(8,128)S(1)} collective-permute-done((f32[256,256]{1,0:T(8,128)S(1)}, f32[256,256]{1,0:T(8,128)S(1)}, u32[]{:S(2)}, u32[]{:S(2)}) %collective-permute-start.25) | collective-permute-done | bytes 262176 | tf_op jit(solution)/shard_map/ppermute | solution.py:312
  116.1 5.5 %shard_map.161 = (f32[4,384,256]{2,1,0:T(8,128)S(1)}, f32[4,384,256]{2,1,0:T(8,128)S(1)}) custom-call(s32[5]{0:T(128)S(1)} %stack.23.refs_0_, s32[8,12]{1,0:T(8,128)S(1)} %copy-done.4, f32[448,1024]{1,0:T(8,128)S(1)} %copy-done.10, f32[256,1024]{1,0:T(8,128)S(1)} %get-tuple-element.94.refs_5_.refs_3_, f32[1536,256]{1,0:T(8,128)S(1)} %get-tuple-element.95.refs_4_, ...), custom_call_target="tpu_custom_call" | custom-call | flops 6600000000 | tf_op jit(solution)/shard_map/pallas_call | solution.py:105
  123.2 3.0 %collective-permute-done.26.refs_1_ = f32[4,384,256]{2,1,0:T(8,128)S(1)} collective-permute-done((f32[4,384,256]{2,1,0:T(8,128)S(1)}, f32[4,384,256]{2,1,0:T(8,128)S(1)}, u32[]{:S(2)}, u32[]{:S(2)}) %collective-permute-start.26) | collective-permute-done | bytes 1572896 | tf_op jit(solution)/shard_map/ppermute | solution.py:312
  127.6 4.0 %all-to-all-start.3 = ((f32[4,384,256]{2,1,0:T(8,128)}), f32[4,384,256]{2,1,0:T(8,128)S(1)}, u32[]{:S(2)}, u32[]{:S(2)}) async-start(f32[4,384,256]{2,1,0:T(8,128)} %shard_map.162), calls=%async_computation.3 | async-start | bytes 3145728 | tf_op jit(solution)/shard_map/all_to_all | solution.py:320
  134.8 13.6 %collective-permute-done.29.refs_5_ = f32[320,256]{1,0:T(8,128)S(1)} collective-permute-done((f32[320,256]{1,0:T(8,128)S(1)}, f32[320,256]{1,0:T(8,128)S(1)}, u32[]{:S(2)}, u32[]{:S(2)}) %collective-permute-start.29) | collective-permute-done | bytes 327712 | tf_op jit(solution)/shard_map/ppermute | solution.py:312
  148.8 3.0 %all-to-all-done.3.refs_1_ = f32[4,384,256]{2,1,0:T(8,128)S(1)} async-done(((f32[4,384,256]{2,1,0:T(8,128)}), f32[4,384,256]{2,1,0:T(8,128)S(1)}, u32[]{:S(2)}, u32[]{:S(2)}) %all-to-all-start.3) | async-done | bytes 1572896 | tf_op jit(solution)/shard_map/all_to_all | solution.py:320
  151.7 2.3 %shard_map.163 = (f32[16,256]{1,0:T(8,128)}, f32[32,256]{1,0:T(8,128)}, f32[16,256]{1,0:T(8,128)}, f32[64,256]{1,0:T(8,128)}, f32[64,256]{1,0:T(8,128)}, /*index...) custom-call(s32[5]{0:T(128)S(1)} %stack.23.refs_0_, ...), custom_call_target="tpu_custom_call" | custom-call | flops 3300000000 | tf_op jit(solution)/shard_map/pallas_call | solution.py:105
  157.1 11.6 %all_to_all.25.refs_0_ = f32[4,128,256]{2,1,0:T(8,128)S(1)} all-to-all(f32[4,128,256]{2,1,0:T(8,128)S(1)} %shard_map.164), channel_id=1, replica_groups=mesh['h'=2,'q'=2,'p'=2,'y'=4,'c'=2,'x'=4] {'y'}, dimensions={0} | all-to-all | bytes 1048576 | tf_op jit(solution)/shard_map/all_to_all | solution.py:320
  (87 shorter events, 44.7 us)
Async XLA Ops:
  2.8 23.3 %all-to-all-start = ((f32[4,128,256]{2,1,0:T(8,128)}), f32[4,128,256]{2,1,0:T(8,128)S(1)}, u32[]{:S(2)}, u32[]{:S(2)}) async-start(f32[4,128,256]{2,1,0:T(8,128)} %get-tuple-element.64), calls=%async_computation | async-start | bytes 1048576 | tf_op jit(solution)/shard_map/all_to_all | solution.py:320
  7.8 11.9 %collective-permute-start.3 = (f32[128,256]{1,0:T(8,128)}, f32[128,256]{1,0:T(8,128)S(1)}, u32[]{:S(2)}, u32[]{:S(2)}) collective-permute-start(f32[128,256]{1,0:T(8,128)} %get-tuple-element.62.refs_5_), channel_id=1, source_target_pairs={{0,32},{32,0},{1,33},{33,1},{2,34},{34,2},{3,35},{35,3},{4,36},{36... | collective-permute-start | bytes 393224 | tf_op jit(solution)/shard_map/ppermute | solution.py:312
  9.4 7.1 %collective-permute-start.2 = (f32[64,256]{1,0:T(8,128)}, f32[64,256]{1,0:T(8,128)S(1)}, u32[]{:S(2)}, u32[]{:S(2)}) collective-permute-start(f32[64,256]{1,0:T(8,128)} %get-tuple-element.61.refs_1_), channel_id=1, source_target_pairs={{0,96},{32,64},{64,32},{96,0},{1,97},{33,65},{65,33},{97,1},{2,98}... | collective-permute-start | bytes 196616 | tf_op jit(solution)/shard_map/ppermute | solution.py:312
  12.1 7.1 %collective-permute-start.1 = (f32[64,256]{1,0:T(8,128)}, f32[64,256]{1,0:T(8,128)S(1)}, u32[]{:S(2)}, u32[]{:S(2)}) collective-permute-start(f32[64,256]{1,0:T(8,128)} %get-tuple-element.61.refs_1_), channel_id=1, source_target_pairs={{0,64},{32,96},{64,0},{96,32},{1,65},{33,97},{65,1},{97,33},{2,66}... | collective-permute-start | bytes 196616 | tf_op jit(solution)/shard_map/ppermute | solution.py:312
  12.4 7.3 %collective-permute-start = (f32[64,256]{1,0:T(8,128)}, f32[64,256]{1,0:T(8,128)S(1)}, u32[]{:S(2)}, u32[]{:S(2)}) collective-permute-start(f32[64,256]{1,0:T(8,128)} %get-tuple-element.61.refs_1_), channel_id=1, source_target_pairs={{0,32},{32,0},{64,96},{96,64},{1,33},{33,1},{65,97},{97,65},{2,34}... | collective-permute-start | bytes 196616 | tf_op jit(solution)/shard_map/ppermute | solution.py:312
  13.0 10.5 %collective-permute-start.6 = (f32[192,256]{1,0:T(8,128)}, f32[192,256]{1,0:T(8,128)S(1)}, u32[]{:S(2)}, u32[]{:S(2)}) collective-permute-start(f32[192,256]{1,0:T(8,128)} %get-tuple-element.69.refs_1_), channel_id=1, source_target_pairs={{0,3},{1,2},{2,1},{3,0},{4,7},{5,6},{6,5},{7,4},{8,11},{9,10},{10,... | collective-permute-start | bytes 589832 | tf_op jit(solution)/shard_map/ppermute | solution.py:312
  16.5 7.0 %collective-permute-start.5 = (f32[192,256]{1,0:T(8,128)}, f32[192,256]{1,0:T(8,128)S(1)}, u32[]{:S(2)}, u32[]{:S(2)}) collective-permute-start(f32[192,256]{1,0:T(8,128)} %get-tuple-element.69.refs_1_), channel_id=1, source_target_pairs={{0,2},{1,3},{2,0},{3,1},{4,6},{5,7},{6,4},{7,5},{8,10},{9,11},{10,... | collective-permute-start | bytes 589832 | tf_op jit(solution)/shard_map/ppermute | solution.py:312
  19.3 6.8 %collective-permute-start.4 = (f32[192,256]{1,0:T(8,128)}, f32[192,256]{1,0:T(8,128)S(1)}, u32[]{:S(2)}, u32[]{:S(2)}) collective-permute-start(f32[192,256]{1,0:T(8,128)} %get-tuple-element.69.refs_1_), channel_id=1, source_target_pairs={{0,1},{1,0},{2,3},{3,2},{4,5},{5,4},{6,7},{7,6},{8,9},{9,8},{10,11... | collective-permute-start | bytes 589832 | tf_op jit(solution)/shard_map/ppermute | solution.py:312
  26.0 30.8 %all-to-all-start.1 = ((f32[4,320,256]{2,1,0:T(8,128)}), f32[4,320,256]{2,1,0:T(8,128)S(1)}, u32[]{:S(2)}, u32[]{:S(2)}) async-start(f32[4,320,256]{2,1,0:T(8,128)} %get-tuple-element.67), calls=%async_computation.1 | async-start | bytes 2621440 | tf_op jit(solution)/shard_map/all_to_all | solution.py:320
  29.6 21.9 %collective-permute-start.14 = (f32[448,256]{1,0:T(8,128)S(1)}, f32[448,256]{1,0:T(8,128)S(1)}, u32[]{:S(2)}, u32[]{:S(2)}) collective-permute-start(f32[448,256]{1,0:T(8,128)S(1)} %get-tuple-element.76.refs_1_), channel_id=1, source_target_pairs={{0,3},{1,2},{2,1},{3,0},{4,7},{5,6},{6,5},{7,4},{8,11},{9,10},{10,... | collective-permute-start | bytes 1376264 | tf_op jit(solution)/shard_map/ppermute | solution.py:312
  31.0 20.5 %collective-permute-start.13 = (f32[448,256]{1,0:T(8,128)S(1)}, f32[448,256]{1,0:T(8,128)S(1)}, u32[]{:S(2)}, u32[]{:S(2)}) collective-permute-start(f32[448,256]{1,0:T(8,128)S(1)} %get-tuple-element.76.refs_1_), channel_id=1, source_target_pairs={{0,2},{1,3},{2,0},{3,1},{4,6},{5,7},{6,4},{7,5},{8,10},{9,11},{10,... | collective-permute-start | bytes 1376264 | tf_op jit(solution)/shard_map/ppermute | solution.py:312
  32.5 20.8 %collective-permute-start.12 = (f32[448,256]{1,0:T(8,128)S(1)}, f32[448,256]{1,0:T(8,128)S(1)}, u32[]{:S(2)}, u32[]{:S(2)}) collective-permute-start(f32[448,256]{1,0:T(8,128)S(1)} %get-tuple-element.76.refs_1_), channel_id=1, source_target_pairs={{0,1},{1,0},{2,3},{3,2},{4,5},{5,4},{6,7},{7,6},{8,9},{9,8},{10,11... | collective-permute-start | bytes 1376264 | tf_op jit(solution)/shard_map/ppermute | solution.py:312
  32.9 22.5 %collective-permute-start.11 = (f32[4,128,256]{2,1,0:T(8,128)S(1)}, f32[4,128,256]{2,1,0:T(8,128)S(1)}, u32[]{:S(2)}, u32[]{:S(2)}) collective-permute-start(f32[4,128,256]{2,1,0:T(8,128)S(1)} %all-to-all-done.refs_6_), channel_id=1, source_target_pairs={{0,4},{4,0},{1,5},{5,1},{2,6},{6,2},{3,7},{7,3},{8,12},{12,8},{9,1... | collective-permute-start | bytes 1572872 | tf_op jit(solution)/shard_map/ppermute | solution.py:312
  38.0 7.6 %collective-permute-start.7 = (f32[64,256]{1,0:T(8,128)S(1)}, f32[64,256]{1,0:T(8,128)S(1)}, u32[]{:S(2)}, u32[]{:S(2)}) collective-permute-start(f32[64,256]{1,0:T(8,128)S(1)} %get-tuple-element.68), channel_id=1, source_target_pairs={{0,128},{128,0},{1,129},{129,1},{2,130},{130,2},{3,131},{131,3},{4... | collective-permute-start | bytes 196616 | tf_op jit(solution)/shard_map/ppermute | solution.py:312
  45.6 11.2 %collective-permute-start.10 = (f32[64,256]{1,0:T(8,128)S(1)}, f32[64,256]{1,0:T(8,128)S(1)}, u32[]{:S(2)}, u32[]{:S(2)}) collective-permute-start(f32[64,256]{1,0:T(8,128)S(1)} %collective-permute-done.7.refs_4_), channel_id=1, source_target_pairs={{0,3},{1,2},{2,1},{3,0},{4,7},{5,6},{6,5},{7,4},{8,11},{9,10},{10,... | collective-permute-start | bytes 196616 | tf_op jit(solution)/shard_map/ppermute | solution.py:312
  51.5 5.3 %collective-permute-start.8 = (f32[64,256]{1,0:T(8,128)S(1)}, f32[64,256]{1,0:T(8,128)S(1)}, u32[]{:S(2)}, u32[]{:S(2)}) collective-permute-start(f32[64,256]{1,0:T(8,128)S(1)} %collective-permute-done.7.refs_4_), channel_id=1, source_target_pairs={{0,1},{1,0},{2,3},{3,2},{4,5},{5,4},{6,7},{7,6},{8,9},{9,8},{10,11... | collective-permute-start | bytes 196616 | tf_op jit(solution)/shard_map/ppermute | solution.py:312
  56.8 6.2 %collective-permute-start.15 = (f32[4,320,256]{2,1,0:T(8,128)S(1)}, f32[4,320,256]{2,1,0:T(8,128)S(1)}, u32[]{:S(2)}, u32[]{:S(2)}) collective-permute-start(f32[4,320,256]{2,1,0:T(8,128)S(1)} %all-to-all-done.1.refs_8_), channel_id=1, source_target_pairs={{0,4},{4,0},{1,5},{5,1},{2,6},{6,2},{3,7},{7,3},{8,12},{12,8},{9,1... | collective-permute-start | bytes 3932168 | tf_op jit(solution)/shard_map/ppermute | solution.py:312
  69.6 21.7 %all-to-all-start.2 = ((f32[4,320,256]{2,1,0:T(8,128)}), f32[4,320,256]{2,1,0:T(8,128)S(1)}, u32[]{:S(2)}, u32[]{:S(2)}) async-start(f32[4,320,256]{2,1,0:T(8,128)} %get-tuple-element.88), calls=%async_computation.2 | async-start | bytes 2621440 | tf_op jit(solution)/shard_map/all_to_all | solution.py:320
  73.8 5.6 %collective-permute-start.18 = (f32[128,256]{1,0:T(8,128)S(1)}, f32[128,256]{1,0:T(8,128)S(1)}, u32[]{:S(2)}, u32[]{:S(2)}) collective-permute-start(f32[128,256]{1,0:T(8,128)S(1)} %get-tuple-element.86.refs_1_), channel_id=1, source_target_pairs={{0,3},{1,2},{2,1},{3,0},{4,7},{5,6},{6,5},{7,4},{8,11},{9,10},{10,... | collective-permute-start | bytes 393224 | tf_op jit(solution)/shard_map/ppermute | solution.py:312
  75.2 5.4 %collective-permute-start.17 = (f32[128,256]{1,0:T(8,128)S(1)}, f32[128,256]{1,0:T(8,128)S(1)}, u32[]{:S(2)}, u32[]{:S(2)}) collective-permute-start(f32[128,256]{1,0:T(8,128)S(1)} %get-tuple-element.86.refs_1_), channel_id=1, source_target_pairs={{0,2},{1,3},{2,0},{3,1},{4,6},{5,7},{6,4},{7,5},{8,10},{9,11},{10,... | collective-permute-start | bytes 393224 | tf_op jit(solution)/shard_map/ppermute | solution.py:312
  76.0 6.6 %collective-permute-start.16 = (f32[128,256]{1,0:T(8,128)S(1)}, f32[128,256]{1,0:T(8,128)S(1)}, u32[]{:S(2)}, u32[]{:S(2)}) collective-permute-start(f32[128,256]{1,0:T(8,128)S(1)} %get-tuple-element.86.refs_1_), channel_id=1, source_target_pairs={{0,1},{1,0},{2,3},{3,2},{4,5},{5,4},{6,7},{7,6},{8,9},{9,8},{10,11... | collective-permute-start | bytes 393224 | tf_op jit(solution)/shard_map/ppermute | solution.py:312
  83.7 5.4 %collective-permute-start.21 = (f32[128,256]{1,0:T(8,128)S(1)}, f32[128,256]{1,0:T(8,128)S(1)}, u32[]{:S(2)}, u32[]{:S(2)}) collective-permute-start(f32[128,256]{1,0:T(8,128)S(1)} %shard_map.158.refs_4_), channel_id=1, source_target_pairs={{0,3},{1,2},{2,1},{3,0},{4,7},{5,6},{6,5},{7,4},{8,11},{9,10},{10,... | collective-permute-start | bytes 393224 | tf_op jit(solution)/shard_map/ppermute | solution.py:312
  85.1 5.6 %collective-permute-start.20 = (f32[128,256]{1,0:T(8,128)S(1)}, f32[128,256]{1,0:T(8,128)S(1)}, u32[]{:S(2)}, u32[]{:S(2)}) collective-permute-start(f32[128,256]{1,0:T(8,128)S(1)} %shard_map.158.refs_4_), channel_id=1, source_target_pairs={{0,2},{1,3},{2,0},{3,1},{4,6},{5,7},{6,4},{7,5},{8,10},{9,11},{10,... | collective-permute-start | bytes 393224 | tf_op jit(solution)/shard_map/ppermute | solution.py:312
  86.0 5.3 %collective-permute-start.19 = (f32[128,256]{1,0:T(8,128)S(1)}, f32[128,256]{1,0:T(8,128)S(1)}, u32[]{:S(2)}, u32[]{:S(2)}) collective-permute-start(f32[128,256]{1,0:T(8,128)S(1)} %shard_map.158.refs_4_), channel_id=1, source_target_pairs={{0,1},{1,0},{2,3},{3,2},{4,5},{5,4},{6,7},{7,6},{8,9},{9,8},{10,11... | collective-permute-start | bytes 393224 | tf_op jit(solution)/shard_map/ppermute | solution.py:312
  91.3 5.7 %collective-permute-start.22 = (f32[4,320,256]{2,1,0:T(8,128)S(1)}, f32[4,320,256]{2,1,0:T(8,128)S(1)}, u32[]{:S(2)}, u32[]{:S(2)}) collective-permute-start(f32[4,320,256]{2,1,0:T(8,128)S(1)} %all-to-all-done.2.refs_8_), channel_id=1, source_target_pairs={{0,4},{4,0},{1,5},{5,1},{2,6},{6,2},{3,7},{7,3},{8,12},{12,8},{9,1... | collective-permute-start | bytes 3932168 | tf_op jit(solution)/shard_map/ppermute | solution.py:312
  101.3 14.4 %collective-permute-start.25 = (f32[256,256]{1,0:T(8,128)S(1)}, f32[256,256]{1,0:T(8,128)S(1)}, u32[]{:S(2)}, u32[]{:S(2)}) collective-permute-start(f32[256,256]{1,0:T(8,128)S(1)} %get-tuple-element.99.refs_6_.refs_7_), channel_id=1, source_target_pairs={{0,3},{1,2},{2,1},{3,0},{4,7},{5,6},{6,5},{7,4},{8,11},{9,10},{10,... | collective-permute-start | bytes 786440 | tf_op jit(solution)/shard_map/ppermute | solution.py:312
  102.7 13.0 %collective-permute-start.24 = (f32[256,256]{1,0:T(8,128)S(1)}, f32[256,256]{1,0:T(8,128)S(1)}, u32[]{:S(2)}, u32[]{:S(2)}) collective-permute-start(f32[256,256]{1,0:T(8,128)S(1)} %get-tuple-element.99.refs_6_.refs_7_), channel_id=1, source_target_pairs={{0,2},{1,3},{2,0},{3,1},{4,6},{5,7},{6,4},{7,5},{8,10},{9,11},{10,... | collective-permute-start | bytes 786440 | tf_op jit(solution)/shard_map/ppermute | solution.py:312
  103.6 12.5 %collective-permute-start.23 = (f32[256,256]{1,0:T(8,128)S(1)}, f32[256,256]{1,0:T(8,128)S(1)}, u32[]{:S(2)}, u32[]{:S(2)}) collective-permute-start(f32[256,256]{1,0:T(8,128)S(1)} %get-tuple-element.99.refs_6_.refs_7_), channel_id=1, source_target_pairs={{0,1},{1,0},{2,3},{3,2},{4,5},{5,4},{6,7},{7,6},{8,9},{9,8},{10,11... | collective-permute-start | bytes 786440 | tf_op jit(solution)/shard_map/ppermute | solution.py:312
  127.6 24.1 %all-to-all-start.3 = ((f32[4,384,256]{2,1,0:T(8,128)}), f32[4,384,256]{2,1,0:T(8,128)S(1)}, u32[]{:S(2)}, u32[]{:S(2)}) async-start(f32[4,384,256]{2,1,0:T(8,128)} %shard_map.162), calls=%async_computation.3 | async-start | bytes 3145728 | tf_op jit(solution)/shard_map/all_to_all | solution.py:320
  131.6 16.8 %collective-permute-start.29 = (f32[320,256]{1,0:T(8,128)S(1)}, f32[320,256]{1,0:T(8,128)S(1)}, u32[]{:S(2)}, u32[]{:S(2)}) collective-permute-start(f32[320,256]{1,0:T(8,128)S(1)} %get-tuple-element.106.refs_2_), channel_id=1, source_target_pairs={{0,3},{1,2},{2,1},{3,0},{4,7},{5,6},{6,5},{7,4},{8,11},{9,10},{10,... | collective-permute-start | bytes 983048 | tf_op jit(solution)/shard_map/ppermute | solution.py:312
  132.9 15.5 %collective-permute-start.28 = (f32[320,256]{1,0:T(8,128)S(1)}, f32[320,256]{1,0:T(8,128)S(1)}, u32[]{:S(2)}, u32[]{:S(2)}) collective-permute-start(f32[320,256]{1,0:T(8,128)S(1)} %get-tuple-element.106.refs_2_), channel_id=1, source_target_pairs={{0,2},{1,3},{2,0},{3,1},{4,6},{5,7},{6,4},{7,5},{8,10},{9,11},{10,... | collective-permute-start | bytes 983048 | tf_op jit(solution)/shard_map/ppermute | solution.py:312
  133.8 15.0 %collective-permute-start.27 = (f32[320,256]{1,0:T(8,128)S(1)}, f32[320,256]{1,0:T(8,128)S(1)}, u32[]{:S(2)}, u32[]{:S(2)}) collective-permute-start(f32[320,256]{1,0:T(8,128)S(1)} %get-tuple-element.106.refs_2_), channel_id=1, source_target_pairs={{0,1},{1,0},{2,3},{3,2},{4,5},{5,4},{6,7},{7,6},{8,9},{9,8},{10,11... | collective-permute-start | bytes 983048 | tf_op jit(solution)/shard_map/ppermute | solution.py:312
  (20 other events, 120.4 us)
